TPU v7x, 512 devices: a whole 4x8x8 slice. The times are simulated.
512 devices in a mesh: patch: 128 (over z, x, y_lo), slab: 4 (over y_hi, core).
Axes of the slice: x: 4, y: 8 (y_hi: 2, y_lo: 4; y = y_hi * 4 + y_lo), z: 8, core: 2. Of those that a mesh axis runs over, the one named last changes fastest.
Arguments:
- load_vector: float32 [128, 64, 16384], P('patch', 'slab'), may hold values from -6 to 6
- reaction: float32 [128, 64, 16384], P('patch', 'slab'), may hold values from 0.1 to 1
- geometry: float32 [128, 3], P('patch'), may hold values from 0.25 to 64, as said below
- stiff_plane: float32 [128, 128], replicated, as said below
- mass_plane: float32 [128, 128], replicated, as said below
- stiff_vertical: float32 [64, 64], replicated, as said below
- mass_vertical: float32 [64, 64], replicated, as said below
- basis_plane: float32 [128, 128], replicated, as said below
- eigen_plane: float32 [128], replicated, as said below
- basis_vertical: float32 [64, 64], replicated, as said below
- eigen_vertical: float32 [64], replicated, as said below
- restrict_plane: float32 [126, 128], replicated, as said below
- restrict_vertical: float32 [62, 64], replicated, as said below
- patch_links: int32 [128, 3], P('patch'), may hold values from 0 to 3, as said below
Outputs:
- iterate: float32 [128, 64, 16384], P('patch', 'slab')
- coarse_residual: float32 [128, 62, 15876], P('patch', None, 'slab')
Inputs may be any that keep to these rules, and one draw needn't show every extreme that they name: `geometry`: positive scale factors. `patch_links`: column 0 holds a face of 0 to 3, column 1 the opposite face (0 with 1, 2 with 3), column 2 is 0 or 1. `stiff_plane`: Symmetric, zero beyond 4 places from the diagonal, positive definite. `mass_plane`: Symmetric, zero beyond 4 places from the diagonal, positive definite. `stiff_vertical`: Symmetric, zero beyond 4 places from the diagonal, positive definite. `mass_vertical`: Symmetric, zero beyond 4 places from the diagonal, positive definite. `basis_plane`: columns are eigenvectors of stiff_plane against mass_plane with unit mass norm. `eigen_plane`: positive eigenvalues matching basis_plane. `basis_vertical`: columns are eigenvectors of stiff_vertical against mass_vertical with unit mass norm. `eigen_vertical`: positive eigenvalues matching basis_vertical. `restrict_plane`: row c is nonzero at most for fine indices c - 1 to c + 3; fine index 0 feeds only row 0 and the last fine index only the last row. `restrict_vertical`: row m is nonzero at most for fine indices m - 1 to m + 3; fine index 0 feeds only row 0 and the last fine index only the last row.
All inputs are finite; a program needn't handle non-finite values.
Results may differ from a plain program's by a relative error of at most 0.0003.
Values sent between devices are 32-bit elements; how exact they have to be, the bound alone decides.
No kernel may reach another device: no remote copies, remote signals or barrier semaphores. Data moves between devices by JAX's collectives and lax.ppermute only.
A program may use at most 64 MiB of HBM per device.

v0:
```python
import jax
import jax.numpy as jnp
from jax import lax
from jax.sharding import PartitionSpec as P

BAND = 4
SWEEPS = 3


DAMPING = 0.25
HIGHEST = lax.Precision.HIGHEST


def with_halo(block, sides, width, periodic):
    for axis, dim in sides:
        count = lax.axis_size(axis)
        forward = [(i, i + 1) for i in range(count - 1)]
        if periodic:
            forward.append((count - 1, 0))
        backward = [(target, source) for source, target in forward]
        low = lax.ppermute(
            lax.slice_in_dim(block, block.shape[dim] - width, None, axis=dim), axis, forward
        )
        high = lax.ppermute(lax.slice_in_dim(block, 0, width, axis=dim), axis, backward)
        block = jnp.concatenate([low, block, high], axis=dim)
    return block


def face_values(volume, face_id, flip_bit):
    length = volume.shape[1]
    position = jnp.where(face_id % 2 == 0, 0, length - 1).astype(jnp.int32)
    on_rows = lax.dynamic_index_in_dim(volume, position, axis=1, keepdims=False)
    on_cols = lax.dynamic_index_in_dim(volume, position, axis=2, keepdims=False)
    values = jnp.where(face_id < 2, on_rows, on_cols)
    return jnp.where(flip_bit == 1, values[:, ::-1], values)


def add_face(volume, face_id, flip_bit, values):
    length = volume.shape[1]
    oriented = jnp.where(flip_bit == 1, values[:, ::-1], values)
    position = jnp.where(face_id % 2 == 0, 0, length - 1).astype(jnp.int32)
    marker = (jnp.arange(length, dtype=jnp.int32) == position).astype(volume.dtype)
    row_update = marker[None, :, None] * oriented[:, None, :]
    col_update = marker[None, None, :] * oriented[:, :, None]
    return volume + jnp.where(face_id < 2, row_update, col_update)


def assemble(volume, link_row):
    west_face = face_values(volume, link_row[0], link_row[2])
    east_face = face_values(volume, link_row[1], link_row[2])
    stacked = jnp.stack([west_face, east_face])
    extended = with_halo(stacked, (("patch", 0),), 1, True)
    volume = add_face(volume, link_row[0], link_row[2], extended[0])
    return add_face(volume, link_row[1], link_row[2], extended[3])


def apply_operator(
    volume, react_field, scales, stiff_plane, mass_plane, stiff_vertical, mass_vertical
):
    layers = volume.shape[0]
    slab_pos = lax.axis_index("slab")
    padded = with_halo(volume, (("slab", 0),), BAND, False)
    first_row = slab_pos * layers
    band_mass = lax.dynamic_slice(
        jnp.pad(mass_vertical, ((0, 0), (BAND, BAND))),
        (first_row, first_row),
        (layers, layers + 2 * BAND),
    )
    band_stiff = lax.dynamic_slice(
        jnp.pad(stiff_vertical, ((0, 0), (BAND, BAND))),
        (first_row, first_row),
        (layers, layers + 2 * BAND),
    )
    along_mass = jnp.einsum("kl,lij->kij", band_mass, padded, precision=HIGHEST)
    along_stiff = jnp.einsum("kl,lij->kij", band_stiff, padded, precision=HIGHEST)
    mass_mass = jnp.einsum("kij,bj->kib", along_mass, mass_plane, precision=HIGHEST)
    mass_stiff = jnp.einsum("kij,bj->kib", along_mass, stiff_plane, precision=HIGHEST)
    stiff_mass = jnp.einsum("kij,bj->kib", along_stiff, mass_plane, precision=HIGHEST)
    inner_sum = scales[1] * mass_stiff + scales[2] * stiff_mass
    result = scales[0] * jnp.einsum("ai,kib->kab", stiff_plane, mass_mass, precision=HIGHEST)
    result = result + jnp.einsum("ai,kib->kab", mass_plane, inner_sum, precision=HIGHEST)
    return result + react_field * volume


def smooth(residual, scales, basis_plane, eigen_plane, basis_vertical, eigen_vertical):
    slab_pos = lax.axis_index("slab")
    group_size = lax.axis_size("slab")
    plane_size = basis_plane.shape[0]
    first_pass = jnp.einsum("kij,jb->kib", residual, basis_plane, precision=HIGHEST)
    second = jnp.einsum("ia,kib->kab", basis_plane, first_pass, precision=HIGHEST)
    columns = lax.all_to_all(second, "slab", split_axis=1, concat_axis=0, tiled=True)
    local_cols = plane_size // group_size
    lam_rows = lax.dynamic_slice_in_dim(eigen_plane, slab_pos * local_cols, local_cols)
    mixed_rows = jnp.einsum("kc,kab->cab", basis_vertical, columns, precision=HIGHEST)
    denominator = (
        scales[0] * lam_rows[None, :, None]
        + scales[1] * eigen_plane[None, None, :]
        + scales[2] * eigen_vertical[:, None, None]
    )
    scaled = mixed_rows / denominator
    back_rows = jnp.einsum("kc,cab->kab", basis_vertical, scaled, precision=HIGHEST)
    returned = lax.all_to_all(back_rows, "slab", split_axis=0, concat_axis=1, tiled=True)
    across = jnp.einsum("kab,jb->kaj", returned, basis_plane, precision=HIGHEST)
    return jnp.einsum("ia,kaj->kij", basis_plane, across, precision=HIGHEST)


def per_device(
    load_vector,
    reaction,
    geometry,
    stiff_plane,
    mass_plane,
    stiff_vertical,
    mass_vertical,
    basis_plane,
    eigen_plane,
    basis_vertical,
    eigen_vertical,
    restrict_plane,
    restrict_vertical,
    patch_links,
):
    layers = load_vector.shape[1]
    plane_size = basis_plane.shape[0]
    fine_load = load_vector[0].reshape(layers, plane_size, plane_size)
    react_field = reaction[0].reshape(layers, plane_size, plane_size)
    scales = geometry[0]
    link_row = patch_links[0]
    iterate = jnp.zeros_like(fine_load)
    for sweep_index in range(SWEEPS):
        if sweep_index == 0:
            unassembled = fine_load
        else:
            unassembled = fine_load - apply_operator(
                iterate, react_field, scales, stiff_plane, mass_plane, stiff_vertical, mass_vertical
            )
        residual = assemble(unassembled, link_row)
        correction = smooth(
            residual, scales, basis_plane, eigen_plane, basis_vertical, eigen_vertical
        )
        iterate = iterate + DAMPING * assemble(correction, link_row)
    final_local = fine_load - apply_operator(
        iterate, react_field, scales, stiff_plane, mass_plane, stiff_vertical, mass_vertical
    )
    coarse_size = restrict_plane.shape[0]
    halfway = jnp.einsum("ci,kij->kcj", restrict_plane, final_local, precision=HIGHEST)
    plane_coarse = jnp.einsum("kcj,dj->kcd", halfway, restrict_plane, precision=HIGHEST)
    plane_coarse = assemble(plane_coarse, link_row)
    flattened = plane_coarse.reshape(layers, coarse_size * coarse_size)
    gathered_rows = lax.all_to_all(flattened, "slab", split_axis=1, concat_axis=0, tiled=True)
    coarse = jnp.dot(
        restrict_vertical, gathered_rows, precision=HIGHEST, preferred_element_type=jnp.float32
    )
    return (iterate.reshape(1, layers, plane_size * plane_size), coarse[None])


def solution(mesh):
    in_specs = (
        P("patch", "slab", None),
        P("patch", "slab", None),
        P("patch", None),
        P(),
        P(),
        P(),
        P(),
        P(),
        P(),
        P(),
        P(),
        P(),
        P(),
        P("patch", None),
    )
    out_specs = (P("patch", "slab", None), P("patch", None, "slab"))
    return jax.shard_map(
        per_device, mesh=mesh, in_specs=in_specs, out_specs=out_specs, check_vma=False
    )
```

profile of v0, /device:TPU:1, one launch (start us, length us, event | category | flops | bytes accessed | tf_op | source)
XLA Modules:
  0.0 463.6 jit_solution(2385658831620934072)
XLA Ops:
  9.7 4.0 collective-permute-start
  14.4 14.6 %collective-permute-start.1 = (f32[1,16,128]{2,1,0:T(8,128)S(1)}, f32[1,16,128]{2,1,0:T(8,128)S(1)}, u32[]{:S(2)}, u32[]{:S(2)}) collective-permute-start(f32[1,16,128]{2,1,0:T(8,128)S(1)} %select_bitcast_fusion.12), channel_id=1, source_target_pairs={{4,0},{8,4},{12,8},{16,12},{20,16},{24,20},{28,24},{32,28},{36,32}... | collective-permute-start | bytes 24584 | tf_op jit(solution)/shard_map/ppermute | solution.py:24
  33.9 6.0 %all-to-all-start = ((f32[16,128,128]{2,0,1:T(8,128)}), f32[16,128,128]{2,0,1:T(8,128)S(1)}, u32[]{:S(2)}, u32[]{:S(2)}) async-start(f32[16,128,128]{2,0,1:T(8,128)} %copy.160), calls=%async_computation | async-start | bytes 2097152 | tf_op jit(solution)/shard_map/all_to_all | solution.py:91
  42.7 17.9 %all-to-all-done = f32[16,128,128]{2,0,1:T(8,128)S(1)} async-done(((f32[16,128,128]{2,0,1:T(8,128)}), f32[16,128,128]{2,0,1:T(8,128)S(1)}, u32[]{:S(2)}, u32[]{:S(2)}) %all-to-all-start) | async-done | bytes 1048608 | tf_op jit(solution)/shard_map/all_to_all | solution.py:91
  64.3 32.0 %all_to_all.127 = f32[64,32,128]{2,1,0:T(8,128)S(1)} all-to-all(f32[64,32,128]{2,1,0:T(8,128)S(1)} %copy.165), channel_id=1, replica_groups=mesh['patch'=128,'slab'=4] {'slab'}, dimensions={0} | all-to-all | bytes 2097152 | tf_op jit(solution)/shard_map/all_to_all | solution.py:102
  101.8 12.7 %collective-permute-start.3 = (f32[1,16,128]{2,1,0:T(8,128)S(1)}, f32[1,16,128]{2,1,0:T(8,128)S(1)}, u32[]{:S(2)}, u32[]{:S(2)}) collective-permute-start(f32[1,16,128]{2,1,0:T(8,128)S(1)} %select_bitcast_fusion.10), channel_id=1, source_target_pairs={{4,0},{8,4},{12,8},{16,12},{20,16},{24,20},{28,24},{32,28},{36,32}... | collective-permute-start | bytes 24584 | tf_op jit(solution)/shard_map/ppermute | solution.py:24
  117.9 7.6 %collective-permute-start.4 = (f32[4,128,128]{1,2,0:T(8,128)}, f32[4,128,128]{1,2,0:T(8,128)}, u32[]{:S(2)}, u32[]{:S(2)}) collective-permute-start(f32[4,128,128]{1,2,0:T(8,128)} %get-tuple-element.40), channel_id=1, source_target_pairs={{0,1},{1,2},{2,3},{4,5},{5,6},{6,7},{8,9},{9,10},{10,11},{12,13},{... | collective-permute-start | bytes 786440 | tf_op jit(solution)/shard_map/ppermute | solution.py:21
  130.3 7.2 %collective-permute-done.5 = f32[4,128,128]{1,2,0:T(8,128)} collective-permute-done((f32[4,128,128]{1,2,0:T(8,128)}, f32[4,128,128]{1,2,0:T(8,128)}, u32[]{:S(2)}, u32[]{:S(2)}) %collective-permute-start.5) | collective-permute-done | bytes 262176 | tf_op jit(solution)/shard_map/ppermute | solution.py:24
  137.5 2.7 pad_maximum_fusion
  140.2 3.0 copy.168
  143.2 2.6 fusion.146
  160.0 10.3 %collective-permute-start.7 = (f32[1,16,128]{2,1,0:T(8,128)S(1)}, f32[1,16,128]{2,1,0:T(8,128)S(1)}, u32[]{:S(2)}, u32[]{:S(2)}) collective-permute-start(f32[1,16,128]{2,1,0:T(8,128)S(1)} %select_bitcast_fusion.8), channel_id=1, source_target_pairs={{4,0},{8,4},{12,8},{16,12},{20,16},{24,20},{28,24},{32,28},{36,32}... | collective-permute-start | bytes 24584 | tf_op jit(solution)/shard_map/ppermute | solution.py:24
  170.8 3.0 fusion.35
  175.3 20.6 %all_to_all.128 = f32[16,128,128]{2,0,1:T(8,128)S(1)} all-to-all(f32[16,128,128]{2,0,1:T(8,128)S(1)} %copy.179), channel_id=1, replica_groups=mesh['patch'=128,'slab'=4] {'slab'}, dimensions={1} | all-to-all | bytes 2097152 | tf_op jit(solution)/shard_map/all_to_all | solution.py:91
  199.7 22.2 %all_to_all.129 = f32[64,32,128]{2,1,0:T(8,128)S(1)} all-to-all(f32[64,32,128]{2,1,0:T(8,128)S(1)} %copy.184), channel_id=1, replica_groups=mesh['patch'=128,'slab'=4] {'slab'}, dimensions={0} | all-to-all | bytes 2097152 | tf_op jit(solution)/shard_map/all_to_all | solution.py:102
  225.4 15.5 %collective-permute-start.8 = (f32[1,16,128]{2,1,0:T(8,128)S(1)}, f32[1,16,128]{2,1,0:T(8,128)S(1)}, u32[]{:S(2)}, u32[]{:S(2)}) collective-permute-start(f32[1,16,128]{2,1,0:T(8,128)S(1)} %select_bitcast_fusion.7), channel_id=1, source_target_pairs={{0,4},{4,8},{8,12},{12,16},{16,20},{20,24},{24,28},{28,32},{32,36}... | collective-permute-start | bytes 24584 | tf_op jit(solution)/shard_map/ppermute | solution.py:21
  241.0 10.6 %collective-permute-start.9 = (f32[1,16,128]{2,1,0:T(8,128)S(1)}, f32[1,16,128]{2,1,0:T(8,128)S(1)}, u32[]{:S(2)}, u32[]{:S(2)}) collective-permute-start(f32[1,16,128]{2,1,0:T(8,128)S(1)} %select_bitcast_fusion.6), channel_id=1, source_target_pairs={{4,0},{8,4},{12,8},{16,12},{20,16},{24,20},{28,24},{32,28},{36,32}... | collective-permute-start | bytes 24584 | tf_op jit(solution)/shard_map/ppermute | solution.py:24
  253.8 7.6 %collective-permute-start.10 = (f32[4,128,128]{1,2,0:T(8,128)S(1)}, f32[4,128,128]{1,2,0:T(8,128)S(1)}, u32[]{:S(2)}, u32[]{:S(2)}) collective-permute-start(f32[4,128,128]{1,2,0:T(8,128)S(1)} %get-tuple-element.34), channel_id=1, source_target_pairs={{0,1},{1,2},{2,3},{4,5},{5,6},{6,7},{8,9},{9,10},{10,11},{12,13},{... | collective-permute-start | bytes 786440 | tf_op jit(solution)/shard_map/ppermute | solution.py:21
  261.4 2.1 collective-permute-start.11
  264.7 8.4 %collective-permute-done.11 = f32[4,128,128]{1,2,0:T(8,128)S(1)} collective-permute-done((f32[4,128,128]{1,2,0:T(8,128)S(1)}, f32[4,128,128]{1,2,0:T(8,128)S(1)}, u32[]{:S(2)}, u32[]{:S(2)}) %collective-permute-start.11) | collective-permute-done | bytes 262176 | tf_op jit(solution)/shard_map/ppermute | solution.py:24
  274.4 3.0 copy.187
  277.4 2.6 fusion.144
  293.3 10.1 %collective-permute-start.13 = (f32[1,16,128]{2,1,0:T(8,128)S(1)}, f32[1,16,128]{2,1,0:T(8,128)S(1)}, u32[]{:S(2)}, u32[]{:S(2)}) collective-permute-start(f32[1,16,128]{2,1,0:T(8,128)S(1)} %select_bitcast_fusion.4), channel_id=1, source_target_pairs={{4,0},{8,4},{12,8},{16,12},{20,16},{24,20},{28,24},{32,28},{36,32}... | collective-permute-start | bytes 24584 | tf_op jit(solution)/shard_map/ppermute | solution.py:24
  307.2 20.7 %all_to_all.130 = f32[16,128,128]{2,0,1:T(8,128)S(1)} all-to-all(f32[16,128,128]{2,0,1:T(8,128)S(1)} %copy.198), channel_id=1, replica_groups=mesh['patch'=128,'slab'=4] {'slab'}, dimensions={1} | all-to-all | bytes 2097152 | tf_op jit(solution)/shard_map/all_to_all | solution.py:91
  331.7 32.0 %all_to_all.131 = f32[64,32,128]{2,1,0:T(8,128)S(1)} all-to-all(f32[64,32,128]{2,1,0:T(8,128)S(1)} %copy.203), channel_id=1, replica_groups=mesh['patch'=128,'slab'=4] {'slab'}, dimensions={0} | all-to-all | bytes 2097152 | tf_op jit(solution)/shard_map/all_to_all | solution.py:102
  369.2 14.3 %collective-permute-start.15 = (f32[1,16,128]{2,1,0:T(8,128)S(1)}, f32[1,16,128]{2,1,0:T(8,128)S(1)}, u32[]{:S(2)}, u32[]{:S(2)}) collective-permute-start(f32[1,16,128]{2,1,0:T(8,128)S(1)} %select_bitcast_fusion.2), channel_id=1, source_target_pairs={{4,0},{8,4},{12,8},{16,12},{20,16},{24,20},{28,24},{32,28},{36,32}... | collective-permute-start | bytes 24584 | tf_op jit(solution)/shard_map/ppermute | solution.py:24
  385.1 7.5 %collective-permute-start.16 = (f32[4,128,128]{1,2,0:T(8,128)S(1)}, f32[4,128,128]{1,2,0:T(8,128)S(1)}, u32[]{:S(2)}, u32[]{:S(2)}) collective-permute-start(f32[4,128,128]{1,2,0:T(8,128)S(1)} %get-tuple-element.28), channel_id=1, source_target_pairs={{0,1},{1,2},{2,3},{4,5},{5,6},{6,7},{8,9},{9,10},{10,11},{12,13},{... | collective-permute-start | bytes 786440 | tf_op jit(solution)/shard_map/ppermute | solution.py:21
  392.7 2.3 collective-permute-start.17
  396.0 8.4 %collective-permute-done.17 = f32[4,128,128]{1,2,0:T(8,128)S(1)} collective-permute-done((f32[4,128,128]{1,2,0:T(8,128)S(1)}, f32[4,128,128]{1,2,0:T(8,128)S(1)}, u32[]{:S(2)}, u32[]{:S(2)}) %collective-permute-start.17) | collective-permute-done | bytes 262176 | tf_op jit(solution)/shard_map/ppermute | solution.py:24
  425.0 9.8 %collective-permute-start.19 = (f32[1,16,126]{2,1,0:T(8,128)S(1)}, f32[1,16,126]{2,1,0:T(8,128)S(1)}, u32[]{:S(2)}, u32[]{:S(2)}) collective-permute-start(f32[1,16,126]{2,1,0:T(8,128)S(1)} %select_bitcast_fusion), channel_id=1, source_target_pairs={{4,0},{8,4},{12,8},{16,12},{20,16},{24,20},{28,24},{32,28},{36,32}... | collective-permute-start | bytes 24200 | tf_op jit(solution)/shard_map/ppermute | solution.py:24
  439.4 3.5 all-to-all-start.6
  444.4 15.9 %all-to-all-done.6 = f32[16,4,3969]{2,0,1:T(8,128)S(1)} async-done(((f32[16,4,3969]{2,0,1:T(8,128)}), f32[16,4,3969]{2,0,1:T(8,128)S(1)}, u32[]{:S(2)}, u32[]{:S(2)}) %all-to-all-start.6) | async-done | bytes 1016096 | tf_op jit(solution)/shard_map/all_to_all | solution.py:150
  (231 shorter events, 115.0 us)
Async XLA Ops:
  0.6 29.3 %copy-start = (f32[128,128]{1,0:T(8,128)S(1)}, f32[128,128]{1,0:T(8,128)}, u32[]{:S(2)}) copy-start(f32[128,128]{1,0:T(8,128)} %param.21) | copy-start | bytes 196612
  9.7 19.8 %collective-permute-start = (f32[1,16,128]{2,1,0:T(8,128)S(1)}, f32[1,16,128]{2,1,0:T(8,128)S(1)}, u32[]{:S(2)}, u32[]{:S(2)}) collective-permute-start(f32[1,16,128]{2,1,0:T(8,128)S(1)} %select_bitcast_fusion.13), channel_id=1, source_target_pairs={{0,4},{4,8},{8,12},{12,16},{16,20},{20,24},{24,28},{28,32},{32,36}... | collective-permute-start | bytes 24584 | tf_op jit(solution)/shard_map/ppermute | solution.py:21
  14.4 15.4 %collective-permute-start.1 = (f32[1,16,128]{2,1,0:T(8,128)S(1)}, f32[1,16,128]{2,1,0:T(8,128)S(1)}, u32[]{:S(2)}, u32[]{:S(2)}) collective-permute-start(f32[1,16,128]{2,1,0:T(8,128)S(1)} %select_bitcast_fusion.12), channel_id=1, source_target_pairs={{4,0},{8,4},{12,8},{16,12},{20,16},{24,20},{28,24},{32,28},{36,32}... | collective-permute-start | bytes 24584 | tf_op jit(solution)/shard_map/ppermute | solution.py:24
  29.4 124.5 %copy-start.1 = (f32[16,128,128]{1,2,0:T(8,128)}, f32[16,128,128]{1,2,0:T(8,128)S(1)}, u32[]{:S(2)}) copy-start(f32[16,128,128]{1,2,0:T(8,128)S(1)} %copy.157) | copy-start | bytes 3145732
  33.9 6.1 %copy-start.20 = (f32[1,3]{1,0:T(1,128)S(1)}, f32[1,3]{1,0:T(1,128)}, u32[]{:S(2)}) copy-start(f32[1,3]{1,0:T(1,128)} %param.16) | copy-start | bytes 40
  33.9 6.7 %copy-start.21 = (f32[128]{0:T(128)S(1)}, f32[128]{0:T(128)}, u32[]{:S(2)}) copy-start(f32[128]{0:T(128)} %param.22) | copy-start | bytes 1540
  33.9 8.0 %copy-start.22 = (f32[64]{0:T(128)S(1)}, f32[64]{0:T(128)}, u32[]{:S(2)}) copy-start(f32[64]{0:T(128)} %param.24) | copy-start | bytes 772
  33.9 26.7 %all-to-all-start = ((f32[16,128,128]{2,0,1:T(8,128)}), f32[16,128,128]{2,0,1:T(8,128)S(1)}, u32[]{:S(2)}, u32[]{:S(2)}) async-start(f32[16,128,128]{2,0,1:T(8,128)} %copy.160), calls=%async_computation | async-start | bytes 2097152 | tf_op jit(solution)/shard_map/all_to_all | solution.py:91
  39.9 20.9 %copy-start.15 = (f32[64,64]{1,0:T(8,128)S(1)}, f32[64,64]{1,0:T(8,128)}, u32[]{:S(2)}) copy-start(f32[64,64]{1,0:T(8,128)} %param.23) | copy-start | bytes 49156
  99.8 14.7 %collective-permute-start.2 = (f32[1,16,128]{2,1,0:T(8,128)S(1)}, f32[1,16,128]{2,1,0:T(8,128)S(1)}, u32[]{:S(2)}, u32[]{:S(2)}) collective-permute-start(f32[1,16,128]{2,1,0:T(8,128)S(1)} %select_bitcast_fusion.11), channel_id=1, source_target_pairs={{0,4},{4,8},{8,12},{12,16},{16,20},{20,24},{24,28},{28,32},{32,36}... | collective-permute-start | bytes 24584 | tf_op jit(solution)/shard_map/ppermute | solution.py:21
  101.8 13.5 %collective-permute-start.3 = (f32[1,16,128]{2,1,0:T(8,128)S(1)}, f32[1,16,128]{2,1,0:T(8,128)S(1)}, u32[]{:S(2)}, u32[]{:S(2)}) collective-permute-start(f32[1,16,128]{2,1,0:T(8,128)S(1)} %select_bitcast_fusion.10), channel_id=1, source_target_pairs={{4,0},{8,4},{12,8},{16,12},{20,16},{24,20},{28,24},{32,28},{36,32}... | collective-permute-start | bytes 24584 | tf_op jit(solution)/shard_map/ppermute | solution.py:24
  115.4 12.2 %copy-start.14 = (f32[1,16,16384]{2,1,0:T(8,128)S(1)}, f32[1,16,16384]{2,1,0:T(8,128)}, u32[]{:S(2)}) copy-start(f32[1,16,16384]{2,1,0:T(8,128)} %param.15) | copy-start | bytes 3145732
  117.9 12.4 %collective-permute-start.4 = (f32[4,128,128]{1,2,0:T(8,128)}, f32[4,128,128]{1,2,0:T(8,128)}, u32[]{:S(2)}, u32[]{:S(2)}) collective-permute-start(f32[4,128,128]{1,2,0:T(8,128)} %get-tuple-element.40), channel_id=1, source_target_pairs={{0,1},{1,2},{2,3},{4,5},{5,6},{6,7},{8,9},{9,10},{10,11},{12,13},{... | collective-permute-start | bytes 786440 | tf_op jit(solution)/shard_map/ppermute | solution.py:21
  125.6 11.9 %collective-permute-start.5 = (f32[4,128,128]{1,2,0:T(8,128)}, f32[4,128,128]{1,2,0:T(8,128)}, u32[]{:S(2)}, u32[]{:S(2)}) collective-permute-start(f32[4,128,128]{1,2,0:T(8,128)} %get-tuple-element.41), channel_id=1, source_target_pairs={{1,0},{2,1},{3,2},{5,4},{6,5},{7,6},{9,8},{10,9},{11,10},{13,12},{... | collective-permute-start | bytes 786440 | tf_op jit(solution)/shard_map/ppermute | solution.py:24
  130.3 23.6 %copy-start.4 = (f32[16,128,128]{1,2,0:T(8,128)}, f32[16,128,128]{1,2,0:T(8,128)S(1)}, u32[]{:S(2)}) copy-start(f32[16,128,128]{1,2,0:T(8,128)S(1)} %copy.175) | copy-start | bytes 3145732
  140.2 3.0 copy-start.16
  158.1 12.3 %collective-permute-start.6 = (f32[1,16,128]{2,1,0:T(8,128)S(1)}, f32[1,16,128]{2,1,0:T(8,128)S(1)}, u32[]{:S(2)}, u32[]{:S(2)}) collective-permute-start(f32[1,16,128]{2,1,0:T(8,128)S(1)} %select_bitcast_fusion.9), channel_id=1, source_target_pairs={{0,4},{4,8},{8,12},{12,16},{16,20},{20,24},{24,28},{28,32},{32,36}... | collective-permute-start | bytes 24584 | tf_op jit(solution)/shard_map/ppermute | solution.py:21
  160.0 10.7 %collective-permute-start.7 = (f32[1,16,128]{2,1,0:T(8,128)S(1)}, f32[1,16,128]{2,1,0:T(8,128)S(1)}, u32[]{:S(2)}, u32[]{:S(2)}) collective-permute-start(f32[1,16,128]{2,1,0:T(8,128)S(1)} %select_bitcast_fusion.8), channel_id=1, source_target_pairs={{4,0},{8,4},{12,8},{16,12},{20,16},{24,20},{28,24},{32,28},{36,32}... | collective-permute-start | bytes 24584 | tf_op jit(solution)/shard_map/ppermute | solution.py:24
  225.4 26.1 %collective-permute-start.8 = (f32[1,16,128]{2,1,0:T(8,128)S(1)}, f32[1,16,128]{2,1,0:T(8,128)S(1)}, u32[]{:S(2)}, u32[]{:S(2)}) collective-permute-start(f32[1,16,128]{2,1,0:T(8,128)S(1)} %select_bitcast_fusion.7), channel_id=1, source_target_pairs={{0,4},{4,8},{8,12},{12,16},{16,20},{20,24},{24,28},{28,32},{32,36}... | collective-permute-start | bytes 24584 | tf_op jit(solution)/shard_map/ppermute | solution.py:21
  241.0 11.4 %collective-permute-start.9 = (f32[1,16,128]{2,1,0:T(8,128)S(1)}, f32[1,16,128]{2,1,0:T(8,128)S(1)}, u32[]{:S(2)}, u32[]{:S(2)}) collective-permute-start(f32[1,16,128]{2,1,0:T(8,128)S(1)} %select_bitcast_fusion.6), channel_id=1, source_target_pairs={{4,0},{8,4},{12,8},{16,12},{20,16},{24,20},{28,24},{32,28},{36,32}... | collective-permute-start | bytes 24584 | tf_op jit(solution)/shard_map/ppermute | solution.py:24
  253.8 10.9 %collective-permute-start.10 = (f32[4,128,128]{1,2,0:T(8,128)S(1)}, f32[4,128,128]{1,2,0:T(8,128)S(1)}, u32[]{:S(2)}, u32[]{:S(2)}) collective-permute-start(f32[4,128,128]{1,2,0:T(8,128)S(1)} %get-tuple-element.34), channel_id=1, source_target_pairs={{0,1},{1,2},{2,3},{4,5},{5,6},{6,7},{8,9},{9,10},{10,11},{12,13},{... | collective-permute-start | bytes 786440 | tf_op jit(solution)/shard_map/ppermute | solution.py:21
  261.4 11.7 %collective-permute-start.11 = (f32[4,128,128]{1,2,0:T(8,128)S(1)}, f32[4,128,128]{1,2,0:T(8,128)S(1)}, u32[]{:S(2)}, u32[]{:S(2)}) collective-permute-start(f32[4,128,128]{1,2,0:T(8,128)S(1)} %get-tuple-element.35), channel_id=1, source_target_pairs={{1,0},{2,1},{3,2},{5,4},{6,5},{7,6},{9,8},{10,9},{11,10},{13,12},{... | collective-permute-start | bytes 786440 | tf_op jit(solution)/shard_map/ppermute | solution.py:24
  291.4 12.1 %collective-permute-start.12 = (f32[1,16,128]{2,1,0:T(8,128)S(1)}, f32[1,16,128]{2,1,0:T(8,128)S(1)}, u32[]{:S(2)}, u32[]{:S(2)}) collective-permute-start(f32[1,16,128]{2,1,0:T(8,128)S(1)} %select_bitcast_fusion.5), channel_id=1, source_target_pairs={{0,4},{4,8},{8,12},{12,16},{16,20},{20,24},{24,28},{28,32},{32,36}... | collective-permute-start | bytes 24584 | tf_op jit(solution)/shard_map/ppermute | solution.py:21
  293.3 10.7 %collective-permute-start.13 = (f32[1,16,128]{2,1,0:T(8,128)S(1)}, f32[1,16,128]{2,1,0:T(8,128)S(1)}, u32[]{:S(2)}, u32[]{:S(2)}) collective-permute-start(f32[1,16,128]{2,1,0:T(8,128)S(1)} %select_bitcast_fusion.4), channel_id=1, source_target_pairs={{4,0},{8,4},{12,8},{16,12},{20,16},{24,20},{28,24},{32,28},{36,32}... | collective-permute-start | bytes 24584 | tf_op jit(solution)/shard_map/ppermute | solution.py:24
  367.2 16.2 %collective-permute-start.14 = (f32[1,16,128]{2,1,0:T(8,128)S(1)}, f32[1,16,128]{2,1,0:T(8,128)S(1)}, u32[]{:S(2)}, u32[]{:S(2)}) collective-permute-start(f32[1,16,128]{2,1,0:T(8,128)S(1)} %select_bitcast_fusion.3), channel_id=1, source_target_pairs={{0,4},{4,8},{8,12},{12,16},{16,20},{20,24},{24,28},{28,32},{32,36}... | collective-permute-start | bytes 24584 | tf_op jit(solution)/shard_map/ppermute | solution.py:21
  369.2 15.1 %collective-permute-start.15 = (f32[1,16,128]{2,1,0:T(8,128)S(1)}, f32[1,16,128]{2,1,0:T(8,128)S(1)}, u32[]{:S(2)}, u32[]{:S(2)}) collective-permute-start(f32[1,16,128]{2,1,0:T(8,128)S(1)} %select_bitcast_fusion.2), channel_id=1, source_target_pairs={{4,0},{8,4},{12,8},{16,12},{20,16},{24,20},{28,24},{32,28},{36,32}... | collective-permute-start | bytes 24584 | tf_op jit(solution)/shard_map/ppermute | solution.py:24
  385.1 10.8 %collective-permute-start.16 = (f32[4,128,128]{1,2,0:T(8,128)S(1)}, f32[4,128,128]{1,2,0:T(8,128)S(1)}, u32[]{:S(2)}, u32[]{:S(2)}) collective-permute-start(f32[4,128,128]{1,2,0:T(8,128)S(1)} %get-tuple-element.28), channel_id=1, source_target_pairs={{0,1},{1,2},{2,3},{4,5},{5,6},{6,7},{8,9},{9,10},{10,11},{12,13},{... | collective-permute-start | bytes 786440 | tf_op jit(solution)/shard_map/ppermute | solution.py:21
  392.7 11.7 %collective-permute-start.17 = (f32[4,128,128]{1,2,0:T(8,128)S(1)}, f32[4,128,128]{1,2,0:T(8,128)S(1)}, u32[]{:S(2)}, u32[]{:S(2)}) collective-permute-start(f32[4,128,128]{1,2,0:T(8,128)S(1)} %get-tuple-element.29), channel_id=1, source_target_pairs={{1,0},{2,1},{3,2},{5,4},{6,5},{7,6},{9,8},{10,9},{11,10},{13,12},{... | collective-permute-start | bytes 786440 | tf_op jit(solution)/shard_map/ppermute | solution.py:24
  423.1 11.7 %collective-permute-start.18 = (f32[1,16,126]{2,1,0:T(8,128)S(1)}, f32[1,16,126]{2,1,0:T(8,128)S(1)}, u32[]{:S(2)}, u32[]{:S(2)}) collective-permute-start(f32[1,16,126]{2,1,0:T(8,128)S(1)} %select_bitcast_fusion.1), channel_id=1, source_target_pairs={{0,4},{4,8},{8,12},{12,16},{16,20},{20,24},{24,28},{28,32},{32,36}... | collective-permute-start | bytes 24200 | tf_op jit(solution)/shard_map/ppermute | solution.py:21
  425.0 10.6 %collective-permute-start.19 = (f32[1,16,126]{2,1,0:T(8,128)S(1)}, f32[1,16,126]{2,1,0:T(8,128)S(1)}, u32[]{:S(2)}, u32[]{:S(2)}) collective-permute-start(f32[1,16,126]{2,1,0:T(8,128)S(1)} %select_bitcast_fusion), channel_id=1, source_target_pairs={{4,0},{8,4},{12,8},{16,12},{20,16},{24,20},{28,24},{32,28},{36,32}... | collective-permute-start | bytes 24200 | tf_op jit(solution)/shard_map/ppermute | solution.py:24
  439.4 20.9 %all-to-all-start.6 = ((f32[16,4,3969]{2,0,1:T(8,128)}), f32[16,4,3969]{2,0,1:T(8,128)S(1)}, u32[]{:S(2)}, u32[]{:S(2)}) async-start(f32[16,4,3969]{2,0,1:T(8,128)} %copy.217), calls=%async_computation.6 | async-start | bytes 2097152 | tf_op jit(solution)/shard_map/all_to_all | solution.py:150
  443.2 17.1 %copy-start.19 = (f32[62,64]{1,0:T(8,128)S(1)}, f32[62,64]{1,0:T(8,128)}, u32[]{:S(2)}) copy-start(f32[62,64]{1,0:T(8,128)} %param.26) | copy-start | bytes 47620
  (13 other events, 25.0 us)
where the time goes:
time: 472 us; the launch traced here: 464 us
  starting transfers between devices  150 us (32%)
  blocking collectives  127 us (27%)
  waiting for transfers between devices  63.7 us (13%)
  matrix products  63.6 us (13%)
  local copies, waits for them, and re-layouts  39.7 us (8%)
  other arithmetic  11.2 us (2%)
  between operations  7.62 us (2%)
    ppermute x10, starting transfers between devices, with_halo(): lax.ppermute(lax.slice_in_dim(block, 0, width, axis=dim), axis, backward)  88.8 us
    all_to_all x3, blocking collectives, smooth(): lax.all_to_all(back_rows, 'slab', split_axis=0, concat_axis=1, tiled=True)  86.2 us
    ppermute x10, starting transfers between devices, with_halo(): lax.ppermute(lax.slice_in_dim(block, block.shape[dim] - width, None, axis...  51.9 us
    all_to_all x2, blocking collectives, smooth(): lax.all_to_all(second, 'slab', split_axis=1, concat_axis=0, tiled=True)  41.3 us
    ppermute x10, waiting for transfers between devices, with_halo(): lax.ppermute(lax.slice_in_dim(block, 0, width, axis=dim), axis, backward)  27.8 us
    all_to_all x1, waiting for transfers between devices, smooth(): lax.all_to_all(second, 'slab', split_axis=1, concat_axis=0, tiled=True)  17.9 us
    all_to_all x1, waiting for transfers between devices, per_device(): lax.all_to_all(flattened, 'slab', split_axis=1, concat_axis=0, tiled=True)  15.9 us
  transfers between devices with their start and end apart: 22, of which 14 were waited for; matrix products, arithmetic and copies ran while one was open for 2% of the time, Pallas kernels for 0%

commit v1 on v0

v1 whole, which is shorter than its diff:
```python
import jax
import jax.numpy as jnp
from jax import lax
from jax.experimental import pallas as pl
from jax.experimental.pallas import tpu as pltpu
from jax.sharding import PartitionSpec as P

BAND = 4
SWEEPS = 3
DAMPING = 0.25
KEEP = 1.0 - DAMPING
HIGHEST = lax.Precision.HIGHEST
F32 = jnp.float32
BF16 = jnp.bfloat16

N = 128
LAYERS = 64
HALF = 32
BLOCK = 16
REACH = HALF + BAND
ROWS = 40
TOP = HALF - BAND
CHUNK = 32
COARSE = N - 2


def split(x):
    high = x.astype(BF16)
    return high, (x - high.astype(F32)).astype(BF16)


def right_mul(x, packed):
    high, low = split(x)
    both = jnp.dot(jnp.concatenate([high, low], axis=-1), packed, preferred_element_type=F32)
    return both[:, :N] + both[:, N:]


def left_mul_planes(packed, planes):
    out = []
    for q in range(0, len(planes), 2):
        high, low = split(jnp.concatenate(planes[q:q + 2], axis=1))
        wide = jnp.dot(packed, jnp.concatenate([high, high], axis=0), preferred_element_type=F32)
        wide = wide + jnp.dot(packed[:, :N], low, preferred_element_type=F32)
        out += [wide[:, :N], wide[:, N:]]
    return out


def dot_full(x, y):
    return jnp.dot(x, y, precision=HIGHEST, preferred_element_type=F32)


def pack_right(a):
    high, low = split(a)
    top = jnp.concatenate([high, low], axis=1)
    bottom = jnp.concatenate([high, jnp.zeros_like(low)], axis=1)
    return jnp.concatenate([top, bottom], axis=0)


def pack_left(a):
    return jnp.concatenate(split(a), axis=1)


def call(kernel, outs, ints, *args, flops=0, scratch=(), floats=None):
    smem = [ints] if floats is None else [ints, floats]
    specs = [pl.BlockSpec(memory_space=pltpu.SMEM)] * len(smem)
    specs += [pl.BlockSpec(memory_space=pltpu.VMEM)] * len(args)
    shapes = [s if isinstance(s, jax.ShapeDtypeStruct) else jax.ShapeDtypeStruct(s, F32) for s in outs]
    moved = sum(a.size * a.dtype.itemsize for a in args) + sum(4 * s.size for s in shapes)
    return pl.pallas_call(
        kernel,
        out_shape=shapes,
        in_specs=specs,
        out_specs=[pl.BlockSpec(memory_space=pltpu.VMEM)] * len(outs),
        scratch_shapes=list(scratch),
        compiler_params=pltpu.CompilerParams(vmem_limit_bytes=20 * 1024 * 1024),
        cost_estimate=pl.CostEstimate(
            flops=flops, bytes_accessed=moved, transcendentals=0
        ),
    )(*smem, *args)


def source_layer(ints, t):
    inside = jnp.where(ints[2] == 1, HALF - 1 - t, t)
    return inside // BLOCK, inside % BLOCK


def load_layer(ints, own_ref, other_ref, out_ref, t):
    block, index = source_layer(ints, t)
    mine = own_ref[index]
    theirs = other_ref[index]
    value = jnp.where(block == ints[3], mine, theirs)
    out_ref[t] = value

    @pl.when(ints[1] == 1)
    def _():
        out_ref[t] = value.T


def slots(ints, west, east, slot_refs):
    odd = ints[0] == 1
    slot_refs[0][...] = jnp.where(odd, east, west)
    slot_refs[1][...] = jnp.where(odd, west, east)


def sides(ints, received0, received1):
    odd = ints[0] == 1
    return jnp.where(odd, received1, received0), jnp.where(odd, received0, received1)


def face_rows(ints, ref, side):
    position = ints[4 + side]
    return jnp.where(position == 0, ref[:, 0, :], ref[:, N - 1, :])


def load_kernel(ints, own, other, scal, f_ref, pay_ref, slot0, slot1):
    def body(t, carry):
        load_layer(ints, own, other, f_ref, t)
        return carry

    lax.fori_loop(0, HALF, body, 0, unroll=4)
    packs = []
    for side in range(2):
        rows = face_rows(ints, f_ref, side)
        packs.append(
            jnp.concatenate([rows, jnp.zeros((ROWS - HALF, N), F32), scal[side]], axis=0)
        )
        pay_ref[side] = packs[side]
    slots(ints, packs[0], packs[1], (slot0, slot1))


def reaction_kernel(ints, own, other, r_ref, face_ref):
    def body(t, carry):
        load_layer(ints, own, other, r_ref, t)
        return carry

    lax.fori_loop(0, HALF, body, 0, unroll=4)
    for side in range(2):
        face_ref[side] = face_rows(ints, r_ref, side)


def forward_planes(x, wb, lbt):
    count = x.shape[0]
    first = right_mul(x.reshape(count * N, N), wb).reshape(count, N, N)
    return left_mul_planes(lbt, [first[q] for q in range(count)])


GROUP = 16


def transform_kernel(ints, f_ref, wb, lbt, out_ref):
    def body(g, carry):
        t = g * GROUP
        planes = forward_planes(f_ref[pl.ds(t, GROUP)], wb[...], lbt[...])
        for q in range(GROUP):
            out_ref[t + q] = planes[q]
        return carry

    lax.fori_loop(0, HALF // GROUP, body, 0)


FACTOR_ROWS = 16


def factor_kernel(
    ints, alpha_ref, bands, modes, l_ref, dinv_ref, lu_ref, lo_ref, do_ref, mend_ref, zs
):
    def coefficient(alpha, which, t, d):
        return alpha * bands[which, 0, d, t:t + 1, :] + bands[which, 1, d, t:t + 1, :]

    def mode(which, t):
        return modes[which, t:t + 1, :]

    def row_weights(a, l, t, least):
        w = {}
        for d in range(min(BAND, t), least - 1, -1):
            v = a[d]
            for m in range(d + 1, min(BAND, t) + 1):
                v = v - w[m] * l[t - d][m - d]
            w[d] = v
        return w

    def eliminate(a, l, dinv, t):
        w = row_weights(a, l, t, 1)
        row = {d: w[d] * dinv[t - d] for d in w}
        pivot = a[0]
        for d in w:
            pivot = pivot - w[d] * row[d]
        return row, 1.0 / pivot

    def body(c, carry):
        part = pl.ds(c * FACTOR_ROWS, FACTOR_ROWS)
        alpha = alpha_ref[part, :]
        l, dinv, sent = {}, {}, {}
        for t in range(HALF):
            a = [coefficient(alpha, 1, t, d) for d in range(min(BAND, t) + 1)]
            l[t], dinv[t] = eliminate(a, l, dinv, t)
            sent[t] = jnp.broadcast_to(mode(2, t), alpha.shape)
            for d in l[t]:
                sent[t] = sent[t] - l[t][d] * sent[t - d]
            if t >= TOP:
                for d in range(1, BAND + 1):
                    lo_ref[t - TOP, d - 1, part, :] = l[t][d]
                do_ref[t - TOP, part, :] = dinv[t]
        outer = {}
        for j in range(BAND):
            t = HALF + j
            a = [coefficient(alpha, 1, t, d) for d in range(BAND + 1)]
            outer[j] = row_weights(a, l, t, j + 1)
            l[t] = {d: outer[j][d] * dinv[t - d] for d in outer[j]}
            for d in range(1, BAND + 1):
                lo_ref[BAND + j, d - 1, part, :] = l[t][d] if d in l[t] else jnp.zeros_like(alpha)
        schur = {}
        for j in range(BAND):
            for i in range(j + 1):
                total = None
                for s in range(TOP + j, HALF):
                    term = outer[j][HALF + j - s] * l[HALF + i][HALF + i - s] if HALF + i - s <= BAND else None
                    if term is not None:
                        total = term if total is None else total + term
                schur[(j, i)] = schur[(i, j)] = total
        shift = {}
        for j in range(BAND):
            for d in range(j + 1, BAND + 1):
                term = l[HALF + j][d] * sent[HALF + j - d]
                shift[j] = term if j not in shift else shift[j] + term
        l, dinv, z = {}, {}, {}
        plain, plain_inv = None, None
        for t in range(HALF):
            a = [coefficient(alpha, 0, t, d) for d in range(min(BAND, t) + 1)]
            if t == TOP:
                plain, plain_inv = dict(l), dict(dinv)
            if t >= TOP:
                plain[t], plain_inv[t] = eliminate(a, plain, plain_inv, t)
                for d in range(1, BAND + 1):
                    lu_ref[t - TOP, d - 1, part, :] = plain[t][d]
                j = HALF - 1 - t
                for d in range(t - TOP + 1):
                    a[d] = a[d] - schur[(j, j + d)]
            l[t], dinv[t] = eliminate(a, l, dinv, t)
            for d in range(1, BAND + 1):
                l_ref[t, d - 1, part, :] = l[t][d] if d in l[t] else jnp.zeros_like(alpha)
            dinv_ref[t, part, :] = dinv[t]
            z[t] = jnp.broadcast_to(mode(1, t), alpha.shape)
            if t >= TOP:
                z[t] = z[t] - shift[HALF - 1 - t]
            for d in l[t]:
                z[t] = z[t] - l[t][d] * z[t - d]
            zs[t] = z[t]
        exact = 1.0 / (alpha + modes[3, 0:1, :])
        y, miss, norm = {}, jnp.zeros_like(alpha), jnp.zeros_like(modes[3, 0:1, :])
        for t in range(HALF - 1, -1, -1):
            y[t] = zs[t] * dinv_ref[t, part, :]
            for d in range(1, min(BAND, HALF - 1 - t) + 1):
                y[t] = y[t] - l_ref[t + d, d - 1, part, :] * y[t + d]
            miss = miss + mode(1, t) * (mode(0, t) * exact - y[t])
            norm = norm + mode(1, t) * mode(0, t)
        mend_ref[part, :] = jnp.where(norm > 0.01, miss / jnp.maximum(norm, 0.01), 0.0)
        return carry

    lax.fori_loop(0, N // FACTOR_ROWS, body, 0)


def four(get):
    return [get(side, who) for side in range(2) for who in range(2)]


def vertical_apply(products, vert, scal_k, scal_m, scal_v):
    mass = [k * p[:, :N] + m * p[:, N:] for p, k, m in zip(products, scal_k, scal_m)]
    stiff = [v * p[:, :N] for p, v in zip(products, scal_v)]
    out = dot_full(vert[0], jnp.concatenate(mass, axis=1))
    out = out + dot_full(vert[1], jnp.concatenate(stiff, axis=1))
    return [out[:, q * N:(q + 1) * N] for q in range(len(products))]


def plane_products(faces, mk):
    stacked = dot_full(jnp.concatenate(faces, axis=0), mk[...])
    return [stacked[q * ROWS:(q + 1) * ROWS] for q in range(len(faces))]


def flip_masks(scal, nscal):
    return [scal[side, 3:4, :] != nscal[side, 3:4, :] for side in range(2)]


def orient_all(arrays, mirror, masks):
    turned = dot_full(jnp.concatenate([a for _, a in arrays], axis=0), mirror[...])
    return [
        jnp.where(masks[side], turned[q * ROWS:(q + 1) * ROWS], a)
        for q, (side, a) in enumerate(arrays)
    ]


def update_faces(c_faces, state, scal, nscal, mirror, mk, vert):
    masks = flip_masks(scal, nscal)
    residual = four(lambda side, who: state[4][2 * side + who])
    arrays = []
    for side in range(2):
        for who in range(2):
            arrays.append((side, c_faces[2 * side + 1 - who]))
    for side in range(2):
        for who in range(2):
            arrays.append((side, residual[2 * side + 1 - who]))
    turned = orient_all(arrays, mirror, masks)
    e, added = turned[:4], turned[4:]
    products = plane_products(e, mk)
    which = four(lambda side, who: (nscal if who else scal)[side])
    applied = vertical_apply(
        products, vert, [w[0:1] for w in which], [w[1:2] for w in which], [w[2:3] for w in which]
    )
    new = [list(state[s]) for s in range(6)]
    for q in range(4):
        new[2][q] = state[2][q] + DAMPING * (c_faces[q] + e[q])
        new[3][q] = state[3][q] + DAMPING * (residual[q] + added[q] + applied[q])
        new[4][q] = state[0][q] - state[1][q] * new[2][q] - new[3][q]
        new[5][q] = KEEP * state[5][q] + DAMPING * e[q]
    return new, e, masks


def read_state(ref):
    return [[ref[s, q] for q in range(4)] for s in range(6)]


def pad_rows(x):
    return jnp.concatenate([x, jnp.zeros((ROWS - x.shape[0], N), F32)], axis=0)


def eliminate_forward(gh_ref, spread, rows_hat, l_ref, lu_ref, modes, z_ref, msg_ref):
    def body(c, carry):
        part = pl.ds(pl.multiple_of(c * CHUNK, CHUNK), CHUNK)
        west, east = spread[0, part, :], spread[1, part, :]
        z = {}
        lowest = jnp.zeros_like(west)
        for t in range(HALF):
            x = gh_ref[t, part, :] + west * rows_hat[0, t:t + 1, :] + east * rows_hat[1, t:t + 1, :]
            lowest = lowest + modes[0, t:t + 1, :] * x
            z_ref[t, part, :] = x
            table, index = (l_ref, t) if t < TOP else (lu_ref, t - TOP)
            for d in range(1, min(BAND, t) + 1):
                x = x - table[index, d - 1, part, :] * z[t - d]
            z[t] = x
            if t < TOP:
                z_ref[t, part, :] = x
            else:
                msg_ref[t - TOP, part, :] = x
        msg_ref[BAND, part, :] = lowest
        return carry

    lax.fori_loop(0, N // CHUNK, body, 0)


def first_kernel(
    ints, gh, own_pay, rec0, rec1, scal, spread, b_full, mirror, l_ref, lu_ref, modes,
    z_ref, msg_ref, state_ref, rows_u, rows_g, nscal_ref, rows_hat,
):
    received = sides(ints, rec0[...], rec1[...])
    for side in range(2):
        nscal_ref[side] = received[side][ROWS:ROWS + 8]
    masks = flip_masks(scal, nscal_ref)
    state_ref[...] = jnp.zeros_like(state_ref)
    for side in range(2):
        for who in range(2):
            values = received[side][:ROWS] if who else own_pay[side, :ROWS]
            state_ref[0, 2 * side + who] = values
            state_ref[4, 2 * side + who] = values
    turned = orient_all([(side, received[side][:ROWS]) for side in range(2)], mirror, masks)
    rows_u[...] = jnp.zeros_like(rows_u)
    for side in range(2):
        rows_g[side] = turned[side]
        rows_hat[side] = dot_full(turned[side], b_full[...])
    eliminate_forward(gh, spread, rows_hat, l_ref, lu_ref, modes, z_ref, msg_ref)


def next_kernel(
    ints, gh, own_pay, rec0, rec1, state_in, scal, nscal, spread, b_full, mirror, mk, vert,
    l_ref, lu_ref, modes, z_ref, msg_ref, state_ref, rows_u, rows_g, rows_hat,
):
    received = sides(ints, rec0[...], rec1[...])
    state = read_state(state_in)
    if own_pay.shape[1] > ROWS:
        for side in range(2):
            state[1][2 * side] = pad_rows(own_pay[side, ROWS:])
            state[1][2 * side + 1] = pad_rows(received[side][ROWS:])
    c_faces = four(lambda side, who: received[side][:ROWS] if who else own_pay[side, :ROWS])
    state, e, masks = update_faces(c_faces, state, scal, nscal, mirror, mk, vert)
    for s in range(6):
        for q in range(4):
            state_ref[s, q] = state[s][q]
    turned = orient_all([(side, state[4][2 * side + 1]) for side in range(2)], mirror, masks)
    for side in range(2):
        step = DAMPING * e[2 * side]
        rows = turned[side] - state[1][2 * side] * step
        rows_u[side] = step
        rows_g[side] = rows
        rows_hat[side] = dot_full(rows, b_full[...])
    eliminate_forward(gh, spread, rows_hat, l_ref, lu_ref, modes, z_ref, msg_ref)


def solve_kernel(
    ints, z_ref, msg_ref, zr_ref, l_ref, dinv_ref, lo_ref, do_ref, mend, modes, spread, bt_full, state, extra,
    y_ref, pay_ref, slot0, slot1, sums,
):
    sums[...] = jnp.zeros_like(sums)

    def body(c, carry):
        part = pl.ds(pl.multiple_of(c * CHUNK, CHUNK), CHUNK)
        sent = [zr_ref[s, part, :] for s in range(BAND)]
        weights = (spread[0, part, :], spread[1, part, :])

        low = mend[part, :] * (msg_ref[BAND, part, :] + zr_ref[BAND, part, :])

        def put(t, value):
            value = value + low * modes[0, t:t + 1, :]
            y_ref[t, part, :] = value
            for side in range(2):
                product = weights[side] * value
                total = product[0:8]
                for s in range(8, CHUNK, 8):
                    total = total + product[s:s + 8]
                sums[side, t] += total

        z = {t: z_ref[t, part, :] for t in range(TOP - BAND, HALF)}
        for j in range(BAND):
            for d in range(j + 1, BAND + 1):
                z[HALF - 1 - j] = z[HALF - 1 - j] - lo_ref[BAND + j, d - 1, part, :] * sent[BAND + j - d]
        for t in range(TOP, HALF):
            for d in range(1, BAND + 1):
                z[t] = z[t] - l_ref[t, d - 1, part, :] * z[t - d]
        y = {}
        for t in range(HALF - 1, TOP - 1, -1):
            value = z[t] * dinv_ref[t, part, :]
            for d in range(1, HALF - t):
                value = value - l_ref[t + d, d - 1, part, :] * y[t + d]
            y[t] = value
            put(t, value)
        far = {HALF + j: y[HALF - 1 - j] for j in range(BAND)}
        for t in range(HALF - 1, TOP - 1, -1):
            value = sent[t - TOP] * do_ref[t - TOP, part, :]
            for d in range(1, BAND + 1):
                value = value - lo_ref[t + d - TOP, d - 1, part, :] * far[t + d]
            far[t] = value
            put(2 * HALF - 1 - t, value)
        for t in range(TOP - 1, -1, -1):
            source = z[t] if t in z else z_ref[t, part, :]
            value = source * dinv_ref[t, part, :]
            for d in range(1, BAND + 1):
                value = value - l_ref[t + d, d - 1, part, :] * y[t + d]
            y[t] = value
            put(t, value)
        return carry

    lax.fori_loop(0, N // CHUNK, body, 0)
    mixed = jnp.sum(sums[...], axis=2)
    faces = dot_full(mixed.reshape(2 * ROWS, N), bt_full[...])
    packs = []
    for side in range(2):
        c = faces[side * ROWS:(side + 1) * ROWS] - state[2, 2 * side]
        pay_ref[side, :ROWS] = c
        if pay_ref.shape[1] > ROWS:
            pay_ref[side, ROWS:] = extra[side]
    slots(ints, pay_ref[0], pay_ref[1], (slot0, slot1))


def back_planes(y, wbt, lb):
    count = y.shape[0]
    across = right_mul(y.reshape(count * N, N), wbt).reshape(count, N, N)
    return left_mul_planes(lb, [across[q] for q in range(count)])


def make_plane_kernel(sweep):
    last = sweep == SWEEPS - 1

    def kernel(*refs):
        refs = list(refs)
        refs.pop(0)
        y_ref, f_ref, r_ref, rows_u, rows_g, mask, wbt, lb = refs[:8]
        refs = refs[8:]
        if sweep > 0:
            up_in, g_in = refs[:2]
            refs = refs[2:]
        if last:
            wrt, lr, cut, pay_in = refs[:4]
            up_out, coarse_out, pay_out, slot0, slot1, sums = refs[4:]
        else:
            wb, lbt = refs[:2]
            up_out, g_out, gh_out = refs[2:]

        def on_faces(rows, t):
            return mask[0] * rows[0, pl.ds(t, 1), :] + mask[1] * rows[1, pl.ds(t, 1), :]

        def body(g, carry):
            t0 = g * GROUP
            corrections = back_planes(y_ref[pl.ds(t0, GROUP)], wbt[...], lb[...])
            fresh = []
            for q in range(GROUP):
                t = t0 + q
                on_u, on_g = on_faces(rows_u, t), on_faces(rows_g, t)
                load, react = f_ref[t], r_ref[t]
                if sweep == 0:
                    u, total = on_u, DAMPING * (load + on_g)
                else:
                    old = up_in[t]
                    u = old + on_u
                    total = KEEP * g_in[t] + DAMPING * (load - react * old + on_g)
                new = KEEP * u + DAMPING * corrections[q]
                up_out[t] = new
                residual = load - react * new
                if last:
                    residual = residual - total
                    for side in range(2):
                        product = cut[side] * residual
                        part = product[0:8]
                        for s in range(8, N, 8):
                            part = part + product[s:s + 8]
                        sums[side, t] = part
                else:
                    g_out[t] = total
                fresh.append(residual)
            stacked = jnp.concatenate(fresh, axis=0).reshape(GROUP, N, N)
            if last:
                planes = forward_planes(stacked, wrt[...], lr[...])
            else:
                planes = forward_planes(stacked, wb[...], lbt[...])
            for q in range(GROUP):
                (coarse_out if last else gh_out)[t0 + q] = planes[q]
            return carry

        lax.fori_loop(0, HALF // GROUP, body, 0)
        if last:
            ints = kernel_ints[0]
            for side in range(2):
                pay_out[side, :ROWS] = pay_in[side, :ROWS]
                pay_out[side, ROWS:] = jnp.sum(sums[side], axis=1)
            slots(ints, pay_out[0], pay_out[1], (slot0, slot1))

    kernel_ints = []

    def outer(ints, *refs):
        kernel_ints.clear()
        kernel_ints.append(ints)
        kernel(ints, *refs)

    return outer


def final_kernel(
    ints, floats, up, coarse_in, own_pay, rec0, rec1, state_in, scal, nscal, mirror, mirror_coarse, mk, vert,
    rt_full, mask, profile, out_u, out_d, parts, plane,
):
    received = sides(ints, rec0[...], rec1[...])
    state = read_state(state_in)
    c_faces = four(lambda side, who: received[side][:ROWS] if who else own_pay[side, :ROWS])
    state, e, masks = update_faces(c_faces, state, scal, nscal, mirror, mk, vert)
    gathered = state[5]
    products = plane_products(gathered, mk)
    far = vertical_apply(
        [products[1], products[3]], vert,
        [nscal[side, 4:5] for side in range(2)],
        [nscal[side, 5:6] for side in range(2)],
        [nscal[side, 6:7] for side in range(2)],
    )
    one = floats[0]
    near_stiff = vertical_apply([products[0], products[2]], vert, [one] * 2, [floats[3]] * 2, [floats[3]] * 2)
    near_mass = vertical_apply([products[0], products[2]], vert, [floats[3]] * 2, [floats[1]] * 2, [floats[2]] * 2)
    stack = []
    for side in range(2):
        nbr = 2 * side + 1
        theirs = pad_rows(received[side][ROWS:])
        theirs = theirs - nscal[side, 7:8] * DAMPING * state[1][nbr] * e[nbr] - far[side]
        mine = scal[side, 7:8] * DAMPING * state[1][2 * side] * e[2 * side]
        stack += [near_stiff[side], near_mass[side], mine, theirs]
    restricted = dot_full(jnp.concatenate(stack, axis=0), rt_full[...])
    pieces = [restricted[q * ROWS:(q + 1) * ROWS] for q in range(8)]
    turned = dot_full(jnp.concatenate([pieces[3], pieces[7]], axis=0), mirror_coarse[...])
    for side in range(2):
        added = jnp.where(masks[side], turned[side * ROWS:(side + 1) * ROWS], pieces[4 * side + 3])
        parts[3 * side] = -pieces[4 * side]
        parts[3 * side + 1] = -pieces[4 * side + 1]
        parts[3 * side + 2] = added - pieces[4 * side + 2]

    def coarse_body(t, carry):
        value = coarse_in[t]
        for s in range(6):
            value = value + profile[s] * parts[s, pl.ds(t, 1), :]
        plane[...] = value

        @pl.when(ints[1] == 1)
        def _():
            plane[...] = value.T

        @pl.when(ints[3] == 0)
        def _():
            out_d[0, t] = plane[0:32]
            out_d[1, t] = plane[63:95]

        @pl.when(ints[3] == 1)
        def _():
            out_d[0, t] = plane[31:63]
            out_d[1, t] = plane[94:126]

        return carry

    lax.fori_loop(0, HALF, coarse_body, 0, unroll=2)

    for side in range(2):
        parts[side] = DAMPING * e[2 * side]

    def u_body(index, carry):
        inside = ints[3] * BLOCK + index
        t = jnp.where(ints[2] == 1, HALF - 1 - inside, inside)
        value = up[t] + mask[0] * parts[0, pl.ds(t, 1), :] + mask[1] * parts[1, pl.ds(t, 1), :]
        out_u[index] = value

        @pl.when(ints[1] == 1)
        def _():
            out_u[index] = value.T

        return carry

    lax.fori_loop(0, BLOCK, u_body, 0, unroll=2)


def prepare_kernel(
    ints, floats, stiff, mass, stiff_v, mass_v, basis, eigen, basis_v, eigen_v, restrict,
    wb, wbt, wrt, lb, lbt, lr, bt_out, rt_out, mk, mirror, mirror_coarse, vert, scal, spread, mask, cut,
    profile, alpha, bands, modes,
):
    a1, a2, a3 = floats[0], floats[1], floats[2]
    rows = lax.broadcasted_iota(jnp.int32, (N, N), 0)
    lanes = lax.broadcasted_iota(jnp.int32, (N, N), 1)
    eye = rows == lanes

    def column(row):
        picked = jnp.sum(jnp.where(eye, row, 0.0), axis=1, keepdims=True)
        return jnp.broadcast_to(picked, (N, N))

    b, k, m = basis[...], stiff[...], mass[...]
    bt = b.T
    r = jnp.concatenate([restrict[...], jnp.zeros((N - COARSE, N), F32)], axis=0)
    rt = r.T
    wb[...], wbt[...], wrt[...] = pack_right(b), pack_right(bt), pack_right(rt)
    lb[...], lbt[...], lr[...] = pack_left(b), pack_left(bt), pack_left(r)
    bt_out[...], rt_out[...] = bt, rt
    mk[:, :N], mk[:, N:] = m, k
    mirror[...] = (rows + lanes == N - 1).astype(F32)
    mirror_coarse[...] = (rows + lanes == COARSE - 1).astype(F32)
    alpha[...] = a1 * column(eigen[...]) + a2 * eigen[...]

    turn = (
        lax.broadcasted_iota(jnp.int32, (LAYERS, LAYERS), 0)
        + lax.broadcasted_iota(jnp.int32, (LAYERS, LAYERS), 1)
        == LAYERS - 1
    ).astype(F32)
    first = ints[2] == 0
    kv, mv = stiff_v[...], mass_v[...]
    ordered = []
    for matrix in (mv, a3 * kv):
        turned = dot_full(dot_full(turn, matrix), turn)
        ordered.append((jnp.where(first, matrix, turned), jnp.where(first, turned, matrix)))
    deep = lax.broadcasted_iota(jnp.int32, (ROWS, LAYERS), 0)
    wide = lax.broadcasted_iota(jnp.int32, (ROWS, LAYERS), 1)
    inside = (deep < HALF) & (wide < REACH)
    own_stiff = jnp.where(first, kv, dot_full(dot_full(turn, kv), turn))
    vert[0] = jnp.where(inside, ordered[0][0][:ROWS], 0.0)[:, :ROWS]
    vert[1] = jnp.where(inside, own_stiff[:ROWS], 0.0)[:, :ROWS]
    for which in range(2):
        for s in range(2):
            for d in range(BAND + 1):
                picked = jnp.where(deep - wide == d, ordered[s][which][:ROWS], 0.0)
                bands[which, s, d] = jnp.broadcast_to(jnp.sum(picked, axis=1, keepdims=True), (ROWS, N))

    mu = eigen_v[...]
    least = jnp.min(mu, axis=1, keepdims=True)
    number = lax.broadcasted_iota(jnp.int32, (1, LAYERS), 1)
    chosen = jnp.min(jnp.where(mu == least, number, LAYERS), axis=1, keepdims=True)
    low = jnp.sum(jnp.where(number == chosen, basis_v[...], 0.0), axis=1, keepdims=True)
    low = jnp.broadcast_to(low, (LAYERS, N))
    low_mass = dot_full(mv, low)
    low_turned, mass_turned = dot_full(turn, low), dot_full(turn, low_mass)
    modes[0] = jnp.where(first, low, low_turned)[:ROWS]
    modes[1] = jnp.where(first, low_mass, mass_turned)[:ROWS]
    modes[2] = jnp.where(first, mass_turned, low_mass)[:ROWS]
    modes[3] = jnp.broadcast_to(a3 * least, (ROWS, N))

    for side in range(2):
        start = ints[4 + side] == 0

        def end_row(matrix, count=N):
            return jnp.where(start, matrix[0:1, :], matrix[count - 1:count, :])

        def corner(matrix):
            value = jnp.where(start, matrix[0:1, 0:1], matrix[N - 1:N, N - 1:N])
            return jnp.broadcast_to(value, (1, N))

        cut_row = end_row(r, COARSE)
        cut_at = jnp.broadcast_to(jnp.where(start, cut_row[:, 0:1], cut_row[:, N - 1:N]), (1, N))
        stiff_profile = jnp.broadcast_to(jnp.sum(r * end_row(k), axis=1, keepdims=True), (N, N))
        mass_profile = jnp.broadcast_to(jnp.sum(r * end_row(m), axis=1, keepdims=True), (N, N))
        at_face = jnp.where(start, 0, COARSE - 1)
        profile[3 * side] = stiff_profile
        profile[3 * side + 1] = mass_profile
        profile[3 * side + 2] = (rows == at_face).astype(F32)
        spread[side] = column(end_row(b))
        mask[side] = (rows == ints[4 + side]).astype(F32)
        cut[side] = column(cut_row)
        scal[side] = jnp.concatenate(
            [
                corner(k) * a1,
                corner(m) * a2,
                corner(m) * a3,
                jnp.broadcast_to(ints[6].astype(F32), (1, N)),
                end_row(stiff_profile, COARSE) * a1,
                end_row(mass_profile, COARSE) * a2,
                end_row(mass_profile, COARSE) * a3,
                cut_at,
            ],
            axis=0,
        )


def per_device(
    load_vector,
    reaction,
    geometry,
    stiff_plane,
    mass_plane,
    stiff_vertical,
    mass_vertical,
    basis_plane,
    eigen_plane,
    basis_vertical,
    eigen_vertical,
    restrict_plane,
    restrict_vertical,
    patch_links,
):
    slab = lax.axis_index("slab")
    half, core = slab // 2, slab % 2
    patch = lax.axis_index("patch")
    patches = lax.axis_size("patch")
    links = patch_links[0]
    geo = geometry[0]
    kind = links[0] // 2
    west_end, east_end = links[0] % 2, links[1] % 2
    ints = jnp.stack(
        [patch % 2, kind, half, core, (N - 1) * west_end, (N - 1) * east_end, links[2], kind]
    ).astype(jnp.int32)
    a1 = jnp.where(kind == 0, geo[0], geo[1])
    a2 = jnp.where(kind == 0, geo[1], geo[0])
    floats = jnp.stack([a1, a2, geo[2], jnp.zeros_like(a1)])
    square, two = (N, N), (2, N, N)
    right = jax.ShapeDtypeStruct((2 * N, 2 * N), BF16)
    left = jax.ShapeDtypeStruct((N, 2 * N), BF16)
    (
        wb, wbt, wrt, lb, lbt, lr, basis_t, restrict_t, mk, mirror, mirror_coarse, vert, scal, spread, mask,
        cut, profile, alpha, bands, modes,
    ) = call(
        prepare_kernel,
        [
            right, right, right, left, left, left, square, square, (N, 2 * N), square, square,
            (2, ROWS, ROWS), (2, 8, N), two, two, two, (6, N, N), square, (2, 2, BAND + 1, ROWS, N), (4, ROWS, N),
        ],
        ints, stiff_plane, mass_plane, stiff_vertical, mass_vertical, basis_plane, eigen_plane.reshape(1, N),
        basis_vertical, eigen_vertical.reshape(1, LAYERS), restrict_plane,
        floats=floats, flops=20_000_000,
    )

    pair = [(0, 1), (1, 0), (2, 3), (3, 2)]
    cross = [(0, 2), (2, 0), (1, 3), (3, 1)]
    even = [(i, i ^ 1) for i in range(patches)]
    odd = [(i, (i + 1) % patches if i % 2 else (i - 1) % patches) for i in range(patches)]

    def swap_faces(slot0, slot1):
        return lax.ppermute(slot0, "patch", odd), lax.ppermute(slot1, "patch", even)

    field = (HALF, N, N)
    own_load = load_vector[0].reshape(BLOCK, N, N)
    own_react = reaction[0].reshape(BLOCK, N, N)
    other_load = lax.ppermute(own_load, "slab", pair)
    other_react = lax.ppermute(own_react, "slab", pair)
    size = ROWS + 8
    f, pay, slot0, slot1 = call(
        load_kernel, [field, (2, size, N), (size, N), (size, N)], ints, own_load, other_load, scal
    )
    rec0, rec1 = swap_faces(slot0, slot1)
    r, react_faces = call(reaction_kernel, [field, (2, HALF, N)], ints, own_react, other_react)
    l, dinv, lu, lo, do, mend = call(
        factor_kernel,
        [(HALF, BAND, N, N), field, (BAND, BAND, N, N), (2 * BAND, BAND, N, N), (BAND, N, N), square],
        ints, alpha, bands, modes, scratch=[pltpu.VMEM((HALF, FACTOR_ROWS, N), F32)], flops=40_000_000,
    )
    (gh,) = call(transform_kernel, [field], ints, f, wb, lbt, flops=1_000_000_000)
    rows_hat = pltpu.VMEM((2, ROWS, N), F32)
    sums = pltpu.VMEM((2, ROWS, 8, N), F32)
    message = (BAND + 1, N, N)
    state_shape = (6, 4, ROWS, N)
    rows_shape = (2, ROWS, N)
    up = total = None
    for sweep in range(SWEEPS):
        if sweep == 0:
            z, msg, state, rows_u, rows_g, nscal = call(
                first_kernel,
                [field, message, state_shape, rows_shape, rows_shape, (2, 8, N)],
                ints, gh, pay, rec0, rec1, scal, spread, basis_plane, mirror, l, lu, modes,
                scratch=[rows_hat], flops=10_000_000,
            )
        else:
            z, msg, state, rows_u, rows_g = call(
                next_kernel,
                [field, message, state_shape, rows_shape, rows_shape],
                ints, gh, pay, rec0, rec1, state, scal, nscal, spread, basis_plane, mirror, mk, vert, l, lu, modes,
                scratch=[rows_hat], flops=10_000_000,
            )
        received = lax.ppermute(msg, "slab", cross)
        last = sweep == SWEEPS - 1
        size = ROWS + HALF if sweep == 0 else ROWS
        y, pay, slot0, slot1 = call(
            solve_kernel,
            [(REACH, N, N), (2, size, N), (size, N), (size, N)],
            ints, z, msg, received, l, dinv, lo, do, mend, modes, spread, basis_t, state, react_faces,
            scratch=[sums], flops=10_000_000,
        )
        args = [y, f, r, rows_u, rows_g, mask, wbt, lb]
        if sweep > 0:
            args += [up, total]
        plane_kernel = make_plane_kernel(sweep)
        if last:
            size = ROWS + HALF
            up, coarse, pay, slot0, slot1 = call(
                plane_kernel,
                [field, field, (2, size, N), (size, N), (size, N)],
                ints, *args, wrt, lr, cut, pay,
                scratch=[pltpu.VMEM((2, HALF, 8, N), F32)], flops=2_000_000_000,
            )
            rec0, rec1 = swap_faces(slot0, slot1)
        else:
            rec0, rec1 = swap_faces(slot0, slot1)
            up, total, gh = call(
                plane_kernel, [field, field, field], ints, *args, wb, lbt, flops=2_000_000_000
            )
    out_u, blocks = call(
        final_kernel,
        [(BLOCK, N, N), (2, HALF, 32, N)],
        ints, up, coarse, pay, rec0, rec1, state, scal, nscal, mirror, mirror_coarse, mk, vert,
        restrict_t, mask, profile, floats=floats,
        scratch=[pltpu.VMEM((6, ROWS, N), F32), pltpu.VMEM((N, N), F32)], flops=10_000_000,
    )
    kept = lax.dynamic_index_in_dim(blocks, half, 0, keepdims=False)
    sent = lax.dynamic_index_in_dim(blocks, 1 - half, 0, keepdims=False)
    arrived = lax.ppermute(sent, "slab", cross)
    turned = restrict_vertical[:, ::-1]
    near = jnp.where(half == 0, restrict_vertical[:, :HALF], turned[:, :HALF])
    far = jnp.where(half == 0, turned[:, :HALF], restrict_vertical[:, :HALF])
    coarse = jnp.einsum("mt,tcd->mcd", near, kept, precision=HIGHEST)
    coarse = coarse + jnp.einsum("mt,tcd->mcd", far, arrived, precision=HIGHEST)
    flat = coarse[:, :, :COARSE].reshape(coarse.shape[0], 32 * COARSE)
    share = COARSE * COARSE // 4
    flat = lax.dynamic_slice_in_dim(flat, core * (COARSE // 2), share, axis=1)
    return out_u.reshape(1, BLOCK, N * N), flat[None]


def solution(mesh):
    in_specs = (
        P("patch", "slab", None),
        P("patch", "slab", None),
        P("patch", None),
        P(), P(), P(), P(), P(), P(), P(), P(), P(), P(),
        P("patch", None),
    )
    out_specs = (P("patch", "slab", None), P("patch", None, "slab"))
    return jax.shard_map(
        per_device, mesh=mesh, in_specs=in_specs, out_specs=out_specs, check_vma=False
    )
```

time: 472 us -> 215 us (0.46); the launches traced: 464 us -> 214 us
  blocking collectives: 127 us -> 0 us
  starting transfers between devices: 150 us -> 70.5 us
  matrix products: 63.6 us -> 2.2 us
  Pallas kernels: 0 us -> 49.1 us
  local copies, waits for them, and re-layouts: 39.7 us -> 16.9 us
  other arithmetic: 11.2 us -> 0.82 us
    all_to_all x5 -> x0, blocking collectives: 127 us -> none  [the longest x3 86.2 us: smooth(): lax.all_to_all(back_rows, 'slab', split_axis=0, concat_axis=1, tiled=True)]
    ppermute x20 -> x14, starting transfers between devices: 141 us -> 70.5 us  [the longest x4 35.6 us: swap_faces(): lax.ppermute(slot0, 'patch', odd)]
    dot_general x42 -> x2, matrix products: 63.6 us -> 2.2 us  [the longest x1 1.24 us: per_device(): coarse = jnp.einsum('mt,tcd->mcd', near, kept, precision=HIGHEST)]
    pallas_call x0 -> x15, Pallas kernels: none -> 49.1 us  [call(): pl.pallas_call(kernel, out_shape=shapes, in_specs=specs, out_specs=[pl.Bl...]
    ppermute x20 -> x14, waiting for transfers between devices: 30 us -> 66.1 us  [the longest x3 36.7 us: per_device(): received = lax.ppermute(msg, 'slab', cross)]
    all_to_all x2 -> x0, waiting for transfers between devices: 33.8 us -> none  [the longest x1 17.9 us: smooth(): lax.all_to_all(second, 'slab', split_axis=1, concat_axis=0, tiled=True)]
    all_to_all x2 -> x0, starting transfers between devices: 9.55 us -> none  [the longest x1 6.05 us: smooth(): lax.all_to_all(second, 'slab', split_axis=1, concat_axis=0, tiled=True)]
    concatenate x3 -> x0, local copies, waits for them, and re-layouts: 7.99 us -> none  [with_halo(): block = jnp.concatenate([low, block, high], axis=dim)]
  transfers between devices with their start and end apart: 22 -> 14, of which waited for: 14 -> 7; matrix products, arithmetic and copies ran while one was open for 2% -> 3% of each run, Pallas kernels for 0% -> 12%
where the time goes in v1:
time: 215 us; the launch traced here: 214 us
  starting transfers between devices  70.5 us (33%)
  waiting for transfers between devices  66.1 us (31%)
  Pallas kernels  49.1 us (23%)
  local copies, waits for them, and re-layouts  16.9 us (8%)
  between operations  8.21 us (4%)
  matrix products  2.2 us (1%)
    pallas_call x15, Pallas kernels, call(): pl.pallas_call(kernel, out_shape=shapes, in_specs=specs, out_specs=[pl.Bl...  49.1 us
    ppermute x3, waiting for transfers between devices, per_device(): received = lax.ppermute(msg, 'slab', cross)  36.7 us
    ppermute x4, starting transfers between devices, swap_faces(): lax.ppermute(slot0, 'patch', odd)  35.6 us
    ppermute x1, waiting for transfers between devices, per_device(): arrived = lax.ppermute(sent, 'slab', cross)  19.4 us
    ppermute x3, starting transfers between devices, per_device(): received = lax.ppermute(msg, 'slab', cross)  11.2 us
    unnamed x44, local copies, waits for them, and re-layouts  9.56 us
    ppermute x1, starting transfers between devices, per_device(): other_load = lax.ppermute(own_load, 'slab', pair)  8.79 us
    ppermute x4, waiting for transfers between devices, swap_faces(): lax.ppermute(slot1, 'patch', even)  8.68 us
  transfers between devices with their start and end apart: 14, of which 7 were waited for; matrix products, arithmetic and copies ran while one was open for 3% of the time, Pallas kernels for 12%

profile of v1, /device:TPU:1, one launch (start us, length us, event | category | flops | bytes accessed | tf_op | source)
XLA Modules:
  0.0 213.8 jit_solution(13621693391862741886)
XLA Ops:
  2.2 8.8 %collective-permute-start = (f32[16,128,128]{2,1,0:T(8,128)S(1)}, f32[16,128,128]{2,1,0:T(8,128)}, u32[]{:S(2)}, u32[]{:S(2)}) collective-permute-start(f32[16,128,128]{2,1,0:T(8,128)S(1)} %bitcast.35), channel_id=1, source_target_pairs={{0,1},{1,0},{2,3},{3,2},{4,5},{5,4},{6,7},{7,6},{8,9},{9,8},{10,11... | collective-permute-start | bytes 3145736 | tf_op jit(solution)/shard_map/ppermute | solution.py:777
  11.3 1.9 collective-permute-start.4
  27.3 7.9 %shard_map.152 = (f32[32,4,128,128]{3,2,1,0:T(8,128)S(1)}, f32[32,128,128]{2,1,0:T(8,128)S(1)}, f32[4,4,128,128]{3,2,1,0:T(8,128)S(1)}, f32[8,4,128,128]{3,2,1,0...) custom-call(s32[8]{0:T(128)S(1)} %stack.37.ints, f32[128,128]{1,0:T(8,128)S(1)} %get-tuple-element.82.alpha_ref, ...), custom_call_target="tpu_custom_call" | custom-call | flops 40000000 | bytes 14516224 | tf_op jit(solution)/shard_map/pallas_call | solution.py:69
  35.2 1.9 shard_map.150
  37.2 13.2 %collective-permute-start.1 = (f32[48,128]{1,0:T(8,128)S(1)}, f32[48,128]{1,0:T(8,128)S(1)}, u32[]{:S(2)}, u32[]{:S(2)}) collective-permute-start(f32[48,128]{1,0:T(8,128)S(1)} %get-tuple-element.78), channel_id=1, source_target_pairs={{0,508},{4,8},{8,4},{12,16},{16,12},{20,24},{24,20},{28,32},{32,28... | collective-permute-start | bytes 73736 | tf_op jit(solution)/shard_map/ppermute | solution.py:772
  50.4 1.9 collective-permute-start.2
  52.3 2.3 %shard_map.151.gh = f32[32,128,128]{2,1,0:T(8,128)S(1)} custom-call(s32[8]{0:T(128)S(1)} %stack.37.ints, f32[32,128,128]{2,1,0:T(8,128)S(1)} %get-tuple-element.74.f_ref.refs_1_, bf16[256,256]{1,0:T(8,128)(2,1)S(1)} %get-tuple-element.75.wb.refs_8_.refs_10_, bf16[128,256]{1,0:T(8,128)(2,1)S(1)} %get-tuple-element.76.lbt.refs_9_.refs_11_), custom_call_target="tpu_custom_call" | custom-call | flops 1000000000 | bytes 4390912 | tf_op jit(solution)/shard_map/pallas_call | solution.py:69
  54.6 6.9 %collective-permute-done.2.rec1 = f32[48,128]{1,0:T(8,128)S(1)} collective-permute-done((f32[48,128]{1,0:T(8,128)S(1)}, f32[48,128]{1,0:T(8,128)S(1)}, u32[]{:S(2)}, u32[]{:S(2)}) %collective-permute-start.2) | collective-permute-done | bytes 24608 | tf_op jit(solution)/shard_map/ppermute | solution.py:772
  61.5 2.0 shard_map.153
  63.5 2.6 %collective-permute-start.3 = (f32[5,128,128]{2,1,0:T(8,128)S(1)}, f32[5,128,128]{2,1,0:T(8,128)S(1)}, u32[]{:S(2)}, u32[]{:S(2)}) collective-permute-start(f32[5,128,128]{2,1,0:T(8,128)S(1)} %get-tuple-element.88.msg_ref), channel_id=1, source_target_pairs={{0,2},{2,0},{1,3},{3,1},{4,6},{6,4},{5,7},{7,5},{8,10},{10,8},{9,1... | collective-permute-start | bytes 983048 | tf_op jit(solution)/shard_map/ppermute | solution.py:812
  66.1 1.9 shard_map.154
  68.1 10.0 %collective-permute-done.3.zr_ref = f32[5,128,128]{2,1,0:T(8,128)S(1)} collective-permute-done((f32[5,128,128]{2,1,0:T(8,128)S(1)}, f32[5,128,128]{2,1,0:T(8,128)S(1)}, u32[]{:S(2)}, u32[]{:S(2)}) %collective-permute-start.3) | collective-permute-done | bytes 327712 | tf_op jit(solution)/shard_map/ppermute | solution.py:812
  78.1 2.2 %shard_map.155 = (f32[36,128,128]{2,1,0:T(8,128)S(1)}, f32[2,72,128]{2,1,0:T(8,128)S(1)}, f32[72,128]{1,0:T(8,128)S(1)}, f32[72,128]{1,0:T(8,128)S(1)}) custom-call(s32[8]{0:T(128)S(1)} %stack.37.ints, f32[32,128,128]{2,1,0:T(8,128)S(1)} %get-tuple-element.87.z_ref, f32[5,128,128]{2,1,0:T(8,128)S(1)} %get-tuple-element.88.msg_ref, ...), custom_call_target="tpu_custom_call" | custom-call | flops 10000000 | bytes 18972672 | tf_op jit(solution)/shard_map/pallas_call | solution.py:69
  80.3 5.7 %collective-permute-start.5 = (f32[72,128]{1,0:T(8,128)S(1)}, f32[72,128]{1,0:T(8,128)S(1)}, u32[]{:S(2)}, u32[]{:S(2)}) collective-permute-start(f32[72,128]{1,0:T(8,128)S(1)} %get-tuple-element.105), channel_id=1, source_target_pairs={{0,508},{4,8},{8,4},{12,16},{16,12},{20,24},{24,20},{28,32},{32,28... | collective-permute-start | bytes 110600 | tf_op jit(solution)/shard_map/ppermute | solution.py:772
  88.0 4.2 %shard_map.156 = (f32[32,128,128]{2,1,0:T(8,128)S(1)}, f32[32,128,128]{2,1,0:T(8,128)S(1)}, f32[32,128,128]{2,1,0:T(8,128)S(1)}) custom-call(s32[8]{0:T(128)S(1)} %stack.37.ints, f32[36,128,128]{2,1,0:T(8,128)S(1)} %get-tuple-element.96.refs_0_, f32[32,128,128]{2,1,0:T(8,128)S(1)} %get-tuple-element.74.f_ref.refs_1_, ...), custom_call_target="tpu_custom_call" | custom-call | flops 2000000000 | bytes 13451264 | tf_op jit(solution)/shard_map/pallas_call | solution.py:69
  92.2 2.9 %shard_map.157 = (f32[32,128,128]{2,1,0:T(8,128)S(1)}, f32[5,128,128]{2,1,0:T(8,128)S(1)}, f32[6,4,40,128]{3,2,1,0:T(8,128)S(1)}, f32[2,40,128]{2,1,0:T(8,128)S(1)}, f32[2,40,128]{2,1,0:T(8,128)S(1)}) custom-call(s32[8]{0:T(128)S(1)} %stack.37.ints, f32[32,128,128]{2,1,0:T(8,128)S(1)} %get-tuple-element.103.gh, ...), custom_call_target="tpu_custom_call" | custom-call | flops 10000000 | bytes 15675904 | tf_op jit(solution)/shard_map/pallas_call | solution.py:69
  95.1 5.9 %collective-permute-start.7 = (f32[5,128,128]{2,1,0:T(8,128)S(1)}, f32[5,128,128]{2,1,0:T(8,128)S(1)}, u32[]{:S(2)}, u32[]{:S(2)}) collective-permute-start(f32[5,128,128]{2,1,0:T(8,128)S(1)} %get-tuple-element.111.msg_ref), channel_id=1, source_target_pairs={{0,2},{2,0},{1,3},{3,1},{4,6},{6,4},{5,7},{7,5},{8,10},{10,8},{9,1... | collective-permute-start | bytes 983048 | tf_op jit(solution)/shard_map/ppermute | solution.py:812
  101.1 12.1 %collective-permute-done.7.zr_ref = f32[5,128,128]{2,1,0:T(8,128)S(1)} collective-permute-done((f32[5,128,128]{2,1,0:T(8,128)S(1)}, f32[5,128,128]{2,1,0:T(8,128)S(1)}, u32[]{:S(2)}, u32[]{:S(2)}) %collective-permute-start.7) | collective-permute-done | bytes 327712 | tf_op jit(solution)/shard_map/ppermute | solution.py:812
  113.1 2.2 %shard_map.158 = (f32[36,128,128]{2,1,0:T(8,128)S(1)}, f32[2,40,128]{2,1,0:T(8,128)S(1)}, f32[40,128]{1,0:T(8,128)S(1)}, f32[40,128]{1,0:T(8,128)S(1)}) custom-call(s32[8]{0:T(128)S(1)} %stack.37.ints, f32[32,128,128]{2,1,0:T(8,128)S(1)} %get-tuple-element.110.z_ref, f32[5,128,128]{2,1,0:T(8,128)S(1)} %get-tuple-element.111.msg_ref, ...), custom_call_target="tpu_custom_call" | custom-call | flops 10000000 | bytes 18907136 | tf_op jit(solution)/shard_map/pallas_call | solution.py:69
  115.4 8.8 %collective-permute-start.8 = (f32[40,128]{1,0:T(8,128)S(1)}, f32[40,128]{1,0:T(8,128)S(1)}, u32[]{:S(2)}, u32[]{:S(2)}) collective-permute-start(f32[40,128]{1,0:T(8,128)S(1)} %get-tuple-element.120), channel_id=1, source_target_pairs={{0,508},{4,8},{8,4},{12,16},{16,12},{20,24},{24,20},{28,32},{32,28... | collective-permute-start | bytes 61448 | tf_op jit(solution)/shard_map/ppermute | solution.py:772
  126.2 4.4 %shard_map.159 = (f32[32,128,128]{2,1,0:T(8,128)S(1)}, f32[32,128,128]{2,1,0:T(8,128)S(1)}, f32[32,128,128]{2,1,0:T(8,128)S(1)}) custom-call(s32[8]{0:T(128)S(1)} %stack.37.ints, f32[36,128,128]{2,1,0:T(8,128)S(1)} %get-tuple-element.113.refs_0_, f32[32,128,128]{2,1,0:T(8,128)S(1)} %get-tuple-element.74.f_ref.refs_1_, ...), custom_call_target="tpu_custom_call" | custom-call | flops 2000000000 | bytes 17645568 | tf_op jit(solution)/shard_map/pallas_call | solution.py:69
  130.6 3.0 %shard_map.160 = (f32[32,128,128]{2,1,0:T(8,128)S(1)}, f32[5,128,128]{2,1,0:T(8,128)S(1)}, f32[6,4,40,128]{3,2,1,0:T(8,128)S(1)}, f32[2,40,128]{2,1,0:T(8,128)S(1)}, f32[2,40,128]{2,1,0:T(8,128)S(1)}) custom-call(s32[8]{0:T(128)S(1)} %stack.37.ints, f32[32,128,128]{2,1,0:T(8,128)S(1)} %get-tuple-element.118.gh, ...), custom_call_target="tpu_custom_call" | custom-call | flops 10000000 | bytes 15610368 | tf_op jit(solution)/shard_map/pallas_call | solution.py:69
  133.6 2.6 %collective-permute-start.10 = (f32[5,128,128]{2,1,0:T(8,128)S(1)}, f32[5,128,128]{2,1,0:T(8,128)S(1)}, u32[]{:S(2)}, u32[]{:S(2)}) collective-permute-start(f32[5,128,128]{2,1,0:T(8,128)S(1)} %get-tuple-element.123.msg_ref), channel_id=1, source_target_pairs={{0,2},{2,0},{1,3},{3,1},{4,6},{6,4},{5,7},{7,5},{8,10},{10,8},{9,1... | collective-permute-start | bytes 983048 | tf_op jit(solution)/shard_map/ppermute | solution.py:812
  136.2 14.7 %collective-permute-done.10.zr_ref = f32[5,128,128]{2,1,0:T(8,128)S(1)} collective-permute-done((f32[5,128,128]{2,1,0:T(8,128)S(1)}, f32[5,128,128]{2,1,0:T(8,128)S(1)}, u32[]{:S(2)}, u32[]{:S(2)}) %collective-permute-start.10) | collective-permute-done | bytes 327712 | tf_op jit(solution)/shard_map/ppermute | solution.py:812
  150.9 2.9 %shard_map.161 = (f32[36,128,128]{2,1,0:T(8,128)S(1)}, f32[2,40,128]{2,1,0:T(8,128)S(1)}, f32[40,128]{1,0:T(8,128)}, f32[40,128]{1,0:T(8,128)}) custom-call(s32[8]{0:T(128)S(1)} %stack.37.ints, f32[32,128,128]{2,1,0:T(8,128)S(1)} %get-tuple-element.122.z_ref, f32[5,128,128]{2,1,0:T(8,128)S(1)} %get-tuple-element.123.msg_ref, ...), custom_call_target="tpu_custom_call" | custom-call | flops 10000000 | bytes 18907136 | tf_op jit(solution)/shard_map/pallas_call | solution.py:69
  153.8 5.4 %shard_map.162 = (f32[32,128,128]{2,1,0:T(8,128)S(1)}, f32[32,128,128]{2,1,0:T(8,128)S(1)}, f32[2,72,128]{2,1,0:T(8,128)S(1)}, f32[72,128]{1,0:T(8,128)}, f32[72,128]{1,0:T(8,128)}) custom-call(s32[8]{0:T(128)S(1)} %stack.37.ints, f32[36,128,128]{2,1,0:T(8,128)S(1)} %get-tuple-element.125.refs_0_, f32[32,128,128]{2,1,0:T(8,128)S(1)} %get-tuple-element.74.f_ref.refs_1_, ...), custom_call_target="tpu_custom_call" | custom-call | flops 2000000000 | bytes 15867904 | tf_op jit(solution)/shard_map/pallas_call | solution.py:69
  160.5 7.8 %collective-permute-start.11 = (f32[72,128]{1,0:T(8,128)}, f32[72,128]{1,0:T(8,128)}, u32[]{:S(2)}, u32[]{:S(2)}) collective-permute-start(f32[72,128]{1,0:T(8,128)} %get-tuple-element.137), channel_id=1, source_target_pairs={{0,508},{4,8},{8,4},{12,16},{16,12},{20,24},{24,20},{28,32},{32,28... | collective-permute-start | bytes 110600 | tf_op jit(solution)/shard_map/ppermute | solution.py:772
  168.3 1.9 collective-permute-start.12
  175.8 4.5 %shard_map.163 = (f32[16,128,128]{2,1,0:T(8,128)S(1)}, f32[2,32,32,128]{3,2,1,0:T(8,128)S(1)}) custom-call(s32[8]{0:T(128)S(1)} %stack.37.ints, f32[4]{0:T(128)S(1)} %pad_maximum_fusion.floats, f32[32,128,128]{2,1,0:T(8,128)S(1)} %get-tuple-element.134.up, f32[32,128,128]{2,1,0:T(8,128)S(1)} %copy-done.1, f32[2,72,128]{2,1,0:T(8,128)S(1)} %get-tuple-element.136.own_pay, ...), custom_call_target="tpu_custom_call" | custom-call | flops 10000000 | bytes 7811584 | tf_op jit(solution)/shard_map/pallas_call | solution.py:69
  181.7 5.3 %collective-permute-start.13 = (f32[32,32,128]{2,0,1:T(8,128)S(1)}, f32[32,32,128]{2,0,1:T(8,128)S(1)}, u32[]{:S(2)}, u32[]{:S(2)}) collective-permute-start(f32[32,32,128]{2,0,1:T(8,128)S(1)} %copy.20), channel_id=1, source_target_pairs={{0,2},{2,0},{1,3},{3,1},{4,6},{6,4},{5,7},{7,5},{8,10},{10,8},{9,1... | collective-permute-start | bytes 1572872 | tf_op jit(solution)/shard_map/ppermute | solution.py:848
  189.6 19.4 %collective-permute-done.13 = f32[32,32,128]{2,0,1:T(8,128)S(1)} collective-permute-done((f32[32,32,128]{2,0,1:T(8,128)S(1)}, f32[32,32,128]{2,0,1:T(8,128)S(1)}, u32[]{:S(2)}, u32[]{:S(2)}) %collective-permute-start.13) | collective-permute-done | bytes 524320 | tf_op jit(solution)/shard_map/ppermute | solution.py:848
  211.7 2.1 broadcast_in_dim.3
  (71 shorter events, 26.0 us)
Async XLA Ops:
  0.6 10.4 %copy-start.17 = (f32[1,16,16384]{2,1,0:T(8,128)S(1)}, f32[1,16,16384]{2,1,0:T(8,128)}, u32[]{:S(2)}) copy-start(f32[1,16,16384]{2,1,0:T(8,128)} %param.15) | copy-start | bytes 3145732
  0.6 12.5 %copy-start.19 = (s32[1,3]{1,0:T(1,128)S(1)}, s32[1,3]{1,0:T(1,128)}, u32[]{:S(2)}) copy-start(s32[1,3]{1,0:T(1,128)} %param.27) | copy-start | bytes 40
  0.7 15.8 %copy-start.20 = (f32[1,3]{1,0:T(1,128)S(1)}, f32[1,3]{1,0:T(1,128)}, u32[]{:S(2)}) copy-start(f32[1,3]{1,0:T(1,128)} %param.16) | copy-start | bytes 40
  0.7 22.2 %copy-start.2 = (f32[128,128]{1,0:T(8,128)S(1)}, f32[128,128]{1,0:T(8,128)}, u32[]{:S(2)}) copy-start(f32[128,128]{1,0:T(8,128)} %b_full.5) | copy-start | bytes 196612
  0.7 22.2 %copy-start.9 = (f32[128,128]{1,0:T(8,128)S(1)}, f32[128,128]{1,0:T(8,128)}, u32[]{:S(2)}) copy-start(f32[128,128]{1,0:T(8,128)} %stiff.1) | copy-start | bytes 196612
  0.7 22.2 %copy-start.12 = (f32[64,64]{1,0:T(8,128)S(1)}, f32[64,64]{1,0:T(8,128)}, u32[]{:S(2)}) copy-start(f32[64,64]{1,0:T(8,128)} %stiff_v.1) | copy-start | bytes 49156
  0.7 22.2 %copy-start.13 = (f32[64,64]{1,0:T(8,128)S(1)}, f32[64,64]{1,0:T(8,128)}, u32[]{:S(2)}) copy-start(f32[64,64]{1,0:T(8,128)} %mass_v.1) | copy-start | bytes 49156
  0.7 22.2 %copy-start.15 = (f32[128]{0:T(128)S(1)}, f32[128]{0:T(128)}, u32[]{:S(2)}) copy-start(f32[128]{0:T(128)} %param.22) | copy-start | bytes 1540
  0.7 22.2 %copy-start.16 = (f32[64]{0:T(128)S(1)}, f32[64]{0:T(128)}, u32[]{:S(2)}) copy-start(f32[64]{0:T(128)} %param.24) | copy-start | bytes 772
  2.2 33.0 %collective-permute-start = (f32[16,128,128]{2,1,0:T(8,128)S(1)}, f32[16,128,128]{2,1,0:T(8,128)}, u32[]{:S(2)}, u32[]{:S(2)}) collective-permute-start(f32[16,128,128]{2,1,0:T(8,128)S(1)} %bitcast.35), channel_id=1, source_target_pairs={{0,1},{1,0},{2,3},{3,2},{4,5},{5,4},{6,7},{7,6},{8,9},{9,8},{10,11... | collective-permute-start | bytes 3145736 | tf_op jit(solution)/shard_map/ppermute | solution.py:777
  11.3 54.9 %collective-permute-start.4 = (f32[16,128,128]{2,1,0:T(8,128)S(1)}, f32[16,128,128]{2,1,0:T(8,128)}, u32[]{:S(2)}, u32[]{:S(2)}) collective-permute-start(f32[16,128,128]{2,1,0:T(8,128)S(1)} %bitcast.33), channel_id=1, source_target_pairs={{0,1},{1,0},{2,3},{3,2},{4,5},{5,4},{6,7},{7,6},{8,9},{9,8},{10,11... | collective-permute-start | bytes 3145736 | tf_op jit(solution)/shard_map/ppermute | solution.py:778
  22.9 0.8 copy-start.10
  27.3 27.3 %copy-start.5 = (f32[128,128]{1,0:T(8,128)}, f32[128,128]{1,0:T(8,128)S(1)}, u32[]{:S(2)}) copy-start(f32[128,128]{1,0:T(8,128)S(1)} %get-tuple-element.140.rt_full) | copy-start | bytes 196612
  37.2 17.5 %collective-permute-start.1 = (f32[48,128]{1,0:T(8,128)S(1)}, f32[48,128]{1,0:T(8,128)S(1)}, u32[]{:S(2)}, u32[]{:S(2)}) collective-permute-start(f32[48,128]{1,0:T(8,128)S(1)} %get-tuple-element.78), channel_id=1, source_target_pairs={{0,508},{4,8},{8,4},{12,16},{16,12},{20,24},{24,20},{28,32},{32,28... | collective-permute-start | bytes 73736 | tf_op jit(solution)/shard_map/ppermute | solution.py:772
  50.4 11.1 %collective-permute-start.2 = (f32[48,128]{1,0:T(8,128)S(1)}, f32[48,128]{1,0:T(8,128)S(1)}, u32[]{:S(2)}, u32[]{:S(2)}) collective-permute-start(f32[48,128]{1,0:T(8,128)S(1)} %get-tuple-element.79), channel_id=1, source_target_pairs={{0,4},{4,0},{8,12},{12,8},{16,20},{20,16},{24,28},{28,24},{32,36},... | collective-permute-start | bytes 73736 | tf_op jit(solution)/shard_map/ppermute | solution.py:772
  63.5 14.6 %collective-permute-start.3 = (f32[5,128,128]{2,1,0:T(8,128)S(1)}, f32[5,128,128]{2,1,0:T(8,128)S(1)}, u32[]{:S(2)}, u32[]{:S(2)}) collective-permute-start(f32[5,128,128]{2,1,0:T(8,128)S(1)} %get-tuple-element.88.msg_ref), channel_id=1, source_target_pairs={{0,2},{2,0},{1,3},{3,1},{4,6},{6,4},{5,7},{7,5},{8,10},{10,8},{9,1... | collective-permute-start | bytes 983048 | tf_op jit(solution)/shard_map/ppermute | solution.py:812
  80.3 11.8 %collective-permute-start.5 = (f32[72,128]{1,0:T(8,128)S(1)}, f32[72,128]{1,0:T(8,128)S(1)}, u32[]{:S(2)}, u32[]{:S(2)}) collective-permute-start(f32[72,128]{1,0:T(8,128)S(1)} %get-tuple-element.105), channel_id=1, source_target_pairs={{0,508},{4,8},{8,4},{12,16},{16,12},{20,24},{24,20},{28,32},{32,28... | collective-permute-start | bytes 110600 | tf_op jit(solution)/shard_map/ppermute | solution.py:772
  86.0 6.1 %collective-permute-start.6 = (f32[72,128]{1,0:T(8,128)S(1)}, f32[72,128]{1,0:T(8,128)S(1)}, u32[]{:S(2)}, u32[]{:S(2)}) collective-permute-start(f32[72,128]{1,0:T(8,128)S(1)} %get-tuple-element.106), channel_id=1, source_target_pairs={{0,4},{4,0},{8,12},{12,8},{16,20},{20,16},{24,28},{28,24},{32,36},... | collective-permute-start | bytes 110600 | tf_op jit(solution)/shard_map/ppermute | solution.py:772
  95.1 18.0 %collective-permute-start.7 = (f32[5,128,128]{2,1,0:T(8,128)S(1)}, f32[5,128,128]{2,1,0:T(8,128)S(1)}, u32[]{:S(2)}, u32[]{:S(2)}) collective-permute-start(f32[5,128,128]{2,1,0:T(8,128)S(1)} %get-tuple-element.111.msg_ref), channel_id=1, source_target_pairs={{0,2},{2,0},{1,3},{3,1},{4,6},{6,4},{5,7},{7,5},{8,10},{10,8},{9,1... | collective-permute-start | bytes 983048 | tf_op jit(solution)/shard_map/ppermute | solution.py:812
  115.4 15.2 %collective-permute-start.8 = (f32[40,128]{1,0:T(8,128)S(1)}, f32[40,128]{1,0:T(8,128)S(1)}, u32[]{:S(2)}, u32[]{:S(2)}) collective-permute-start(f32[40,128]{1,0:T(8,128)S(1)} %get-tuple-element.120), channel_id=1, source_target_pairs={{0,508},{4,8},{8,4},{12,16},{16,12},{20,24},{24,20},{28,32},{32,28... | collective-permute-start | bytes 61448 | tf_op jit(solution)/shard_map/ppermute | solution.py:772
  124.2 6.4 %collective-permute-start.9 = (f32[40,128]{1,0:T(8,128)S(1)}, f32[40,128]{1,0:T(8,128)S(1)}, u32[]{:S(2)}, u32[]{:S(2)}) collective-permute-start(f32[40,128]{1,0:T(8,128)S(1)} %get-tuple-element.121), channel_id=1, source_target_pairs={{0,4},{4,0},{8,12},{12,8},{16,20},{20,16},{24,28},{28,24},{32,36},... | collective-permute-start | bytes 61448 | tf_op jit(solution)/shard_map/ppermute | solution.py:772
  133.6 17.3 %collective-permute-start.10 = (f32[5,128,128]{2,1,0:T(8,128)S(1)}, f32[5,128,128]{2,1,0:T(8,128)S(1)}, u32[]{:S(2)}, u32[]{:S(2)}) collective-permute-start(f32[5,128,128]{2,1,0:T(8,128)S(1)} %get-tuple-element.123.msg_ref), channel_id=1, source_target_pairs={{0,2},{2,0},{1,3},{3,1},{4,6},{6,4},{5,7},{7,5},{8,10},{10,8},{9,1... | collective-permute-start | bytes 983048 | tf_op jit(solution)/shard_map/ppermute | solution.py:812
  153.8 19.6 %copy-start.6 = (f32[128,128]{1,0:T(8,128)S(1)}, f32[128,128]{1,0:T(8,128)}, u32[]{:S(2)}) copy-start(f32[128,128]{1,0:T(8,128)} %copy-done.5) | copy-start | bytes 196612
  159.2 1.3 copy-start
  160.5 11.0 %collective-permute-start.11 = (f32[72,128]{1,0:T(8,128)}, f32[72,128]{1,0:T(8,128)}, u32[]{:S(2)}, u32[]{:S(2)}) collective-permute-start(f32[72,128]{1,0:T(8,128)} %get-tuple-element.137), channel_id=1, source_target_pairs={{0,508},{4,8},{8,4},{12,16},{16,12},{20,24},{24,20},{28,32},{32,28... | collective-permute-start | bytes 110600 | tf_op jit(solution)/shard_map/ppermute | solution.py:772
  168.3 5.0 %collective-permute-start.12 = (f32[72,128]{1,0:T(8,128)}, f32[72,128]{1,0:T(8,128)}, u32[]{:S(2)}, u32[]{:S(2)}) collective-permute-start(f32[72,128]{1,0:T(8,128)} %get-tuple-element.138), channel_id=1, source_target_pairs={{0,4},{4,0},{8,12},{12,8},{16,20},{20,16},{24,28},{28,24},{32,36},... | collective-permute-start | bytes 110600 | tf_op jit(solution)/shard_map/ppermute | solution.py:772
  173.4 1.6 copy-start.1
  175.0 0.8 copy-start.8
  180.3 1.0 copy-start.3
  181.3 5.7 %copy-start.18 = (f32[62,64]{1,0:T(8,128)S(1)}, f32[62,64]{1,0:T(8,128)}, u32[]{:S(2)}) copy-start(f32[62,64]{1,0:T(8,128)} %param.26) | copy-start | bytes 47620
  181.3 5.9 %copy-start.4 = (f32[16,128,128]{2,1,0:T(8,128)S(1)}, f32[16,128,128]{2,1,0:T(8,128)}, u32[]{:S(2)}) copy-start(f32[16,128,128]{2,1,0:T(8,128)} %copy-done.3) | copy-start | bytes 3145732
  181.7 27.3 %collective-permute-start.13 = (f32[32,32,128]{2,0,1:T(8,128)S(1)}, f32[32,32,128]{2,0,1:T(8,128)S(1)}, u32[]{:S(2)}, u32[]{:S(2)}) collective-permute-start(f32[32,32,128]{2,0,1:T(8,128)S(1)} %copy.20), channel_id=1, source_target_pairs={{0,2},{2,0},{1,3},{3,1},{4,6},{6,4},{5,7},{7,5},{8,10},{10,8},{9,1... | collective-permute-start | bytes 1572872 | tf_op jit(solution)/shard_map/ppermute | solution.py:848
  (3 other events, 2.2 us)

commit v2 on v1

v2 whole, which is shorter than its diff:
```python
import jax
import jax.numpy as jnp
from jax import lax
from jax.experimental import pallas as pl
from jax.experimental.pallas import tpu as pltpu
from jax.sharding import PartitionSpec as P

BAND = 4
SWEEPS = 3
DAMPING = 0.25
KEEP = 1.0 - DAMPING
HIGHEST = lax.Precision.HIGHEST
F32 = jnp.float32
BF16 = jnp.bfloat16

N = 128
LAYERS = 64
HALF = 32
BLOCK = 16
REACH = HALF + BAND
ROWS = 40
TOP = HALF - BAND
CHUNK = 64
COARSE = N - 2


def split(x):
    high = x.astype(BF16)
    return high, (x - high.astype(F32)).astype(BF16)


def right_mul(x, packed):
    high, low = split(x)
    both = jnp.dot(jnp.concatenate([high, low], axis=-1), packed, preferred_element_type=F32)
    return both[:, :N] + both[:, N:]


def left_mul_planes(packed, planes):
    out = []
    for q in range(0, len(planes), 2):
        high, low = split(jnp.concatenate(planes[q:q + 2], axis=1))
        wide = jnp.dot(packed, jnp.concatenate([high, high], axis=0), preferred_element_type=F32)
        wide = wide + jnp.dot(packed[:, :N], low, preferred_element_type=F32)
        out += [wide[:, :N], wide[:, N:]]
    return out


def dot_full(x, y):
    return jnp.dot(x, y, precision=HIGHEST, preferred_element_type=F32)


def pack_right(a):
    high, low = split(a)
    top = jnp.concatenate([high, low], axis=1)
    bottom = jnp.concatenate([high, jnp.zeros_like(low)], axis=1)
    return jnp.concatenate([top, bottom], axis=0)


def pack_left(a):
    return jnp.concatenate(split(a), axis=1)


def call(kernel, outs, links, *args, flops=0, scratch=(), geometry=None):
    smem = [links] if geometry is None else [links, geometry]
    specs = [pl.BlockSpec(memory_space=pltpu.SMEM)] * len(smem)
    specs += [pl.BlockSpec(memory_space=pltpu.VMEM)] * len(args)
    shapes = [s if isinstance(s, jax.ShapeDtypeStruct) else jax.ShapeDtypeStruct(s, F32) for s in outs]
    moved = sum(a.size * a.dtype.itemsize for a in args) + sum(4 * s.size for s in shapes)

    def body(links_ref, *refs):
        ints = facts(links_ref)
        if geometry is None:
            kernel(ints, *refs)
        else:
            kernel(ints, scales(ints, refs[0]), *refs[1:])

    return pl.pallas_call(
        body,
        out_shape=shapes,
        in_specs=specs,
        out_specs=[pl.BlockSpec(memory_space=pltpu.VMEM)] * len(outs),
        scratch_shapes=list(scratch),
        compiler_params=pltpu.CompilerParams(vmem_limit_bytes=16 * 1024 * 1024),
        cost_estimate=pl.CostEstimate(
            flops=flops, bytes_accessed=moved, transcendentals=0
        ),
    )(*smem, *args)


def facts(links):
    slab = lax.axis_index("slab")
    west, east = links[0, 0], links[0, 1]
    return (
        links[0, 2], jnp.right_shift(west, 1), jnp.right_shift(slab, 1), jnp.bitwise_and(slab, 1),
        (N - 1) * jnp.bitwise_and(west, 1), (N - 1) * jnp.bitwise_and(east, 1),
    )


def scales(ints, geometry):
    turned = ints[1] == 1
    first, second = geometry[0, 0], geometry[0, 1]
    return (
        jnp.where(turned, second, first), jnp.where(turned, first, second), geometry[0, 2], jnp.float32(0),
    )


def source_layer(ints, t):
    inside = jnp.where(ints[2] == 1, HALF - 1 - t, t)
    return jnp.right_shift(inside, 4), jnp.bitwise_and(inside, BLOCK - 1)


def load_layer(ints, own_ref, other_ref, out_ref, t):
    block, index = source_layer(ints, t)
    mine = own_ref[index]
    theirs = other_ref[index]
    value = jnp.where(block == ints[3], mine, theirs)
    out_ref[t] = value

    @pl.when(ints[1] == 1)
    def _():
        out_ref[t] = value.T


def slot(ints, west, east, slot_ref):
    slot_ref[...] = jnp.where(ints[3] == 0, west, east)


def face_rows(ints, ref, side):
    position = ints[4 + side]
    return jnp.where(position == 0, ref[:, 0, :], ref[:, N - 1, :])


def load_kernel(ints, own, other, f_ref, pay_ref, slot_ref):
    def body(t, carry):
        load_layer(ints, own, other, f_ref, t)
        return carry

    lax.fori_loop(0, HALF, body, 0, unroll=4)
    flag = jnp.broadcast_to(ints[0].astype(F32), (8, N))
    for side in range(2):
        rows = face_rows(ints, f_ref, side)
        pay_ref[side] = jnp.concatenate([rows, jnp.zeros((ROWS - HALF, N), F32), flag], axis=0)
    slot(ints, pay_ref[0], pay_ref[1], slot_ref)


def reaction_kernel(ints, ready, own, other, r_ref, face_ref):
    def body(t, carry):
        load_layer(ints, own, other, r_ref, t)
        return carry

    lax.fori_loop(0, HALF, body, 0, unroll=4)
    for side in range(2):
        face_ref[side] = face_rows(ints, r_ref, side)


def forward_planes(x, wb, lbt):
    count = x.shape[0]
    first = right_mul(x.reshape(count * N, N), wb).reshape(count, N, N)
    return left_mul_planes(lbt, [first[q] for q in range(count)])


GROUP = 32


def transform_kernel(ints, f_ref, wb, lbt, out_ref):
    def body(g, carry):
        t = g * GROUP
        planes = forward_planes(f_ref[pl.ds(t, GROUP)], wb[...], lbt[...])
        for q in range(GROUP):
            out_ref[t + q] = planes[q]
        return carry

    lax.fori_loop(0, HALF // GROUP, body, 0)


FACTOR_ROWS = 16


def coefficient(bands, alpha, which, t, d):
    return alpha * bands[which, 0, d, t:t + 1, :] + bands[which, 1, d, t:t + 1, :]


def row_weights(a, l, t, least):
    w = {}
    for d in range(min(BAND, t), least - 1, -1):
        v = a[d]
        for m in range(d + 1, min(BAND, t) + 1):
            v = v - w[m] * l[t - d][m - d]
        w[d] = v
    return w


def eliminate(a, l, dinv, t):
    w = row_weights(a, l, t, 1)
    row = {d: w[d] * dinv[t - d] for d in w}
    pivot = a[0]
    for d in w:
        pivot = pivot - w[d] * row[d]
    return row, 1.0 / pivot


def factor_kernel(ints, ready, alpha_ref, bands, l_ref, dinv_ref):
    def body(c, carry):
        part = pl.ds(c * FACTOR_ROWS, FACTOR_ROWS)
        alpha = alpha_ref[part, :]
        l, dinv = {}, {}
        for t in range(HALF):
            a = [coefficient(bands, alpha, 0, t, d) for d in range(min(BAND, t) + 1)]
            l[t], dinv[t] = eliminate(a, l, dinv, t)
            for d in l[t]:
                l_ref[t, d - 1, part, :] = l[t][d]
            dinv_ref[t, part, :] = dinv[t]
        return carry

    lax.fori_loop(0, N // FACTOR_ROWS, body, 0)


def meet_kernel(
    ints, alpha_ref, bands, modes, l_ref, dinv_ref, lm_ref, dm_ref, lo_ref, do_ref, mend_ref, zs
):
    def mode(which, t):
        return modes[which, t:t + 1, :]

    def body(c, carry):
        part = pl.ds(c * FACTOR_ROWS, FACTOR_ROWS)
        alpha = alpha_ref[part, :]
        l, dinv, sent = {}, {}, {}
        for t in range(HALF):
            a = [coefficient(bands, alpha, 1, t, d) for d in range(min(BAND, t) + 1)]
            l[t], dinv[t] = eliminate(a, l, dinv, t)
            sent[t] = jnp.broadcast_to(mode(2, t), alpha.shape)
            for d in l[t]:
                sent[t] = sent[t] - l[t][d] * sent[t - d]
            if t >= TOP:
                for d in range(1, BAND + 1):
                    lo_ref[t - TOP, d - 1, part, :] = l[t][d]
                do_ref[t - TOP, part, :] = dinv[t]
        outer = {}
        for j in range(BAND):
            t = HALF + j
            a = [coefficient(bands, alpha, 1, t, d) for d in range(BAND + 1)]
            outer[j] = row_weights(a, l, t, j + 1)
            l[t] = {d: outer[j][d] * dinv[t - d] for d in outer[j]}
            for d in l[t]:
                lo_ref[BAND + j, d - 1, part, :] = l[t][d]
        schur = {}
        for j in range(BAND):
            for i in range(j + 1):
                total = None
                for s in range(TOP + j, HALF):
                    term = outer[j][HALF + j - s] * l[HALF + i][HALF + i - s]
                    total = term if total is None else total + term
                schur[(j, i)] = schur[(i, j)] = total
        shift = {}
        for j in range(BAND):
            for d in range(j + 1, BAND + 1):
                term = l[HALF + j][d] * sent[HALF + j - d]
                shift[j] = term if j not in shift else shift[j] + term
        z = {}
        for t in range(TOP):
            z[t] = jnp.broadcast_to(mode(1, t), alpha.shape)
            for d in range(1, min(BAND, t) + 1):
                z[t] = z[t] - l_ref[t, d - 1, part, :] * z[t - d]
            zs[t] = z[t]
        l = {
            t: {d: l_ref[t, d - 1, part, :] for d in range(1, BAND + 1)} for t in range(TOP - BAND, TOP)
        }
        dinv = {t: dinv_ref[t, part, :] for t in range(TOP - BAND, TOP)}
        for t in range(TOP, HALF):
            a = [coefficient(bands, alpha, 0, t, d) for d in range(BAND + 1)]
            j = HALF - 1 - t
            for d in range(t - TOP + 1):
                a[d] = a[d] - schur[(j, j + d)]
            l[t], dinv[t] = eliminate(a, l, dinv, t)
            for d in range(1, BAND + 1):
                lm_ref[t - TOP, d - 1, part, :] = l[t][d]
            dm_ref[t - TOP, part, :] = dinv[t]
            z[t] = mode(1, t) - shift[j]
            for d in range(1, BAND + 1):
                z[t] = z[t] - l[t][d] * z[t - d]
        exact = 1.0 / (alpha + modes[3, 0:1, :])
        y, miss, norm = {}, jnp.zeros_like(alpha), jnp.zeros_like(modes[3, 0:1, :])
        for t in range(HALF - 1, -1, -1):
            y[t] = z[t] * dinv[t] if t >= TOP else zs[t] * dinv_ref[t, part, :]
            for d in range(1, min(BAND, HALF - 1 - t) + 1):
                factor = l[t + d][d] if t + d >= TOP else l_ref[t + d, d - 1, part, :]
                y[t] = y[t] - factor * y[t + d]
            miss = miss + mode(1, t) * (mode(0, t) * exact - y[t])
            norm = norm + mode(1, t) * mode(0, t)
        mend_ref[part, :] = jnp.where(norm > 0.01, miss / jnp.maximum(norm, 0.01), 0.0)
        return carry

    lax.fori_loop(0, N // FACTOR_ROWS, body, 0)


def four(get):
    return [get(side, who) for side in range(2) for who in range(2)]


def vertical_apply(products, vert, scal_k, scal_m, scal_v):
    mass = [k * p[:, :N] + m * p[:, N:] for p, k, m in zip(products, scal_k, scal_m)]
    stiff = [v * p[:, :N] for p, v in zip(products, scal_v)]
    out = dot_full(vert[0], jnp.concatenate(mass, axis=1))
    out = out + dot_full(vert[1], jnp.concatenate(stiff, axis=1))
    return [out[:, q * N:(q + 1) * N] for q in range(len(products))]


def plane_products(faces, mk):
    stacked = dot_full(jnp.concatenate(faces, axis=0), mk[...])
    return [stacked[q * ROWS:(q + 1) * ROWS] for q in range(len(faces))]


def flip_masks(scal, nscal):
    return [scal[side, 3:4, :] != nscal[side, 3:4, :] for side in range(2)]


def orient_all(arrays, mirror, masks):
    turned = dot_full(jnp.concatenate([a for _, a in arrays], axis=0), mirror[...])
    return [
        jnp.where(masks[side], turned[q * ROWS:(q + 1) * ROWS], a)
        for q, (side, a) in enumerate(arrays)
    ]


def update_faces(c_faces, state, scal, nscal, mirror, mk, vert):
    masks = flip_masks(scal, nscal)
    residual = four(lambda side, who: state[4][2 * side + who])
    arrays = []
    for side in range(2):
        for who in range(2):
            arrays.append((side, c_faces[2 * side + 1 - who]))
    for side in range(2):
        for who in range(2):
            arrays.append((side, residual[2 * side + 1 - who]))
    turned = orient_all(arrays, mirror, masks)
    e, added = turned[:4], turned[4:]
    products = plane_products(e, mk)
    which = four(lambda side, who: (nscal if who else scal)[side])
    applied = vertical_apply(
        products, vert, [w[0:1] for w in which], [w[1:2] for w in which], [w[2:3] for w in which]
    )
    new = [list(state[s]) for s in range(6)]
    for q in range(4):
        new[2][q] = state[2][q] + DAMPING * (c_faces[q] + e[q])
        new[3][q] = state[3][q] + DAMPING * (residual[q] + added[q] + applied[q])
        new[4][q] = state[0][q] - state[1][q] * new[2][q] - new[3][q]
        new[5][q] = KEEP * state[5][q] + DAMPING * e[q]
    return new, e, masks


def read_state(ref):
    return [[ref[s, q] for q in range(4)] for s in range(6)]


def pad_rows(x):
    return jnp.concatenate([x, jnp.zeros((ROWS - x.shape[0], N), F32)], axis=0)


def eliminate_forward(gh_ref, spread, rows_hat, l_ref, modes, z_ref, msg_ref, low_ref, core):
    def body(c, carry):
        part = pl.ds(pl.multiple_of(c * CHUNK, CHUNK), CHUNK)
        west, east = spread[0, part, :], spread[1, part, :]
        z = {}
        lowest = jnp.zeros_like(west)
        for t in range(HALF):
            x = gh_ref[t, part, :] + west * rows_hat[0, t:t + 1, :] + east * rows_hat[1, t:t + 1, :]
            lowest = lowest + modes[0, t:t + 1, :] * x
            z_ref[t, part, :] = x
            for d in range(min(BAND, t), 0, -1):
                x = x - l_ref[t, d - 1, part, :] * z[t - d]
            z[t] = x
            if t < TOP:
                z_ref[t, part, :] = x
        low_ref[part, :] = lowest

        @pl.when(c == core)
        def _():
            there = pl.ds(0, CHUNK)
            for s in range(BAND):
                msg_ref[s, there, :] = z[TOP + s]
            msg_ref[BAND, there, :] = lowest

        return carry

    lax.fori_loop(0, N // CHUNK, body, 0)


def first_kernel(
    ints, gh, own_pay, rec, scal, spread, b_full, mirror, l_ref, modes,
    z_ref, msg_ref, low_ref, state_ref, rows_u, rows_g, rows_hat,
):
    received = (rec[0], rec[1])
    masks = [received[side][ROWS:ROWS + 1] != scal[side, 3:4, :] for side in range(2)]
    state_ref[...] = jnp.zeros_like(state_ref)
    for side in range(2):
        for who in range(2):
            values = received[side][:ROWS] if who else own_pay[side, :ROWS]
            state_ref[0, 2 * side + who] = values
            state_ref[4, 2 * side + who] = values
    turned = orient_all([(side, received[side][:ROWS]) for side in range(2)], mirror, masks)
    rows_u[...] = jnp.zeros_like(rows_u)
    for side in range(2):
        rows_g[side] = turned[side]
        rows_hat[side] = dot_full(turned[side], b_full[...])
    eliminate_forward(gh, spread, rows_hat, l_ref, modes, z_ref, msg_ref, low_ref, ints[3])


def next_kernel(
    ints, gh, own_pay, rec, state_in, scal, nscal, spread, b_full, mirror, mk, vert,
    l_ref, modes, z_ref, msg_ref, low_ref, state_ref, rows_u, rows_g, rows_hat,
):
    received = (rec[0], rec[1])
    state = read_state(state_in)
    if own_pay.shape[1] > ROWS:
        for side in range(2):
            state[1][2 * side] = pad_rows(own_pay[side, ROWS:ROWS + HALF])
            state[1][2 * side + 1] = pad_rows(received[side][ROWS:ROWS + HALF])
    c_faces = four(lambda side, who: received[side][:ROWS] if who else own_pay[side, :ROWS])
    state, e, masks = update_faces(c_faces, state, scal, nscal, mirror, mk, vert)
    for s in range(6):
        for q in range(4):
            state_ref[s, q] = state[s][q]
    turned = orient_all([(side, state[4][2 * side + 1]) for side in range(2)], mirror, masks)
    for side in range(2):
        step = DAMPING * e[2 * side]
        rows = turned[side] - state[1][2 * side] * step
        rows_u[side] = step
        rows_g[side] = rows
        rows_hat[side] = dot_full(rows, b_full[...])
    eliminate_forward(gh, spread, rows_hat, l_ref, modes, z_ref, msg_ref, low_ref, ints[3])


def solve_kernel(
    ints, z_ref, low_ref, zr_ref, l_ref, dinv_ref, lm_ref, dm_ref, lo_ref, do_ref, mend, modes, spread, bt_full, state, *refs,
):
    extra, (y_ref, pay_ref, slot_ref, sums) = refs[:-4], refs[-4:]
    sums[...] = jnp.zeros_like(sums)

    def body(c, carry):
        part = pl.ds(pl.multiple_of(c * CHUNK, CHUNK), CHUNK)
        source = c
        if zr_ref.shape[0] > 2:
            source = source + 2 * (1 - ints[2])
        there = pl.ds(0, CHUNK)
        sent = [zr_ref[source, s, there, :] for s in range(BAND)]
        weights = (spread[0, part, :], spread[1, part, :])

        low = mend[part, :] * (low_ref[part, :] + zr_ref[source, BAND, there, :])

        def put(t, value):
            value = value + low * modes[0, t:t + 1, :]
            y_ref[t, part, :] = value
            for side in range(2):
                product = weights[side] * value
                total = product[0:8]
                for s in range(8, CHUNK, 8):
                    total = total + product[s:s + 8]
                sums[side, t] += total

        z = {t: z_ref[t, part, :] for t in range(TOP - BAND, HALF)}
        for j in range(BAND):
            for d in range(j + 1, BAND + 1):
                z[HALF - 1 - j] = z[HALF - 1 - j] - lo_ref[BAND + j, d - 1, part, :] * sent[BAND + j - d]
        for t in range(TOP, HALF):
            for d in range(BAND, 0, -1):
                z[t] = z[t] - lm_ref[t - TOP, d - 1, part, :] * z[t - d]

        def factor(t, d):
            return lm_ref[t - TOP, d - 1, part, :] if t >= TOP else l_ref[t, d - 1, part, :]

        y = {}
        for t in range(HALF - 1, TOP - 1, -1):
            value = z[t] * dm_ref[t - TOP, part, :]
            for d in range(HALF - 1 - t, 0, -1):
                value = value - factor(t + d, d) * y[t + d]
            y[t] = value
            put(t, value)
        far = {HALF + j: y[HALF - 1 - j] for j in range(BAND)}
        for t in range(HALF - 1, TOP - 1, -1):
            value = sent[t - TOP] * do_ref[t - TOP, part, :]
            for d in range(BAND, 0, -1):
                value = value - lo_ref[t + d - TOP, d - 1, part, :] * far[t + d]
            far[t] = value
            put(2 * HALF - 1 - t, value)
        for t in range(TOP - 1, -1, -1):
            known = z[t] if t in z else z_ref[t, part, :]
            value = known * dinv_ref[t, part, :]
            for d in range(BAND, 0, -1):
                value = value - factor(t + d, d) * y[t + d]
            y[t] = value
            put(t, value)
        return carry

    lax.fori_loop(0, N // CHUNK, body, 0)
    mixed = jnp.sum(sums[...], axis=2)
    faces = dot_full(mixed.reshape(2 * ROWS, N), bt_full[...])
    packs = []
    for side in range(2):
        c = faces[side * ROWS:(side + 1) * ROWS] - state[2, 2 * side]
        pay_ref[side, :ROWS] = c
        if extra:
            pay_ref[side, ROWS:ROWS + HALF] = extra[0][side]
            pay_ref[side, ROWS + HALF:] = extra[1][side]
    slot(ints, pay_ref[0], pay_ref[1], slot_ref)


def back_planes(y, wbt, lb):
    count = y.shape[0]
    across = right_mul(y.reshape(count * N, N), wbt).reshape(count, N, N)
    return left_mul_planes(lb, [across[q] for q in range(count)])


def make_plane_kernel(sweep):
    last = sweep == SWEEPS - 1

    def kernel(ints, *refs):
        refs = list(refs)
        y_ref, f_ref, r_ref, rows_u, rows_g, mask, wbt, lb = refs[:8]
        refs = refs[8:]
        if sweep > 0:
            up_in, g_in = refs[:2]
            refs = refs[2:]
        if last:
            cut, pay_in = refs[:2]
            up_out, final_out, pay_out, slot_ref, sums = refs[2:]
        else:
            wb, lbt = refs[:2]
            up_out, g_out, gh_out = refs[2:]

        def on_faces(rows, t):
            return mask[0] * rows[0, pl.ds(t, 1), :] + mask[1] * rows[1, pl.ds(t, 1), :]

        def body(g, carry):
            t0 = g * GROUP
            corrections = back_planes(y_ref[pl.ds(t0, GROUP)], wbt[...], lb[...])
            fresh = []
            for q in range(GROUP):
                t = t0 + q
                on_u, on_g = on_faces(rows_u, t), on_faces(rows_g, t)
                load, react = f_ref[t], r_ref[t]
                if sweep == 0:
                    u, total = on_u, DAMPING * (load + on_g)
                else:
                    old = up_in[t]
                    u = old + on_u
                    total = KEEP * g_in[t] + DAMPING * (load - react * old + on_g)
                new = KEEP * u + DAMPING * corrections[q]
                if last:
                    block, index = source_layer(ints, t)

                    @pl.when(block == ints[3])
                    def _():
                        up_out[index] = new
                else:
                    up_out[t] = new
                residual = load - react * new
                if last:
                    residual = residual - total
                    for side in range(2):
                        product = cut[side] * residual
                        part = product[0:8]
                        for s in range(8, N, 8):
                            part = part + product[s:s + 8]
                        sums[side, t] = part
                else:
                    g_out[t] = total
                if last:
                    final_out[t] = residual
                fresh.append(residual)
            if not last:
                stacked = jnp.concatenate(fresh, axis=0).reshape(GROUP, N, N)
                planes = forward_planes(stacked, wb[...], lbt[...])
                for q in range(GROUP):
                    gh_out[t0 + q] = planes[q]
            return carry

        lax.fori_loop(0, HALF // GROUP, body, 0)
        if last:
            for side in range(2):
                pay_out[side, :ROWS] = pay_in[side, :ROWS]
                pay_out[side, ROWS:] = jnp.sum(sums[side], axis=1)
            slot(ints, pay_out[0], pay_out[1], slot_ref)

    return kernel


def restrict_kernel(ints, final, wrt, lr, kept, sent, plane):
    def body(g, carry):
        t0 = g * GROUP
        planes = forward_planes(final[pl.ds(t0, GROUP)], wrt[...], lr[...])
        for q in range(GROUP):
            plane[q] = planes[q]

        @pl.when(ints[1] == 1)
        def _():
            for q in range(GROUP):
                plane[q] = planes[q].T

        for half in range(2):
            for core in range(2):
                first = half * (COARSE // 2) + core * 31

                @pl.when((ints[2] == half) & (ints[3] == core))
                def _():
                    kept[pl.ds(t0, GROUP)] = plane[:, first:first + 32]

                @pl.when((ints[2] != half) & (ints[3] == core))
                def _():
                    sent[pl.ds(t0, GROUP)] = plane[:, first:first + 32]

        return carry

    lax.fori_loop(0, HALF // GROUP, body, 0)


def final_kernel(
    ints, floats, own_pay, rec, state_in, scal, nscal, mirror, mirror_coarse, mk, vert, rt_full, parts, rows_u,
):
    received = (rec[0], rec[1])
    state = read_state(state_in)
    c_faces = four(lambda side, who: received[side][:ROWS] if who else own_pay[side, :ROWS])
    state, e, masks = update_faces(c_faces, state, scal, nscal, mirror, mk, vert)
    gathered = state[5]
    products = plane_products(gathered, mk)
    far = vertical_apply(
        [products[1], products[3]], vert,
        [nscal[side, 4:5] for side in range(2)],
        [nscal[side, 5:6] for side in range(2)],
        [nscal[side, 6:7] for side in range(2)],
    )
    one = floats[0]
    near_stiff = vertical_apply([products[0], products[2]], vert, [one] * 2, [floats[3]] * 2, [floats[3]] * 2)
    near_mass = vertical_apply([products[0], products[2]], vert, [floats[3]] * 2, [floats[1]] * 2, [floats[2]] * 2)
    stack = []
    for side in range(2):
        nbr = 2 * side + 1
        theirs = pad_rows(received[side][ROWS:])
        theirs = theirs - nscal[side, 7:8] * DAMPING * state[1][nbr] * e[nbr] - far[side]
        mine = scal[side, 7:8] * DAMPING * state[1][2 * side] * e[2 * side]
        stack += [near_stiff[side], near_mass[side], mine, theirs]
    restricted = dot_full(jnp.concatenate(stack, axis=0), rt_full[...])
    pieces = [restricted[q * ROWS:(q + 1) * ROWS] for q in range(8)]
    turned = dot_full(jnp.concatenate([pieces[3], pieces[7]], axis=0), mirror_coarse[...])
    for side in range(2):
        added = jnp.where(masks[side], turned[side * ROWS:(side + 1) * ROWS], pieces[4 * side + 3])
        parts[3 * side] = -pieces[4 * side][:HALF]
        parts[3 * side + 1] = -pieces[4 * side + 1][:HALF]
        parts[3 * side + 2] = (added - pieces[4 * side + 2])[:HALF]
        rows_u[side] = DAMPING * e[2 * side]

def iterate_kernel(ints, up, rows_u, mask, out_u):
    def body(index, carry):
        inside = ints[3] * BLOCK + index
        t = jnp.where(ints[2] == 1, HALF - 1 - inside, inside)
        value = up[index] + mask[0] * rows_u[0, pl.ds(t, 1), :] + mask[1] * rows_u[1, pl.ds(t, 1), :]
        out_u[index] = value

        @pl.when(ints[1] == 1)
        def _():
            out_u[index] = value.T

        return carry

    lax.fori_loop(0, BLOCK, body, 0, unroll=2)


def coarse_kernel(
    ints, kept, arrived, parts, far_parts, profile, profile_rows, vertical, out, blocks, columns,
):
    deep = vertical.shape[0]
    spots = [0, 31, COARSE // 2, COARSE // 2 + 31]
    weights = vertical[...]
    stacked = [jnp.concatenate([parts[s], far_parts[s]], axis=0) for s in range(6)]
    mixed = dot_full(weights, jnp.concatenate(stacked, axis=1))
    mixed = [mixed[:, s * N:(s + 1) * N] for s in range(6)]
    for c in range(32):
        rows = pl.ds(c, HALF, stride=32)
        both = jnp.concatenate([kept[rows, :], arrived[rows, :]], axis=0)
        blocks[c] = dot_full(weights, both)

    @pl.when(ints[1] == 0)
    def _():
        first = ints[2] * (COARSE // 2) + ints[3] * 31

        def body(c, carry):
            value = blocks[c]
            for s in range(6):
                value = value + profile[s, pl.ds(first + c, 1), :] * mixed[s]
            blocks[c] = value
            return carry

        lax.fori_loop(0, 32, body, 0)

    @pl.when(ints[1] == 1)
    def _():
        for half in range(2):
            for core in range(2):
                shift = (N - spots[2 * half + core]) % N

                @pl.when((ints[2] == half) & (ints[3] == core))
                def _():
                    for s in range(6):
                        columns[s] = pltpu.roll(mixed[s], shift, 1) if shift else mixed[s]

        for c in range(32):
            value = blocks[c]
            for s in range(6):
                value = value + columns[s, :, c:c + 1] * profile_rows[s:s + 1, :]
            blocks[c] = value

    share = out.shape[1]
    lane = lax.broadcasted_iota(jnp.int32, (deep, N), 1)
    for core in range(2):

        @pl.when(ints[3] == core)
        def _():
            start = core * (COARSE // 2)
            held = {}

            def turned(c):
                if c not in held:
                    shift = (c * COARSE - start) % N
                    held[c] = pltpu.roll(blocks[c], shift, 1) if shift else blocks[c]
                return held[c]

            for tile in range(-(-share // N)):
                low = tile * N + start
                c = low // COARSE
                value = turned(c)
                after = (c + 1) * COARSE - low
                if after < N and c + 1 < 32:
                    value = jnp.where(lane < after, value, turned(c + 1))
                if after + COARSE < N and c + 2 < 32:
                    value = jnp.where(lane < after + COARSE, value, turned(c + 2))
                width = min(N, share - tile * N)
                out[:, tile * N:tile * N + width] = value[:, :width]


def prepare_kernel(
    ints, floats, stiff, mass, stiff_v, mass_v, basis, eigen, basis_v, eigen_v, restrict, restrict_v,
    wb, wbt, wrt, lb, lbt, lr, bt_out, rt_out, mk, mirror, mirror_coarse, vert, scal, spread, mask, cut,
    profile, profile_rows, alpha, bands, modes, vertical,
):
    a1, a2, a3 = floats[0], floats[1], floats[2]
    rows = lax.broadcasted_iota(jnp.int32, (N, N), 0)
    lanes = lax.broadcasted_iota(jnp.int32, (N, N), 1)
    eye = rows == lanes

    def column(row):
        picked = jnp.sum(jnp.where(eye, row, 0.0), axis=1, keepdims=True)
        return jnp.broadcast_to(picked, (N, N))

    b, k, m = basis[...], stiff[...], mass[...]
    bt = b.T
    r = jnp.concatenate([restrict[...], jnp.zeros((N - COARSE, N), F32)], axis=0)
    rt = r.T
    wb[...], wbt[...], wrt[...] = pack_right(b), pack_right(bt), pack_right(rt)
    lb[...], lbt[...], lr[...] = pack_left(b), pack_left(bt), pack_left(r)
    bt_out[...], rt_out[...] = bt, rt
    mk[:, :N], mk[:, N:] = m, k
    mirror[...] = (rows + lanes == N - 1).astype(F32)
    mirror_coarse[...] = (rows + lanes == COARSE - 1).astype(F32)
    alpha[...] = a1 * column(eigen[...]) + a2 * eigen[...]

    turn = (
        lax.broadcasted_iota(jnp.int32, (LAYERS, LAYERS), 0)
        + lax.broadcasted_iota(jnp.int32, (LAYERS, LAYERS), 1)
        == LAYERS - 1
    ).astype(F32)
    first = ints[2] == 0
    kv, mv = stiff_v[...], mass_v[...]
    ordered = []
    for matrix in (mv, a3 * kv):
        turned = dot_full(dot_full(turn, matrix), turn)
        ordered.append((jnp.where(first, matrix, turned), jnp.where(first, turned, matrix)))
    deep = lax.broadcasted_iota(jnp.int32, (ROWS, LAYERS), 0)
    wide = lax.broadcasted_iota(jnp.int32, (ROWS, LAYERS), 1)
    inside = (deep < HALF) & (wide < REACH)
    own_stiff = jnp.where(first, kv, dot_full(dot_full(turn, kv), turn))
    vert[0] = jnp.where(inside, ordered[0][0][:ROWS], 0.0)[:, :ROWS]
    vert[1] = jnp.where(inside, own_stiff[:ROWS], 0.0)[:, :ROWS]
    for which in range(2):
        for s in range(2):
            for d in range(BAND + 1):
                picked = jnp.where(deep - wide == d, ordered[s][which][:ROWS], 0.0)
                bands[which, s, d] = jnp.broadcast_to(jnp.sum(picked, axis=1, keepdims=True), (ROWS, N))

    rv = restrict_v[...]
    backwards = dot_full(rv, turn)
    vertical[:, :HALF] = jnp.where(first, rv, backwards)[:, :HALF]
    vertical[:, HALF:] = jnp.where(first, backwards, rv)[:, :HALF]

    mu = eigen_v[...]
    least = jnp.min(mu, axis=1, keepdims=True)
    number = lax.broadcasted_iota(jnp.int32, (1, LAYERS), 1)
    chosen = jnp.min(jnp.where(mu == least, number, LAYERS), axis=1, keepdims=True)
    low = jnp.sum(jnp.where(number == chosen, basis_v[...], 0.0), axis=1, keepdims=True)
    low = jnp.broadcast_to(low, (LAYERS, N))
    low_mass = dot_full(mv, low)
    low_turned, mass_turned = dot_full(turn, low), dot_full(turn, low_mass)
    modes[0] = jnp.where(first, low, low_turned)[:ROWS]
    modes[1] = jnp.where(first, low_mass, mass_turned)[:ROWS]
    modes[2] = jnp.where(first, mass_turned, low_mass)[:ROWS]
    modes[3] = jnp.broadcast_to(a3 * least, (ROWS, N))

    for side in range(2):
        start = ints[4 + side] == 0

        def end_row(matrix, count=N):
            return jnp.where(start, matrix[0:1, :], matrix[count - 1:count, :])

        def corner(matrix):
            value = jnp.where(start, matrix[0:1, 0:1], matrix[N - 1:N, N - 1:N])
            return jnp.broadcast_to(value, (1, N))

        cut_row = end_row(r, COARSE)
        cut_at = jnp.broadcast_to(jnp.where(start, cut_row[:, 0:1], cut_row[:, N - 1:N]), (1, N))
        stiff_profile = jnp.broadcast_to(jnp.sum(r * end_row(k), axis=1, keepdims=True), (N, N))
        mass_profile = jnp.broadcast_to(jnp.sum(r * end_row(m), axis=1, keepdims=True), (N, N))
        at_face = jnp.where(start, 0, COARSE - 1)
        at_rows = [stiff_profile, mass_profile, (rows == at_face).astype(F32)]
        for s in range(3):
            turned_row = jnp.sum(jnp.where(eye, at_rows[s], 0.0), axis=0, keepdims=True)
            profile_rows[3 * side + s:3 * side + s + 1, :] = turned_row
        profile[3 * side] = stiff_profile
        profile[3 * side + 1] = mass_profile
        profile[3 * side + 2] = (rows == at_face).astype(F32)
        spread[side] = column(end_row(b))
        mask[side] = (rows == ints[4 + side]).astype(F32)
        cut[side] = column(cut_row)
        scal[side] = jnp.concatenate(
            [
                corner(k) * a1,
                corner(m) * a2,
                corner(m) * a3,
                jnp.broadcast_to(ints[0].astype(F32), (1, N)),
                end_row(stiff_profile, COARSE) * a1,
                end_row(mass_profile, COARSE) * a2,
                end_row(mass_profile, COARSE) * a3,
                cut_at,
            ],
            axis=0,
        )


def per_device(
    load_vector,
    reaction,
    geometry,
    stiff_plane,
    mass_plane,
    stiff_vertical,
    mass_vertical,
    basis_plane,
    eigen_plane,
    basis_vertical,
    eigen_vertical,
    restrict_plane,
    restrict_vertical,
    patch_links,
):
    patches = lax.axis_size("patch")
    links = patch_links
    square, two = (N, N), (2, N, N)
    right = jax.ShapeDtypeStruct((2 * N, 2 * N), BF16)
    left = jax.ShapeDtypeStruct((N, 2 * N), BF16)
    (
        wb, wbt, wrt, lb, lbt, lr, basis_t, restrict_t, mk, mirror, mirror_coarse, vert, scal, spread, mask,
        cut, profile, profile_rows, alpha, bands, modes, vertical,
    ) = call(
        prepare_kernel,
        [
            right, right, right, left, left, left, square, square, (N, 2 * N), square, square,
            (2, ROWS, ROWS), (2, 8, N), two, two, two, (6, N, N), (8, N), square, (2, 2, BAND + 1, ROWS, N), (4, ROWS, N),
            restrict_vertical.shape,
        ],
        links, stiff_plane, mass_plane, stiff_vertical, mass_vertical, basis_plane, eigen_plane.reshape(1, N),
        basis_vertical, eigen_vertical.reshape(1, LAYERS), restrict_plane, restrict_vertical,
        geometry=geometry, flops=20_000_000,
    )

    pair = [(0, 1), (1, 0), (2, 3), (3, 2)]
    cross = [(0, 2), (2, 0), (1, 3), (3, 1)]
    chips = [[0, 1], [2, 3]]
    faces = []
    for p in range(patches):
        for h in range(2):
            west, east = 4 * p + 2 * h + 1, 4 * ((p + 1) % patches) + 2 * h
            faces += [(west, east), (east, west)]

    def swap_faces(slot_values):
        arrived = lax.ppermute(slot_values, ("patch", "slab"), faces)
        return lambda: lax.all_gather(arrived, "slab", axis_index_groups=chips)

    field = (HALF, N, N)
    own_load = load_vector[0].reshape(BLOCK, N, N)
    own_react = reaction[0].reshape(BLOCK, N, N)
    other_load = lax.ppermute(own_load, "slab", pair)
    other_react = lax.ppermute(own_react, "slab", pair)
    size = ROWS + 8
    f, pay, slot_values = call(
        load_kernel, [field, (2, size, N), (size, N)], links, own_load, other_load
    )
    arriving = swap_faces(slot_values)
    l, dinv = call(
        factor_kernel, [(HALF, BAND, N, N), field], links, slot_values, alpha, bands, flops=3_000_000_000
    )
    (gh,) = call(transform_kernel, [field], links, f, wb, lbt, flops=2_000_000_000)
    rec = arriving()
    rows_hat = pltpu.VMEM((2, ROWS, N), F32)
    sums = pltpu.VMEM((2, ROWS, 8, N), F32)
    message = (BAND + 1, N // 2, N)
    message_full = (BAND, N, N)
    state_shape = (6, 4, ROWS, N)
    rows_shape = (2, ROWS, N)
    up = total = None
    for sweep in range(SWEEPS):
        if sweep == 0:
            z, msg, low, state, rows_u, rows_g = call(
                first_kernel,
                [field, message, square, state_shape, rows_shape, rows_shape],
                links, gh, pay, rec, scal, spread, basis_plane, mirror, l, modes,
                scratch=[rows_hat], flops=10_000_000,
            )
        else:
            if sweep == 1:
                nscal = rec[:, ROWS + HALF:]
            z, msg, low, state, rows_u, rows_g = call(
                next_kernel,
                [field, message, square, state_shape, rows_shape, rows_shape],
                links, gh, pay, rec, state, scal, nscal, spread, basis_plane, mirror, mk, vert, l, modes,
                scratch=[rows_hat], flops=10_000_000,
            )
        if sweep > 0:
            received = lax.all_gather(msg, "slab")
        else:
            crossing = lax.ppermute(msg, "slab", cross)
            r, react_faces = call(reaction_kernel, [field, (2, HALF, N)], links, msg, own_react, other_react)
            lm, dm, lo, do, mend = call(
                meet_kernel,
                [(BAND, BAND, N, N), message_full, (2 * BAND, BAND, N, N), message_full, square],
                links, alpha, bands, modes, l, dinv,
                scratch=[pltpu.VMEM((TOP, FACTOR_ROWS, N), F32)], flops=5_000_000_000,
            )
            received = lax.all_gather(crossing, "slab", axis_index_groups=chips)
        last = sweep == SWEEPS - 1
        size = ROWS + HALF + 8 if sweep == 0 else ROWS
        extra = [react_faces, scal] if sweep == 0 else []
        y, pay, slot_values = call(
            solve_kernel,
            [(REACH, N, N), (2, size, N), (size, N)],
            links, z, low, received, l, dinv, lm, dm, lo, do, mend, modes, spread, basis_t, state, *extra,
            scratch=[sums], flops=10_000_000,
        )
        args = [y, f, r, rows_u, rows_g, mask, wbt, lb]
        if sweep > 0:
            args += [up, total]
        plane_kernel = make_plane_kernel(sweep)
        if last:
            size = ROWS + HALF
            block = (HALF, 32, N)
            up, final, pay, slot_values = call(
                plane_kernel,
                [(BLOCK, N, N), field, (2, size, N), (size, N)],
                links, *args, cut, pay,
                scratch=[pltpu.VMEM((2, HALF, 8, N), F32)], flops=3_000_000_000,
            )
            arriving = swap_faces(slot_values)
            kept, sent = call(
                restrict_kernel, [block, block], links, final, wrt, lr,
                scratch=[pltpu.VMEM((GROUP, N, N), F32)], flops=3_000_000_000,
            )
            arrived = lax.ppermute(sent, "slab", cross)
            rec = arriving()
        else:
            arriving = swap_faces(slot_values)
            up, total, gh = call(
                plane_kernel, [field, field, field], links, *args, wb, lbt, flops=4_000_000_000
            )
            rec = arriving()
    parts, rows_u = call(
        final_kernel,
        [(6, HALF, N), rows_shape],
        links, pay, rec, state, scal, nscal, mirror, mirror_coarse, mk, vert, restrict_t,
        geometry=geometry, flops=80_000_000_000,
    )
    far_parts = lax.ppermute(parts, "slab", cross)
    (out_u,) = call(iterate_kernel, [(BLOCK, N, N)], links, up, rows_u, mask, flops=2_000_000_000)
    deep = restrict_vertical.shape[0]
    share = COARSE * COARSE // 4
    (flat,) = call(
        coarse_kernel,
        [(deep, share)],
        links, kept.reshape(HALF * 32, N), arrived.reshape(HALF * 32, N), parts, far_parts,
        profile, profile_rows, vertical,
        scratch=[pltpu.VMEM((32, deep, N), F32), pltpu.VMEM((6, deep, N), F32)],
        flops=10_000_000,
    )
    return out_u.reshape(1, BLOCK, N * N), flat[None]


def solution(mesh):
    in_specs = (
        P("patch", "slab", None),
        P("patch", "slab", None),
        P("patch", None),
        P(), P(), P(), P(), P(), P(), P(), P(), P(), P(),
        P("patch", None),
    )
    out_specs = (P("patch", "slab", None), P("patch", None, "slab"))
    return jax.shard_map(
        per_device, mesh=mesh, in_specs=in_specs, out_specs=out_specs, check_vma=False
    )
```

time: 215 us -> 159 us (0.74)
  blocking collectives: 0 us -> 58.3 us
  waiting for transfers between devices: 66.1 us -> 12.5 us
  starting transfers between devices: 70.5 us -> 32.4 us
  local copies, waits for them, and re-layouts: 16.9 us -> 4.93 us
  between operations: 8.21 us -> 1.1 us
  matrix products: 2.2 us -> 0 us
    all_gather x0 -> x7, blocking collectives: none -> 58.3 us  [the longest x4 31.9 us: swap_faces(): return lambda: lax.all_gather(arrived, 'slab', axis_index_groups=chips)]
    ppermute x11 -> x6, starting transfers between devices: 54.5 us -> 17.3 us  [the longest x4 7.68 us: swap_faces(): arrived = lax.ppermute(slot_values, ('patch', 'slab'), faces)]
    ppermute x11 -> x6, waiting for transfers between devices: 46.7 us -> 12.5 us  [the longest x4 7.92 us: swap_faces(): arrived = lax.ppermute(slot_values, ('patch', 'slab'), faces)]
    ppermute x1, waiting for transfers between devices: 19.4 us -> 0.01 us  [per_device(): arrived = lax.ppermute(sent, 'slab', cross)]
    unnamed x44 -> x29, local copies, waits for them, and re-layouts: 9.56 us -> 3.77 us
    dot_general x2 -> x0, matrix products: 2.2 us -> none  [the longest x1 1.24 us: per_device(): coarse = jnp.einsum('mt,tcd->mcd', near, kept, precision=HIGHEST)]
    pallas_call x15 -> x19, Pallas kernels: 49.1 us -> 49.8 us  [call(): pl.pallas_call(body, out_shape=shapes, in_specs=specs, out_specs=[pl.Bloc...]
  transfers between devices with their start and end apart: 14 -> 9, of which waited for: 7 -> 2; matrix products, arithmetic and copies ran while one was open for 3% -> 1% of each run, Pallas kernels for 12% -> 18%
where the time goes in v2:
time: 159 us
  blocking collectives  58.3 us (37%)
  Pallas kernels  49.8 us (31%)
  starting transfers between devices  32.4 us (20%)
  waiting for transfers between devices  12.5 us (8%)
  local copies, waits for them, and re-layouts  4.93 us (3%)
    pallas_call x19, Pallas kernels, call(): pl.pallas_call(body, out_shape=shapes, in_specs=specs, out_specs=[pl.Bloc...  49.8 us
    all_gather x4, blocking collectives, swap_faces(): return lambda: lax.all_gather(arrived, 'slab', axis_index_groups=chips)  31.9 us
    all_gather x2, blocking collectives, per_device(): received = lax.all_gather(msg, 'slab')  24.1 us
    ppermute x1, starting transfers between devices, per_device(): other_load = lax.ppermute(own_load, 'slab', pair)  8.79 us
    ppermute x4, waiting for transfers between devices, swap_faces(): arrived = lax.ppermute(slot_values, ('patch', 'slab'), faces)  7.92 us
    ppermute x4, starting transfers between devices, swap_faces(): arrived = lax.ppermute(slot_values, ('patch', 'slab'), faces)  7.68 us
    ppermute x1, starting transfers between devices, per_device(): far_parts = lax.ppermute(parts, 'slab', cross)  4.85 us
    ppermute x1, starting transfers between devices, per_device(): crossing = lax.ppermute(msg, 'slab', cross)  4.76 us
  transfers between devices with their start and end apart: 9, of which 2 were waited for; matrix products, arithmetic and copies ran while one was open for 1% of the time, Pallas kernels for 18%

profile of v2, /device:TPU:1, one launch (start us, length us, event | category | flops | bytes accessed | tf_op | source)
XLA Modules:
  0.0 159.1 jit_solution(12159174995594892219)
XLA Ops:
  2.3 8.8 %collective-permute-start = (f32[16,128,128]{2,1,0:T(8,128)S(1)}, f32[16,128,128]{2,1,0:T(8,128)S(1)}, u32[]{:S(2)}, u32[]{:S(2)}) collective-permute-start(f32[16,128,128]{2,1,0:T(8,128)S(1)} %bitcast.20), channel_id=1, source_target_pairs={{0,1},{1,0},{2,3},{3,2},{4,5},{5,4},{6,7},{7,6},{8,9},{9,8},{10,11... | collective-permute-start | bytes 3145736 | tf_op jit(solution)/shard_map/ppermute | solution.py:898
  11.3 1.9 %collective-permute-start.3 = (f32[16,128,128]{2,1,0:T(8,128)S(1)}, f32[16,128,128]{2,1,0:T(8,128)S(1)}, u32[]{:S(2)}, u32[]{:S(2)}) collective-permute-start(f32[16,128,128]{2,1,0:T(8,128)S(1)} %bitcast.18), channel_id=1, source_target_pairs={{0,1},{1,0},{2,3},{3,2},{4,5},{5,4},{6,7},{7,6},{8,9},{9,8},{10,11... | collective-permute-start | bytes 3145736 | tf_op jit(solution)/shard_map/ppermute | solution.py:899
  15.7 1.9 %collective-permute-start.1 = (f32[48,128]{1,0:T(8,128)S(1)}, f32[48,128]{1,0:T(8,128)S(1)}, u32[]{:S(2)}, u32[]{:S(2)}) collective-permute-start(f32[48,128]{1,0:T(8,128)S(1)} %get-tuple-element.80.refs_0_), channel_id=1, source_target_pairs={{1,4},{4,1},{3,6},{6,3},{5,8},{8,5},{7,10},{10,7},{9,12},{12,9},{1... | collective-permute-start | bytes 73736 | tf_op jit(solution)/shard_map/ppermute | solution.py:892
  17.6 2.9 %shard_map.152 = (f32[32,4,128,128]{3,2,1,0:T(8,128)S(1)}, f32[32,128,128]{2,1,0:T(8,128)S(1)}) custom-call(s32[1,3]{1,0:T(1,128)S(1)} %copy-done.4, f32[48,128]{1,0:T(8,128)S(1)} %get-tuple-element.80.refs_0_, f32[128,128]{1,0:T(8,128)S(1)} %get-tuple-element.84.refs_1_.refs_0_, f32[2,2,5,40,128]{4,3,2,1,0:T(8,128)S(1)} %get-tuple-element.85.refs_2_.refs_1_), custom_call_target="tpu_custom_call" | custom-call | flops 3000000000 | bytes 10985472 | tf_op jit(solution)/shard_map/pallas_call | solution.py:77
  20.5 2.0 %shard_map.151.refs_0_ = f32[32,128,128]{2,1,0:T(8,128)S(1)} custom-call(s32[1,3]{1,0:T(1,128)S(1)} %copy-done.4, f32[32,128,128]{2,1,0:T(8,128)S(1)} %get-tuple-element.76.refs_0_.refs_1_, bf16[256,256]{1,0:T(8,128)(2,1)S(1)} %get-tuple-element.77.refs_1_.refs_8_.refs_10_, bf16[128,256]{1,0:T(8,128)(2,1)S(1)} %get-tuple-element.78.refs_2_.refs_9_.refs_11_), custom_call_target="tpu_custom_call" | custom-call | flops 2000000000 | bytes 4390912 | tf_op jit(solution)/shard_map/pallas_call | solution.py:77
  22.5 13.4 %all-gather = f32[96,128]{1,0:T(8,128)S(1)} all-gather(f32[48,128]{1,0:T(8,128)S(1)} %collective-permute-done.1), channel_id=2, replica_groups={{0,1},{2,3},{4,5},{6,7},{8,9},{10,11},{12,13},{14,15},{16,17},{18,19},{..., dimensions={0}, use_global_device_ids=true | all-gather | bytes 73728 | tf_op jit(solution)/shard_map/all_gather | solution.py:893
  35.9 2.1 %shard_map.153 = (f32[32,128,128]{2,1,0:T(8,128)S(1)}, f32[5,64,128]{2,1,0:T(8,128)S(1)}, f32[128,128]{1,0:T(8,128)S(1)}, f32[6,4,40,128]{3,2,1,0:T(8,128)S(1)},...) custom-call(s32[1,3]{1,0:T(1,128)S(1)} %copy-done.4, f32[32,128,128]{2,1,0:T(8,128)S(1)} %shard_map.151.refs_0_, ...), custom_call_target="tpu_custom_call" | custom-call | flops 10000000 | bytes 13836288 | tf_op jit(solution)/shard_map/pallas_call | solution.py:77
  38.0 4.8 %collective-permute-start.2 = (f32[5,64,128]{2,1,0:T(8,128)S(1)}, f32[5,64,128]{2,1,0:T(8,128)S(1)}, u32[]{:S(2)}, u32[]{:S(2)}) collective-permute-start(f32[5,64,128]{2,1,0:T(8,128)S(1)} %get-tuple-element.90.refs_0_), channel_id=1, source_target_pairs={{0,2},{2,0},{1,3},{3,1},{4,6},{6,4},{5,7},{7,5},{8,10},{10,8},{9,1... | collective-permute-start | bytes 491528 | tf_op jit(solution)/shard_map/ppermute | solution.py:937
  42.8 6.3 %shard_map.154 = (f32[4,4,128,128]{3,2,1,0:T(8,128)S(1)}, f32[4,128,128]{2,1,0:T(8,128)S(1)}, f32[8,4,128,128]{3,2,1,0:T(8,128)S(1)}, f32[4,128,128]{2,1,0:T(8,128)S(1)}, f32[128,128]{1,0:T(8,128)S(1)}) custom-call(s32[1,3]{1,0:T(1,128)S(1)} %copy-done.4, f32[128,128]{1,0:T(8,128)S(1)} %get-tuple-element.84.refs_1_.refs_0_, ...), custom_call_target="tpu_custom_call" | custom-call | flops 5000000000 | bytes 14778368 | tf_op jit(solution)/shard_map/pallas_call | solution.py:77
  50.1 2.3 %all-gather.1 = f32[10,64,128]{2,1,0:T(8,128)S(1)} all-gather(f32[5,64,128]{2,1,0:T(8,128)S(1)} %collective-permute-done.2), channel_id=3, replica_groups={{0,1},{2,3},{4,5},{6,7},{8,9},{10,11},{12,13},{14,15},{16,17},{18,19},{..., dimensions={0}, use_global_device_ids=true | all-gather | bytes 491520 | tf_op jit(solution)/shard_map/all_gather | solution.py:945
  52.4 2.3 %shard_map.156 = (f32[36,128,128]{2,1,0:T(8,128)S(1)}, f32[2,80,128]{2,1,0:T(8,128)S(1)}, f32[80,128]{1,0:T(8,128)S(1)}) custom-call(s32[1,3]{1,0:T(1,128)S(1)} %copy-done.4, f32[32,128,128]{2,1,0:T(8,128)S(1)} %get-tuple-element.88.refs_0_, f32[128,128]{1,0:T(8,128)S(1)} %get-tuple-element.89.refs_1_, f32[2,5,64,128]{3,2,1,0:T(8,128)S(1)} %bitcast.25, ...), custom_call_target="tpu_custom_call" | custom-call | flops 10000000 | bytes 20004864 | tf_op jit(solution)/shard_map/pallas_call | solution.py:77
  54.7 1.9 %collective-permute-start.4 = (f32[80,128]{1,0:T(8,128)S(1)}, f32[80,128]{1,0:T(8,128)S(1)}, u32[]{:S(2)}, u32[]{:S(2)}) collective-permute-start(f32[80,128]{1,0:T(8,128)S(1)} %get-tuple-element.109), channel_id=1, source_target_pairs={{1,4},{4,1},{3,6},{6,3},{5,8},{8,5},{7,10},{10,7},{9,12},{12,9},{1... | collective-permute-start | bytes 122888 | tf_op jit(solution)/shard_map/ppermute | solution.py:892
  56.6 3.5 %shard_map.157 = (f32[32,128,128]{2,1,0:T(8,128)S(1)}, f32[32,128,128]{2,1,0:T(8,128)S(1)}, f32[32,128,128]{2,1,0:T(8,128)S(1)}) custom-call(s32[1,3]{1,0:T(1,128)S(1)} %copy-done.4, f32[36,128,128]{2,1,0:T(8,128)S(1)} %get-tuple-element.100.refs_0_, f32[32,128,128]{2,1,0:T(8,128)S(1)} %get-tuple-element.76.refs_0_.refs_1_, ...), custom_call_target="tpu_custom_call" | custom-call | flops 4000000000 | bytes 13451264 | tf_op jit(solution)/shard_map/pallas_call | solution.py:77
  60.1 8.9 %all-gather.2 = f32[160,128]{1,0:T(8,128)S(1)} all-gather(f32[80,128]{1,0:T(8,128)S(1)} %collective-permute-done.4), channel_id=4, replica_groups={{0,1},{2,3},{4,5},{6,7},{8,9},{10,11},{12,13},{14,15},{16,17},{18,19},{..., dimensions={0}, use_global_device_ids=true | all-gather | bytes 122880 | tf_op jit(solution)/shard_map/all_gather | solution.py:893
  69.1 3.1 %shard_map.158 = (f32[32,128,128]{2,1,0:T(8,128)S(1)}, f32[5,64,128]{2,1,0:T(8,128)S(1)}, f32[128,128]{1,0:T(8,128)S(1)}, f32[6,4,40,128]{3,2,1,0:T(8,128)S(1)},...) custom-call(s32[1,3]{1,0:T(1,128)S(1)} %copy-done.4, f32[32,128,128]{2,1,0:T(8,128)S(1)} %get-tuple-element.107.refs_0_, ...), custom_call_target="tpu_custom_call" | custom-call | flops 10000000 | bytes 14545408 | tf_op jit(solution)/shard_map/pallas_call | solution.py:77
  72.2 12.2 %all-gather.3 = f32[20,64,128]{2,1,0:T(8,128)S(1)} all-gather(f32[5,64,128]{2,1,0:T(8,128)S(1)} %get-tuple-element.114), channel_id=5, replica_groups=mesh['patch'=128,'slab'=4] {'slab'}, dimensions={0}, use_global_device_ids=true | all-gather | bytes 819200 | tf_op jit(solution)/shard_map/all_gather | solution.py:935
  84.4 2.3 %shard_map.159 = (f32[36,128,128]{2,1,0:T(8,128)S(1)}, f32[2,40,128]{2,1,0:T(8,128)S(1)}, f32[40,128]{1,0:T(8,128)S(1)}) custom-call(s32[1,3]{1,0:T(1,128)S(1)} %copy-done.4, f32[32,128,128]{2,1,0:T(8,128)S(1)} %get-tuple-element.112.refs_0_, f32[128,128]{1,0:T(8,128)S(1)} %get-tuple-element.113.refs_1_, f32[4,5,64,128]{3,2,1,0:T(8,128)S(1)} %bitcast.24, ...), custom_call_target="tpu_custom_call" | custom-call | flops 10000000 | bytes 20230144 | tf_op jit(solution)/shard_map/pallas_call | solution.py:77
  86.6 1.9 %collective-permute-start.5 = (f32[40,128]{1,0:T(8,128)S(1)}, f32[40,128]{1,0:T(8,128)S(1)}, u32[]{:S(2)}, u32[]{:S(2)}) collective-permute-start(f32[40,128]{1,0:T(8,128)S(1)} %get-tuple-element.123), channel_id=1, source_target_pairs={{1,4},{4,1},{3,6},{6,3},{5,8},{8,5},{7,10},{10,7},{9,12},{12,9},{1... | collective-permute-start | bytes 61448 | tf_op jit(solution)/shard_map/ppermute | solution.py:892
  88.6 3.7 %shard_map.160 = (f32[32,128,128]{2,1,0:T(8,128)S(1)}, f32[32,128,128]{2,1,0:T(8,128)S(1)}, f32[32,128,128]{2,1,0:T(8,128)S(1)}) custom-call(s32[1,3]{1,0:T(1,128)S(1)} %copy-done.4, f32[36,128,128]{2,1,0:T(8,128)S(1)} %get-tuple-element.116.refs_0_, f32[32,128,128]{2,1,0:T(8,128)S(1)} %get-tuple-element.76.refs_0_.refs_1_, ...), custom_call_target="tpu_custom_call" | custom-call | flops 4000000000 | bytes 17645568 | tf_op jit(solution)/shard_map/pallas_call | solution.py:77
  92.3 7.7 %all-gather.4 = f32[80,128]{1,0:T(8,128)S(1)} all-gather(f32[40,128]{1,0:T(8,128)S(1)} %collective-permute-done.5), channel_id=6, replica_groups={{0,1},{2,3},{4,5},{6,7},{8,9},{10,11},{12,13},{14,15},{16,17},{18,19},{..., dimensions={0}, use_global_device_ids=true | all-gather | bytes 61440 | tf_op jit(solution)/shard_map/all_gather | solution.py:893
  100.1 3.1 %shard_map.161 = (f32[32,128,128]{2,1,0:T(8,128)S(1)}, f32[5,64,128]{2,1,0:T(8,128)S(1)}, f32[128,128]{1,0:T(8,128)S(1)}, f32[6,4,40,128]{3,2,1,0:T(8,128)S(1)},...) custom-call(s32[1,3]{1,0:T(1,128)S(1)} %copy-done.4, f32[32,128,128]{2,1,0:T(8,128)S(1)} %get-tuple-element.121.refs_0_, ...), custom_call_target="tpu_custom_call" | custom-call | flops 10000000 | bytes 14463488 | tf_op jit(solution)/shard_map/pallas_call | solution.py:77
  103.2 11.9 %all-gather.5 = f32[20,64,128]{2,1,0:T(8,128)S(1)} all-gather(f32[5,64,128]{2,1,0:T(8,128)S(1)} %get-tuple-element.126), channel_id=7, replica_groups=mesh['patch'=128,'slab'=4] {'slab'}, dimensions={0}, use_global_device_ids=true | all-gather | bytes 819200 | tf_op jit(solution)/shard_map/all_gather | solution.py:935
  115.1 3.0 %shard_map.162 = (f32[36,128,128]{2,1,0:T(8,128)S(1)}, f32[2,40,128]{2,1,0:T(8,128)S(1)}, f32[40,128]{1,0:T(8,128)}) custom-call(s32[1,3]{1,0:T(1,128)S(1)} %copy-done.4, f32[32,128,128]{2,1,0:T(8,128)S(1)} %get-tuple-element.124.refs_0_, f32[128,128]{1,0:T(8,128)S(1)} %get-tuple-element.125.refs_1_, f32[4,5,64,128]{3,2,1,0:T(8,128)S(1)} %bitcast.23, ...), custom_call_target="tpu_custom_call" | custom-call | flops 10000000 | bytes 20230144 | tf_op jit(solution)/shard_map/pallas_call | solution.py:77
  118.1 4.1 %shard_map.163 = (f32[16,128,128]{2,1,0:T(8,128)S(1)}, f32[32,128,128]{2,1,0:T(8,128)S(1)}, f32[2,72,128]{2,1,0:T(8,128)S(1)}, f32[72,128]{1,0:T(8,128)S(1)}) custom-call(s32[1,3]{1,0:T(1,128)S(1)} %copy-done.4, f32[36,128,128]{2,1,0:T(8,128)S(1)} %get-tuple-element.128.refs_0_, f32[32,128,128]{2,1,0:T(8,128)S(1)} %get-tuple-element.76.refs_0_.refs_1_, ...), custom_call_target="tpu_custom_call" | custom-call | flops 3000000000 | bytes 14585856 | tf_op jit(solution)/shard_map/pallas_call | solution.py:77
  124.2 2.3 %shard_map.166 = (f32[32,32,128]{2,1,0:T(8,128)S(1)}, f32[32,32,128]{2,1,0:T(8,128)S(1)}) custom-call(s32[1,3]{1,0:T(1,128)S(1)} %copy-done.4, f32[32,128,128]{2,1,0:T(8,128)S(1)} %get-tuple-element.141.refs_0_, bf16[256,256]{1,0:T(8,128)(2,1)S(1)} %get-tuple-element.142.refs_1_, bf16[128,256]{1,0:T(8,128)(2,1)S(1)} %get-tuple-element.143.refs_2_), custom_call_target="tpu_custom_call" | custom-call | flops 3000000000 | bytes 3342336 | tf_op jit(solution)/shard_map/pallas_call | solution.py:77
  126.5 4.4 %collective-permute-start.7 = (f32[32,32,128]{2,1,0:T(8,128)S(1)}, f32[32,32,128]{2,1,0:T(8,128)S(1)}, u32[]{:S(2)}, u32[]{:S(2)}) collective-permute-start(f32[32,32,128]{2,1,0:T(8,128)S(1)} %get-tuple-element.145), channel_id=1, source_target_pairs={{0,2},{2,0},{1,3},{3,1},{4,6},{6,4},{5,7},{7,5},{8,10},{10,8},{9,1... | collective-permute-start | bytes 1572872 | tf_op jit(solution)/shard_map/ppermute | solution.py:973
  130.9 7.9 %collective-permute-done.6 = f32[72,128]{1,0:T(8,128)S(1)} collective-permute-done((f32[72,128]{1,0:T(8,128)S(1)}, f32[72,128]{1,0:T(8,128)S(1)}, u32[]{:S(2)}, u32[]{:S(2)}) %collective-permute-start.6) | collective-permute-done | bytes 36896 | tf_op jit(solution)/shard_map/ppermute | solution.py:892
  140.7 2.2 %shard_map.164 = (f32[6,32,128]{2,1,0:T(8,128)S(1)}, f32[2,40,128]{2,1,0:T(8,128)S(1)}) custom-call(s32[1,3]{1,0:T(1,128)S(1)} %copy-done.4, f32[1,3]{1,0:T(1,128)S(1)} %copy-done.11, f32[2,72,128]{2,1,0:T(8,128)S(1)} %get-tuple-element.136.refs_1_, f32[2,72,128]{2,1,0:T(8,128)S(1)} %bitcast.32, f32[6,4,40,128]{3,2,1,0:T(8,128)S(1)} %get-tuple-element.127.refs_13_.refs_3_, ...), custom_call_target="tpu_custom_call" | custom-call | flops 80000000000 | bytes 1135104 | tf_op jit(solution)/shard_map/pallas_call | solution.py:77
  142.9 4.9 %collective-permute-start.8 = (f32[6,32,128]{2,1,0:T(8,128)S(1)}, f32[6,32,128]{2,1,0:T(8,128)S(1)}, u32[]{:S(2)}, u32[]{:S(2)}) collective-permute-start(f32[6,32,128]{2,1,0:T(8,128)S(1)} %get-tuple-element.146.refs_2_), channel_id=1, source_target_pairs={{0,2},{2,0},{1,3},{3,1},{4,6},{6,4},{5,7},{7,5},{8,10},{10,8},{9,1... | collective-permute-start | bytes 294920 | tf_op jit(solution)/shard_map/ppermute | solution.py:987
  149.7 4.6 %collective-permute-done.8.refs_3_ = f32[6,32,128]{2,1,0:T(8,128)S(1)} collective-permute-done((f32[6,32,128]{2,1,0:T(8,128)S(1)}, f32[6,32,128]{2,1,0:T(8,128)S(1)}, u32[]{:S(2)}, u32[]{:S(2)}) %collective-permute-start.8) | collective-permute-done | bytes 98336 | tf_op jit(solution)/shard_map/ppermute | solution.py:987
  154.3 2.7 %shard_map.167 = f32[62,3969]{1,0:T(8,128)S(1)} custom-call(s32[1,3]{1,0:T(1,128)S(1)} %copy-done.4, f32[1024,128]{1,0:T(8,128)S(1)} %bitcast.26, f32[1024,128]{1,0:T(8,128)S(1)} %bitcast.27, f32[6,32,128]{2,1,0:T(8,128)S(1)} %get-tuple-element.146.refs_2_, f32[6,32,128]{2,1,0:T(8,128)S(1)} %collective-permute-done.8.refs_3_, ...), custom_call_target="tpu_custom_call" | custom-call | flops 10000000 | bytes 2642680 | tf_op jit(solution)/shard_map/pallas_call | solution.py:77
  157.0 2.0 %copy.17 = f32[1,62,3969]{2,0,1:T(1,128)} copy(f32[1,62,3969]{2,1,0:T(8,128)S(1)} %bitcast.22) | data formatting | bytes 1968624
  (43 shorter events, 10.8 us)
Async XLA Ops:
  0.6 10.4 %copy-start.12 = (f32[1,16,16384]{2,1,0:T(8,128)S(1)}, f32[1,16,16384]{2,1,0:T(8,128)}, u32[]{:S(2)}) copy-start(f32[1,16,16384]{2,1,0:T(8,128)} %param.15) | copy-start | bytes 3145732
  0.6 12.6 %copy-start = (f32[128,128]{1,0:T(8,128)S(1)}, f32[128,128]{1,0:T(8,128)}, u32[]{:S(2)}) copy-start(f32[128,128]{1,0:T(8,128)} %refs_7_.5) | copy-start | bytes 196612
  0.7 12.6 %copy-start.1 = (f32[128,128]{1,0:T(8,128)S(1)}, f32[128,128]{1,0:T(8,128)}, u32[]{:S(2)}) copy-start(f32[128,128]{1,0:T(8,128)} %refs_1_.1) | copy-start | bytes 196612
  0.7 12.6 %copy-start.2 = (f32[128,128]{1,0:T(8,128)S(1)}, f32[128,128]{1,0:T(8,128)}, u32[]{:S(2)}) copy-start(f32[128,128]{1,0:T(8,128)} %refs_2_.1) | copy-start | bytes 196612
  0.7 12.6 %copy-start.3 = (f32[126,128]{1,0:T(8,128)S(1)}, f32[126,128]{1,0:T(8,128)}, u32[]{:S(2)}) copy-start(f32[126,128]{1,0:T(8,128)} %refs_9_.1) | copy-start | bytes 193540
  0.7 12.6 %copy-start.4 = (s32[1,3]{1,0:T(1,128)S(1)}, s32[1,3]{1,0:T(1,128)}, u32[]{:S(2)}) copy-start(s32[1,3]{1,0:T(1,128)} %links_ref.37) | copy-start | bytes 40
  0.7 12.6 %copy-start.5 = (f32[64,64]{1,0:T(8,128)S(1)}, f32[64,64]{1,0:T(8,128)}, u32[]{:S(2)}) copy-start(f32[64,64]{1,0:T(8,128)} %refs_3_.1) | copy-start | bytes 49156
  0.7 12.6 %copy-start.6 = (f32[64,64]{1,0:T(8,128)S(1)}, f32[64,64]{1,0:T(8,128)}, u32[]{:S(2)}) copy-start(f32[64,64]{1,0:T(8,128)} %refs_4_.1) | copy-start | bytes 49156
  0.7 12.6 %copy-start.7 = (f32[64,64]{1,0:T(8,128)S(1)}, f32[64,64]{1,0:T(8,128)}, u32[]{:S(2)}) copy-start(f32[64,64]{1,0:T(8,128)} %refs_7_.3) | copy-start | bytes 49156
  0.7 12.6 %copy-start.8 = (f32[62,64]{1,0:T(8,128)S(1)}, f32[62,64]{1,0:T(8,128)}, u32[]{:S(2)}) copy-start(f32[62,64]{1,0:T(8,128)} %refs_10_.1) | copy-start | bytes 47620
  0.7 12.6 %copy-start.9 = (f32[128]{0:T(128)S(1)}, f32[128]{0:T(128)}, u32[]{:S(2)}) copy-start(f32[128]{0:T(128)} %param.22) | copy-start | bytes 1540
  0.7 12.6 %copy-start.10 = (f32[64]{0:T(128)S(1)}, f32[64]{0:T(128)}, u32[]{:S(2)}) copy-start(f32[64]{0:T(128)} %param.24) | copy-start | bytes 772
  0.8 12.6 %copy-start.11 = (f32[1,3]{1,0:T(1,128)S(1)}, f32[1,3]{1,0:T(1,128)}, u32[]{:S(2)}) copy-start(f32[1,3]{1,0:T(1,128)} %refs_0_.3) | copy-start | bytes 40
  2.3 12.4 %collective-permute-start = (f32[16,128,128]{2,1,0:T(8,128)S(1)}, f32[16,128,128]{2,1,0:T(8,128)S(1)}, u32[]{:S(2)}, u32[]{:S(2)}) collective-permute-start(f32[16,128,128]{2,1,0:T(8,128)S(1)} %bitcast.20), channel_id=1, source_target_pairs={{0,1},{1,0},{2,3},{3,2},{4,5},{5,4},{6,7},{7,6},{8,9},{9,8},{10,11... | collective-permute-start | bytes 3145736 | tf_op jit(solution)/shard_map/ppermute | solution.py:898
  11.3 37.8 %collective-permute-start.3 = (f32[16,128,128]{2,1,0:T(8,128)S(1)}, f32[16,128,128]{2,1,0:T(8,128)S(1)}, u32[]{:S(2)}, u32[]{:S(2)}) collective-permute-start(f32[16,128,128]{2,1,0:T(8,128)S(1)} %bitcast.18), channel_id=1, source_target_pairs={{0,1},{1,0},{2,3},{3,2},{4,5},{5,4},{6,7},{7,6},{8,9},{9,8},{10,11... | collective-permute-start | bytes 3145736 | tf_op jit(solution)/shard_map/ppermute | solution.py:899
  15.7 6.8 %collective-permute-start.1 = (f32[48,128]{1,0:T(8,128)S(1)}, f32[48,128]{1,0:T(8,128)S(1)}, u32[]{:S(2)}, u32[]{:S(2)}) collective-permute-start(f32[48,128]{1,0:T(8,128)S(1)} %get-tuple-element.80.refs_0_), channel_id=1, source_target_pairs={{1,4},{4,1},{3,6},{6,3},{5,8},{8,5},{7,10},{10,7},{9,12},{12,9},{1... | collective-permute-start | bytes 73736 | tf_op jit(solution)/shard_map/ppermute | solution.py:892
  38.0 12.1 %collective-permute-start.2 = (f32[5,64,128]{2,1,0:T(8,128)S(1)}, f32[5,64,128]{2,1,0:T(8,128)S(1)}, u32[]{:S(2)}, u32[]{:S(2)}) collective-permute-start(f32[5,64,128]{2,1,0:T(8,128)S(1)} %get-tuple-element.90.refs_0_), channel_id=1, source_target_pairs={{0,2},{2,0},{1,3},{3,1},{4,6},{6,4},{5,7},{7,5},{8,10},{10,8},{9,1... | collective-permute-start | bytes 491528 | tf_op jit(solution)/shard_map/ppermute | solution.py:937
  54.7 5.4 %collective-permute-start.4 = (f32[80,128]{1,0:T(8,128)S(1)}, f32[80,128]{1,0:T(8,128)S(1)}, u32[]{:S(2)}, u32[]{:S(2)}) collective-permute-start(f32[80,128]{1,0:T(8,128)S(1)} %get-tuple-element.109), channel_id=1, source_target_pairs={{1,4},{4,1},{3,6},{6,3},{5,8},{8,5},{7,10},{10,7},{9,12},{12,9},{1... | collective-permute-start | bytes 122888 | tf_op jit(solution)/shard_map/ppermute | solution.py:892
  86.6 5.7 %collective-permute-start.5 = (f32[40,128]{1,0:T(8,128)S(1)}, f32[40,128]{1,0:T(8,128)S(1)}, u32[]{:S(2)}, u32[]{:S(2)}) collective-permute-start(f32[40,128]{1,0:T(8,128)S(1)} %get-tuple-element.123), channel_id=1, source_target_pairs={{1,4},{4,1},{3,6},{6,3},{5,8},{8,5},{7,10},{10,7},{9,12},{12,9},{1... | collective-permute-start | bytes 61448 | tf_op jit(solution)/shard_map/ppermute | solution.py:892
  122.2 16.6 %collective-permute-start.6 = (f32[72,128]{1,0:T(8,128)S(1)}, f32[72,128]{1,0:T(8,128)S(1)}, u32[]{:S(2)}, u32[]{:S(2)}) collective-permute-start(f32[72,128]{1,0:T(8,128)S(1)} %get-tuple-element.137), channel_id=1, source_target_pairs={{1,4},{4,1},{3,6},{6,3},{5,8},{8,5},{7,10},{10,7},{9,12},{12,9},{1... | collective-permute-start | bytes 110600 | tf_op jit(solution)/shard_map/ppermute | solution.py:892
  126.5 27.8 %collective-permute-start.7 = (f32[32,32,128]{2,1,0:T(8,128)S(1)}, f32[32,32,128]{2,1,0:T(8,128)S(1)}, u32[]{:S(2)}, u32[]{:S(2)}) collective-permute-start(f32[32,32,128]{2,1,0:T(8,128)S(1)} %get-tuple-element.145), channel_id=1, source_target_pairs={{0,2},{2,0},{1,3},{3,1},{4,6},{6,4},{5,7},{7,5},{8,10},{10,8},{9,1... | collective-permute-start | bytes 1572872 | tf_op jit(solution)/shard_map/ppermute | solution.py:973
  142.9 11.4 %collective-permute-start.8 = (f32[6,32,128]{2,1,0:T(8,128)S(1)}, f32[6,32,128]{2,1,0:T(8,128)S(1)}, u32[]{:S(2)}, u32[]{:S(2)}) collective-permute-start(f32[6,32,128]{2,1,0:T(8,128)S(1)} %get-tuple-element.146.refs_2_), channel_id=1, source_target_pairs={{0,2},{2,0},{1,3},{3,1},{4,6},{6,4},{5,7},{7,5},{8,10},{10,8},{9,1... | collective-permute-start | bytes 294920 | tf_op jit(solution)/shard_map/ppermute | solution.py:987

commit v3 on v2

--- a/solution.py
+++ b/solution.py
@@ -20,7 +20,7 @@
 REACH = HALF + BAND
 ROWS = 40
 TOP = HALF - BAND
-CHUNK = 64
+CHUNK = 32
 COARSE = N - 2
 
 
@@ -47,6 +47,14 @@
 
 def dot_full(x, y):
     return jnp.dot(x, y, precision=HIGHEST, preferred_element_type=F32)
+
+
+def mirrored(x, mirror):
+    high, rest = split(x)
+    middle, low = split(x - high.astype(F32))
+    return jnp.dot(
+        jnp.concatenate([high, middle, low], axis=-1), mirror, preferred_element_type=F32
+    )
 
 
 def pack_right(a):
@@ -109,16 +117,25 @@
     return jnp.right_shift(inside, 4), jnp.bitwise_and(inside, BLOCK - 1)
 
 
-def load_layer(ints, own_ref, other_ref, out_ref, t):
-    block, index = source_layer(ints, t)
-    mine = own_ref[index]
-    theirs = other_ref[index]
-    value = jnp.where(block == ints[3], mine, theirs)
-    out_ref[t] = value
+def load_layers(ints, own_ref, other_ref, out_ref):
+    def run(turn):
+        def body(g, carry):
+            for q in range(8):
+                t = g * 8 + q
+                block, index = source_layer(ints, t)
+                value = jnp.where(block == ints[3], own_ref[index], other_ref[index])
+                out_ref[t] = value.T if turn else value
+            return carry
+
+        lax.fori_loop(0, HALF // 8, body, 0)
+
+    @pl.when(ints[1] == 0)
+    def _():
+        run(False)
 
     @pl.when(ints[1] == 1)
     def _():
-        out_ref[t] = value.T
+        run(True)
 
 
 def slot(ints, west, east, slot_ref):
@@ -131,11 +148,7 @@
 
 
 def load_kernel(ints, own, other, f_ref, pay_ref, slot_ref):
-    def body(t, carry):
-        load_layer(ints, own, other, f_ref, t)
-        return carry
-
-    lax.fori_loop(0, HALF, body, 0, unroll=4)
+    load_layers(ints, own, other, f_ref)
     flag = jnp.broadcast_to(ints[0].astype(F32), (8, N))
     for side in range(2):
         rows = face_rows(ints, f_ref, side)
@@ -144,11 +157,7 @@
 
 
 def reaction_kernel(ints, ready, own, other, r_ref, face_ref):
-    def body(t, carry):
-        load_layer(ints, own, other, r_ref, t)
-        return carry
-
-    lax.fori_loop(0, HALF, body, 0, unroll=4)
+    load_layers(ints, own, other, r_ref)
     for side in range(2):
         face_ref[side] = face_rows(ints, r_ref, side)
 
@@ -315,7 +324,7 @@
 
 
 def orient_all(arrays, mirror, masks):
-    turned = dot_full(jnp.concatenate([a for _, a in arrays], axis=0), mirror[...])
+    turned = mirrored(jnp.concatenate([a for _, a in arrays], axis=0), mirror[...])
     return [
         jnp.where(masks[side], turned[q * ROWS:(q + 1) * ROWS], a)
         for q, (side, a) in enumerate(arrays)
@@ -373,9 +382,9 @@
                 z_ref[t, part, :] = x
         low_ref[part, :] = lowest
 
-        @pl.when(c == core)
+        @pl.when(jnp.right_shift(c, 1) == core)
         def _():
-            there = pl.ds(0, CHUNK)
+            there = pl.ds(pl.multiple_of(jnp.bitwise_and(c, 1) * CHUNK, CHUNK), CHUNK)
             for s in range(BAND):
                 msg_ref[s, there, :] = z[TOP + s]
             msg_ref[BAND, there, :] = lowest
@@ -386,7 +395,7 @@
 
 
 def first_kernel(
-    ints, gh, own_pay, rec, scal, spread, b_full, mirror, l_ref, modes,
+    ints, gh, own_pay, rec, scal, spread, wb, mirror, l_ref, modes,
     z_ref, msg_ref, low_ref, state_ref, rows_u, rows_g, rows_hat,
 ):
     received = (rec[0], rec[1])
@@ -401,12 +410,12 @@
     rows_u[...] = jnp.zeros_like(rows_u)
     for side in range(2):
         rows_g[side] = turned[side]
-        rows_hat[side] = dot_full(turned[side], b_full[...])
+        rows_hat[side] = right_mul(turned[side], wb[...])
     eliminate_forward(gh, spread, rows_hat, l_ref, modes, z_ref, msg_ref, low_ref, ints[3])
 
 
 def next_kernel(
-    ints, gh, own_pay, rec, state_in, scal, nscal, spread, b_full, mirror, mk, vert,
+    ints, gh, own_pay, rec, state_in, scal, nscal, spread, wb, mirror, mk, vert,
     l_ref, modes, z_ref, msg_ref, low_ref, state_ref, rows_u, rows_g, rows_hat,
 ):
     received = (rec[0], rec[1])
@@ -426,22 +435,25 @@
         rows = turned[side] - state[1][2 * side] * step
         rows_u[side] = step
         rows_g[side] = rows
-        rows_hat[side] = dot_full(rows, b_full[...])
+        rows_hat[side] = right_mul(rows, wb[...])
     eliminate_forward(gh, spread, rows_hat, l_ref, modes, z_ref, msg_ref, low_ref, ints[3])
 
 
 def solve_kernel(
     ints, z_ref, low_ref, zr_ref, l_ref, dinv_ref, lm_ref, dm_ref, lo_ref, do_ref, mend, modes, spread, bt_full, state, *refs,
 ):
-    extra, (y_ref, pay_ref, slot_ref, sums) = refs[:-4], refs[-4:]
+    sums = refs[-1]
+    extra = refs[:2] if len(refs) > 4 else ()
+    outs = refs[len(extra):-1]
+    y_ref, pay_ref = outs[:2]
     sums[...] = jnp.zeros_like(sums)
 
     def body(c, carry):
         part = pl.ds(pl.multiple_of(c * CHUNK, CHUNK), CHUNK)
-        source = c
+        source = jnp.right_shift(c, 1)
         if zr_ref.shape[0] > 2:
             source = source + 2 * (1 - ints[2])
-        there = pl.ds(0, CHUNK)
+        there = pl.ds(pl.multiple_of(jnp.bitwise_and(c, 1) * CHUNK, CHUNK), CHUNK)
         sent = [zr_ref[source, s, there, :] for s in range(BAND)]
         weights = (spread[0, part, :], spread[1, part, :])
 
@@ -501,7 +513,8 @@
         if extra:
             pay_ref[side, ROWS:ROWS + HALF] = extra[0][side]
             pay_ref[side, ROWS + HALF:] = extra[1][side]
-    slot(ints, pay_ref[0], pay_ref[1], slot_ref)
+    for slot_ref in outs[2:]:
+        slot(ints, pay_ref[0], pay_ref[1], slot_ref)
 
 
 def back_planes(y, wbt, lb):
@@ -640,7 +653,7 @@
         stack += [near_stiff[side], near_mass[side], mine, theirs]
     restricted = dot_full(jnp.concatenate(stack, axis=0), rt_full[...])
     pieces = [restricted[q * ROWS:(q + 1) * ROWS] for q in range(8)]
-    turned = dot_full(jnp.concatenate([pieces[3], pieces[7]], axis=0), mirror_coarse[...])
+    turned = mirrored(jnp.concatenate([pieces[3], pieces[7]], axis=0), mirror_coarse[...])
     for side in range(2):
         added = jnp.where(masks[side], turned[side * ROWS:(side + 1) * ROWS], pieces[4 * side + 3])
         parts[3 * side] = -pieces[4 * side][:HALF]
@@ -664,32 +677,29 @@
     lax.fori_loop(0, BLOCK, body, 0, unroll=2)
 
 
-def coarse_kernel(
-    ints, kept, arrived, parts, far_parts, profile, profile_rows, vertical, out, blocks, columns,
-):
-    deep = vertical.shape[0]
-    spots = [0, 31, COARSE // 2, COARSE // 2 + 31]
-    weights = vertical[...]
-    stacked = [jnp.concatenate([parts[s], far_parts[s]], axis=0) for s in range(6)]
-    mixed = dot_full(weights, jnp.concatenate(stacked, axis=1))
-    mixed = [mixed[:, s * N:(s + 1) * N] for s in range(6)]
+def vertical_kernel(ints, kept, arrived, vertical, blocks):
     for c in range(32):
         rows = pl.ds(c, HALF, stride=32)
         both = jnp.concatenate([kept[rows, :], arrived[rows, :]], axis=0)
-        blocks[c] = dot_full(weights, both)
+        blocks[c] = dot_full(vertical[...], both)
+
+
+def coarse_kernel(ints, start_blocks, parts, far_parts, profile, profile_rows, vertical, out, blocks, columns):
+    deep = vertical.shape[0]
+    spots = [0, 31, COARSE // 2, COARSE // 2 + 31]
+    stacked = [jnp.concatenate([parts[s], far_parts[s]], axis=0) for s in range(6)]
+    mixed = dot_full(vertical[...], jnp.concatenate(stacked, axis=1))
+    mixed = [mixed[:, s * N:(s + 1) * N] for s in range(6)]
 
     @pl.when(ints[1] == 0)
     def _():
         first = ints[2] * (COARSE // 2) + ints[3] * 31
 
-        def body(c, carry):
-            value = blocks[c]
+        for c in range(32):
+            value = start_blocks[c]
             for s in range(6):
                 value = value + profile[s, pl.ds(first + c, 1), :] * mixed[s]
             blocks[c] = value
-            return carry
-
-        lax.fori_loop(0, 32, body, 0)
 
     @pl.when(ints[1] == 1)
     def _():
@@ -703,7 +713,7 @@
                         columns[s] = pltpu.roll(mixed[s], shift, 1) if shift else mixed[s]
 
         for c in range(32):
-            value = blocks[c]
+            value = start_blocks[c]
             for s in range(6):
                 value = value + columns[s, :, c:c + 1] * profile_rows[s:s + 1, :]
             blocks[c] = value
@@ -758,8 +768,9 @@
     lb[...], lbt[...], lr[...] = pack_left(b), pack_left(bt), pack_left(r)
     bt_out[...], rt_out[...] = bt, rt
     mk[:, :N], mk[:, N:] = m, k
-    mirror[...] = (rows + lanes == N - 1).astype(F32)
-    mirror_coarse[...] = (rows + lanes == COARSE - 1).astype(F32)
+    for out, count in ((mirror, N), (mirror_coarse, COARSE)):
+        reverse = (rows + lanes == count - 1).astype(F32).astype(BF16)
+        out[...] = jnp.concatenate([reverse] * 3, axis=0)
     alpha[...] = a1 * column(eigen[...]) + a2 * eigen[...]
 
     turn = (
@@ -864,13 +875,14 @@
     square, two = (N, N), (2, N, N)
     right = jax.ShapeDtypeStruct((2 * N, 2 * N), BF16)
     left = jax.ShapeDtypeStruct((N, 2 * N), BF16)
+    thrice = jax.ShapeDtypeStruct((3 * N, N), BF16)
     (
         wb, wbt, wrt, lb, lbt, lr, basis_t, restrict_t, mk, mirror, mirror_coarse, vert, scal, spread, mask,
         cut, profile, profile_rows, alpha, bands, modes, vertical,
     ) = call(
         prepare_kernel,
         [
-            right, right, right, left, left, left, square, square, (N, 2 * N), square, square,
+            right, right, right, left, left, left, square, square, (N, 2 * N), thrice, thrice,
             (2, ROWS, ROWS), (2, 8, N), two, two, two, (6, N, N), (8, N), square, (2, 2, BAND + 1, ROWS, N), (4, ROWS, N),
             restrict_vertical.shape,
         ],
@@ -919,7 +931,7 @@
             z, msg, low, state, rows_u, rows_g = call(
                 first_kernel,
                 [field, message, square, state_shape, rows_shape, rows_shape],
-                links, gh, pay, rec, scal, spread, basis_plane, mirror, l, modes,
+                links, gh, pay, rec, scal, spread, wb, mirror, l, modes,
                 scratch=[rows_hat], flops=10_000_000,
             )
         else:
@@ -928,7 +940,7 @@
             z, msg, low, state, rows_u, rows_g = call(
                 next_kernel,
                 [field, message, square, state_shape, rows_shape, rows_shape],
-                links, gh, pay, rec, state, scal, nscal, spread, basis_plane, mirror, mk, vert, l, modes,
+                links, gh, pay, rec, state, scal, nscal, spread, wb, mirror, mk, vert, l, modes,
                 scratch=[rows_hat], flops=10_000_000,
             )
         if sweep > 0:
@@ -946,9 +958,9 @@
         last = sweep == SWEEPS - 1
         size = ROWS + HALF + 8 if sweep == 0 else ROWS
         extra = [react_faces, scal] if sweep == 0 else []
-        y, pay, slot_values = call(
+        y, pay, *slot_values = call(
             solve_kernel,
-            [(REACH, N, N), (2, size, N), (size, N)],
+            [(REACH, N, N), (2, size, N)] + ([] if last else [(size, N)]),
             links, z, low, received, l, dinv, lm, dm, lo, do, mend, modes, spread, basis_t, state, *extra,
             scratch=[sums], flops=10_000_000,
         )
@@ -973,7 +985,7 @@
             arrived = lax.ppermute(sent, "slab", cross)
             rec = arriving()
         else:
-            arriving = swap_faces(slot_values)
+            arriving = swap_faces(slot_values[0])
             up, total, gh = call(
                 plane_kernel, [field, field, field], links, *args, wb, lbt, flops=4_000_000_000
             )
@@ -988,13 +1000,16 @@
     (out_u,) = call(iterate_kernel, [(BLOCK, N, N)], links, up, rows_u, mask, flops=2_000_000_000)
     deep = restrict_vertical.shape[0]
     share = COARSE * COARSE // 4
+    (blocks,) = call(
+        vertical_kernel, [(32, deep, N)],
+        links, kept.reshape(HALF * 32, N), arrived.reshape(HALF * 32, N), vertical, flops=2_000_000_000,
+    )
     (flat,) = call(
         coarse_kernel,
         [(deep, share)],
-        links, kept.reshape(HALF * 32, N), arrived.reshape(HALF * 32, N), parts, far_parts,
-        profile, profile_rows, vertical,
+        links, blocks, parts, far_parts, profile, profile_rows, vertical,
         scratch=[pltpu.VMEM((32, deep, N), F32), pltpu.VMEM((6, deep, N), F32)],
-        flops=10_000_000,
+        flops=20_000_000_000,
     )
     return out_u.reshape(1, BLOCK, N * N), flat[None]
 

time: 159 us -> 155 us (0.975)
  blocking collectives: 58.3 us -> 56 us
  starting transfers between devices: 32.4 us -> 30.1 us
  Pallas kernels: 49.8 us -> 47.7 us
  waiting for transfers between devices: 12.5 us -> 14.2 us
    ppermute x1, starting transfers between devices: 4.44 us -> 2.31 us  [per_device(): arrived = lax.ppermute(sent, 'slab', cross)]
    pallas_call x19 -> x20, Pallas kernels: 49.8 us -> 47.7 us  [call(): pl.pallas_call(body, out_shape=shapes, in_specs=specs, out_specs=[pl.Bloc...]
    all_gather x4, blocking collectives: 31.9 us -> 29.9 us  [swap_faces(): return lambda: lax.all_gather(arrived, 'slab', axis_index_groups=chips)]
  transfers between devices with their start and end apart: 9 -> 9, of which waited for: 2 -> 2; matrix products, arithmetic and copies ran while one was open for 1% -> 1% of each run, Pallas kernels for 18% -> 19%
where the time goes in v3:
time: 155 us; the launch traced here: 154 us
  blocking collectives  56 us (36%)
  Pallas kernels  47.7 us (31%)
  starting transfers between devices  30.1 us (19%)
  waiting for transfers between devices  14.2 us (9%)
  local copies, waits for them, and re-layouts  4.93 us (3%)
    pallas_call x20, Pallas kernels, call(): pl.pallas_call(body, out_shape=shapes, in_specs=specs, out_specs=[pl.Bloc...  47.7 us
    all_gather x4, blocking collectives, swap_faces(): return lambda: lax.all_gather(arrived, 'slab', axis_index_groups=chips)  29.9 us
    all_gather x2, blocking collectives, per_device(): received = lax.all_gather(msg, 'slab')  23.9 us
    ppermute x1, starting transfers between devices, per_device(): other_load = lax.ppermute(own_load, 'slab', pair)  8.79 us
    ppermute x4, waiting for transfers between devices, swap_faces(): arrived = lax.ppermute(slot_values, ('patch', 'slab'), faces)  8.29 us
    ppermute x4, starting transfers between devices, swap_faces(): arrived = lax.ppermute(slot_values, ('patch', 'slab'), faces)  7.86 us
    ppermute x1, waiting for transfers between devices, per_device(): far_parts = lax.ppermute(parts, 'slab', cross)  5.89 us
    ppermute x1, starting transfers between devices, per_device(): crossing = lax.ppermute(msg, 'slab', cross)  4.76 us
  transfers between devices with their start and end apart: 9, of which 2 were waited for; matrix products, arithmetic and copies ran while one was open for 1% of the time, Pallas kernels for 19%

profile of v3, /device:TPU:1, one launch (start us, length us, event | category | flops | bytes accessed | tf_op | source)
XLA Modules:
  0.0 154.1 jit_solution(16056744582457054419)
XLA Ops:
  2.3 8.8 %collective-permute-start = (f32[16,128,128]{2,1,0:T(8,128)S(1)}, f32[16,128,128]{2,1,0:T(8,128)S(1)}, u32[]{:S(2)}, u32[]{:S(2)}) collective-permute-start(f32[16,128,128]{2,1,0:T(8,128)S(1)} %bitcast.20), channel_id=1, source_target_pairs={{0,1},{1,0},{2,3},{3,2},{4,5},{5,4},{6,7},{7,6},{8,9},{9,8},{10,11... | collective-permute-start | bytes 3145736 | tf_op jit(solution)/shard_map/ppermute | solution.py:910
  11.3 1.9 %collective-permute-start.3 = (f32[16,128,128]{2,1,0:T(8,128)S(1)}, f32[16,128,128]{2,1,0:T(8,128)S(1)}, u32[]{:S(2)}, u32[]{:S(2)}) collective-permute-start(f32[16,128,128]{2,1,0:T(8,128)S(1)} %bitcast.18), channel_id=1, source_target_pairs={{0,1},{1,0},{2,3},{3,2},{4,5},{5,4},{6,7},{7,6},{8,9},{9,8},{10,11... | collective-permute-start | bytes 3145736 | tf_op jit(solution)/shard_map/ppermute | solution.py:911
  15.5 1.9 %collective-permute-start.1 = (f32[48,128]{1,0:T(8,128)S(1)}, f32[48,128]{1,0:T(8,128)S(1)}, u32[]{:S(2)}, u32[]{:S(2)}) collective-permute-start(f32[48,128]{1,0:T(8,128)S(1)} %get-tuple-element.80.refs_0_), channel_id=1, source_target_pairs={{1,4},{4,1},{3,6},{6,3},{5,8},{8,5},{7,10},{10,7},{9,12},{12,9},{1... | collective-permute-start | bytes 73736 | tf_op jit(solution)/shard_map/ppermute | solution.py:904
  17.5 2.9 %shard_map.152 = (f32[32,4,128,128]{3,2,1,0:T(8,128)S(1)}, f32[32,128,128]{2,1,0:T(8,128)S(1)}) custom-call(s32[1,3]{1,0:T(1,128)S(1)} %copy-done.4, f32[48,128]{1,0:T(8,128)S(1)} %get-tuple-element.80.refs_0_, f32[128,128]{1,0:T(8,128)S(1)} %get-tuple-element.84.refs_1_.refs_0_, f32[2,2,5,40,128]{4,3,2,1,0:T(8,128)S(1)} %get-tuple-element.85.refs_2_.refs_1_), custom_call_target="tpu_custom_call" | custom-call | flops 3000000000 | bytes 10985472 | tf_op jit(solution)/shard_map/pallas_call | solution.py:85
  20.4 2.0 %shard_map.151.refs_0_ = f32[32,128,128]{2,1,0:T(8,128)S(1)} custom-call(s32[1,3]{1,0:T(1,128)S(1)} %copy-done.4, f32[32,128,128]{2,1,0:T(8,128)S(1)} %get-tuple-element.76.refs_0_.refs_1_, bf16[256,256]{1,0:T(8,128)(2,1)S(1)} %get-tuple-element.77.refs_1_.refs_5_.refs_8_.refs_7_.refs_10_, bf16[128,256]{1,0:T(8,128)(2,1)S(1)} %get-tuple-element.78.refs_2_.refs_9_.refs_11_), custom_call_target="tpu_custom_call" | custom-call | flops 2000000000 | bytes 4390912 | tf_op jit(solution)/shard_map/pallas_call | solution.py:85
  22.4 10.5 %all-gather = f32[96,128]{1,0:T(8,128)S(1)} all-gather(f32[48,128]{1,0:T(8,128)S(1)} %collective-permute-done.1), channel_id=2, replica_groups={{0,1},{2,3},{4,5},{6,7},{8,9},{10,11},{12,13},{14,15},{16,17},{18,19},{..., dimensions={0}, use_global_device_ids=true | all-gather | bytes 73728 | tf_op jit(solution)/shard_map/all_gather | solution.py:905
  34.7 4.8 %collective-permute-start.2 = (f32[5,64,128]{2,1,0:T(8,128)S(1)}, f32[5,64,128]{2,1,0:T(8,128)S(1)}, u32[]{:S(2)}, u32[]{:S(2)}) collective-permute-start(f32[5,64,128]{2,1,0:T(8,128)S(1)} %get-tuple-element.90.refs_0_), channel_id=1, source_target_pairs={{0,2},{2,0},{1,3},{3,1},{4,6},{6,4},{5,7},{7,5},{8,10},{10,8},{9,1... | collective-permute-start | bytes 491528 | tf_op jit(solution)/shard_map/ppermute | solution.py:949
  39.4 6.4 %shard_map.154 = (f32[4,4,128,128]{3,2,1,0:T(8,128)S(1)}, f32[4,128,128]{2,1,0:T(8,128)S(1)}, f32[8,4,128,128]{3,2,1,0:T(8,128)S(1)}, f32[4,128,128]{2,1,0:T(8,128)S(1)}, f32[128,128]{1,0:T(8,128)S(1)}) custom-call(s32[1,3]{1,0:T(1,128)S(1)} %copy-done.4, f32[128,128]{1,0:T(8,128)S(1)} %get-tuple-element.84.refs_1_.refs_0_, ...), custom_call_target="tpu_custom_call" | custom-call | flops 5000000000 | bytes 14778368 | tf_op jit(solution)/shard_map/pallas_call | solution.py:85
  46.7 2.3 %all-gather.1 = f32[10,64,128]{2,1,0:T(8,128)S(1)} all-gather(f32[5,64,128]{2,1,0:T(8,128)S(1)} %collective-permute-done.2), channel_id=3, replica_groups={{0,1},{2,3},{4,5},{6,7},{8,9},{10,11},{12,13},{14,15},{16,17},{18,19},{..., dimensions={0}, use_global_device_ids=true | all-gather | bytes 491520 | tf_op jit(solution)/shard_map/all_gather | solution.py:957
  49.0 2.2 %shard_map.156 = (f32[36,128,128]{2,1,0:T(8,128)S(1)}, f32[2,80,128]{2,1,0:T(8,128)S(1)}, f32[80,128]{1,0:T(8,128)S(1)}) custom-call(s32[1,3]{1,0:T(1,128)S(1)} %copy-done.4, f32[32,128,128]{2,1,0:T(8,128)S(1)} %get-tuple-element.88.refs_0_, f32[128,128]{1,0:T(8,128)S(1)} %get-tuple-element.89.refs_1_, f32[2,5,64,128]{3,2,1,0:T(8,128)S(1)} %bitcast.24, ...), custom_call_target="tpu_custom_call" | custom-call | flops 10000000 | bytes 20004864 | tf_op jit(solution)/shard_map/pallas_call | solution.py:85
  51.2 1.9 %collective-permute-start.4 = (f32[80,128]{1,0:T(8,128)S(1)}, f32[80,128]{1,0:T(8,128)S(1)}, u32[]{:S(2)}, u32[]{:S(2)}) collective-permute-start(f32[80,128]{1,0:T(8,128)S(1)} %get-tuple-element.109), channel_id=1, source_target_pairs={{1,4},{4,1},{3,6},{6,3},{5,8},{8,5},{7,10},{10,7},{9,12},{12,9},{1... | collective-permute-start | bytes 122888 | tf_op jit(solution)/shard_map/ppermute | solution.py:904
  53.1 3.5 %shard_map.157 = (f32[32,128,128]{2,1,0:T(8,128)S(1)}, f32[32,128,128]{2,1,0:T(8,128)S(1)}, f32[32,128,128]{2,1,0:T(8,128)S(1)}) custom-call(s32[1,3]{1,0:T(1,128)S(1)} %copy-done.4, f32[36,128,128]{2,1,0:T(8,128)S(1)} %get-tuple-element.100.refs_0_, f32[32,128,128]{2,1,0:T(8,128)S(1)} %get-tuple-element.76.refs_0_.refs_1_, ...), custom_call_target="tpu_custom_call" | custom-call | flops 4000000000 | bytes 13451264 | tf_op jit(solution)/shard_map/pallas_call | solution.py:85
  56.6 9.2 %all-gather.2 = f32[160,128]{1,0:T(8,128)S(1)} all-gather(f32[80,128]{1,0:T(8,128)S(1)} %collective-permute-done.4), channel_id=4, replica_groups={{0,1},{2,3},{4,5},{6,7},{8,9},{10,11},{12,13},{14,15},{16,17},{18,19},{..., dimensions={0}, use_global_device_ids=true | all-gather | bytes 122880 | tf_op jit(solution)/shard_map/all_gather | solution.py:905
  65.7 2.7 %shard_map.158 = (f32[32,128,128]{2,1,0:T(8,128)S(1)}, f32[5,64,128]{2,1,0:T(8,128)S(1)}, f32[128,128]{1,0:T(8,128)S(1)}, f32[6,4,40,128]{3,2,1,0:T(8,128)S(1)},...) custom-call(s32[1,3]{1,0:T(1,128)S(1)} %copy-done.4, f32[32,128,128]{2,1,0:T(8,128)S(1)} %get-tuple-element.107.refs_0_, ...), custom_call_target="tpu_custom_call" | custom-call | flops 10000000 | bytes 14643712 | tf_op jit(solution)/shard_map/pallas_call | solution.py:85
  68.4 12.0 %all-gather.3 = f32[20,64,128]{2,1,0:T(8,128)S(1)} all-gather(f32[5,64,128]{2,1,0:T(8,128)S(1)} %get-tuple-element.114), channel_id=5, replica_groups=mesh['patch'=128,'slab'=4] {'slab'}, dimensions={0}, use_global_device_ids=true | all-gather | bytes 819200 | tf_op jit(solution)/shard_map/all_gather | solution.py:947
  80.4 2.2 %shard_map.159 = (f32[36,128,128]{2,1,0:T(8,128)S(1)}, f32[2,40,128]{2,1,0:T(8,128)S(1)}, f32[40,128]{1,0:T(8,128)S(1)}) custom-call(s32[1,3]{1,0:T(1,128)S(1)} %copy-done.4, f32[32,128,128]{2,1,0:T(8,128)S(1)} %get-tuple-element.112.refs_0_, f32[128,128]{1,0:T(8,128)S(1)} %get-tuple-element.113.refs_1_, f32[4,5,64,128]{3,2,1,0:T(8,128)S(1)} %bitcast.23, ...), custom_call_target="tpu_custom_call" | custom-call | flops 10000000 | bytes 20230144 | tf_op jit(solution)/shard_map/pallas_call | solution.py:85
  82.6 2.1 %collective-permute-start.5 = (f32[40,128]{1,0:T(8,128)S(1)}, f32[40,128]{1,0:T(8,128)S(1)}, u32[]{:S(2)}, u32[]{:S(2)}) collective-permute-start(f32[40,128]{1,0:T(8,128)S(1)} %get-tuple-element.123), channel_id=1, source_target_pairs={{1,4},{4,1},{3,6},{6,3},{5,8},{8,5},{7,10},{10,7},{9,12},{12,9},{1... | collective-permute-start | bytes 61448 | tf_op jit(solution)/shard_map/ppermute | solution.py:904
  84.7 3.7 %shard_map.160 = (f32[32,128,128]{2,1,0:T(8,128)S(1)}, f32[32,128,128]{2,1,0:T(8,128)S(1)}, f32[32,128,128]{2,1,0:T(8,128)S(1)}) custom-call(s32[1,3]{1,0:T(1,128)S(1)} %copy-done.4, f32[36,128,128]{2,1,0:T(8,128)S(1)} %get-tuple-element.116.refs_0_, f32[32,128,128]{2,1,0:T(8,128)S(1)} %get-tuple-element.76.refs_0_.refs_1_, ...), custom_call_target="tpu_custom_call" | custom-call | flops 4000000000 | bytes 17645568 | tf_op jit(solution)/shard_map/pallas_call | solution.py:85
  88.4 8.4 %all-gather.4 = f32[80,128]{1,0:T(8,128)S(1)} all-gather(f32[40,128]{1,0:T(8,128)S(1)} %collective-permute-done.5), channel_id=6, replica_groups={{0,1},{2,3},{4,5},{6,7},{8,9},{10,11},{12,13},{14,15},{16,17},{18,19},{..., dimensions={0}, use_global_device_ids=true | all-gather | bytes 61440 | tf_op jit(solution)/shard_map/all_gather | solution.py:905
  96.7 2.8 %shard_map.161 = (f32[32,128,128]{2,1,0:T(8,128)S(1)}, f32[5,64,128]{2,1,0:T(8,128)S(1)}, f32[128,128]{1,0:T(8,128)S(1)}, f32[6,4,40,128]{3,2,1,0:T(8,128)S(1)},...) custom-call(s32[1,3]{1,0:T(1,128)S(1)} %copy-done.4, f32[32,128,128]{2,1,0:T(8,128)S(1)} %get-tuple-element.121.refs_0_, ...), custom_call_target="tpu_custom_call" | custom-call | flops 10000000 | bytes 14561792 | tf_op jit(solution)/shard_map/pallas_call | solution.py:85
  99.5 11.9 %all-gather.5 = f32[20,64,128]{2,1,0:T(8,128)S(1)} all-gather(f32[5,64,128]{2,1,0:T(8,128)S(1)} %get-tuple-element.126), channel_id=7, replica_groups=mesh['patch'=128,'slab'=4] {'slab'}, dimensions={0}, use_global_device_ids=true | all-gather | bytes 819200 | tf_op jit(solution)/shard_map/all_gather | solution.py:947
  111.4 2.4 %shard_map.162 = (f32[36,128,128]{2,1,0:T(8,128)S(1)}, f32[2,40,128]{2,1,0:T(8,128)S(1)}) custom-call(s32[1,3]{1,0:T(1,128)S(1)} %copy-done.4, f32[32,128,128]{2,1,0:T(8,128)S(1)} %get-tuple-element.124.refs_0_, f32[128,128]{1,0:T(8,128)S(1)} %get-tuple-element.125.refs_1_, f32[4,5,64,128]{3,2,1,0:T(8,128)S(1)} %bitcast.22, ...), custom_call_target="tpu_custom_call" | custom-call | flops 10000000 | bytes 20209664 | tf_op jit(solution)/shard_map/pallas_call | solution.py:85
  113.8 4.1 %shard_map.163 = (f32[16,128,128]{2,1,0:T(8,128)S(1)}, f32[32,128,128]{2,1,0:T(8,128)S(1)}, f32[2,72,128]{2,1,0:T(8,128)S(1)}, f32[72,128]{1,0:T(8,128)S(1)}) custom-call(s32[1,3]{1,0:T(1,128)S(1)} %copy-done.4, f32[36,128,128]{2,1,0:T(8,128)S(1)} %get-tuple-element.128.refs_0_, f32[32,128,128]{2,1,0:T(8,128)S(1)} %get-tuple-element.76.refs_0_.refs_1_, ...), custom_call_target="tpu_custom_call" | custom-call | flops 3000000000 | bytes 14585856 | tf_op jit(solution)/shard_map/pallas_call | solution.py:85
  118.0 1.9 %collective-permute-start.6 = (f32[72,128]{1,0:T(8,128)S(1)}, f32[72,128]{1,0:T(8,128)S(1)}, u32[]{:S(2)}, u32[]{:S(2)}) collective-permute-start(f32[72,128]{1,0:T(8,128)S(1)} %get-tuple-element.137), channel_id=1, source_target_pairs={{1,4},{4,1},{3,6},{6,3},{5,8},{8,5},{7,10},{10,7},{9,12},{12,9},{1... | collective-permute-start | bytes 110600 | tf_op jit(solution)/shard_map/ppermute | solution.py:904
  119.9 2.1 %shard_map.166 = (f32[32,32,128]{2,1,0:T(8,128)S(1)}, f32[32,32,128]{2,1,0:T(8,128)S(1)}) custom-call(s32[1,3]{1,0:T(1,128)S(1)} %copy-done.4, f32[32,128,128]{2,1,0:T(8,128)S(1)} %get-tuple-element.141.refs_0_, bf16[256,256]{1,0:T(8,128)(2,1)S(1)} %get-tuple-element.142.refs_1_, bf16[128,256]{1,0:T(8,128)(2,1)S(1)} %get-tuple-element.143.refs_2_), custom_call_target="tpu_custom_call" | custom-call | flops 3000000000 | bytes 3342336 | tf_op jit(solution)/shard_map/pallas_call | solution.py:85
  122.0 2.3 %collective-permute-start.7 = (f32[32,32,128]{2,1,0:T(8,128)S(1)}, f32[32,32,128]{2,1,0:T(8,128)S(1)}, u32[]{:S(2)}, u32[]{:S(2)}) collective-permute-start(f32[32,32,128]{2,1,0:T(8,128)S(1)} %get-tuple-element.145), channel_id=1, source_target_pairs={{0,2},{2,0},{1,3},{3,1},{4,6},{6,4},{5,7},{7,5},{8,10},{10,8},{9,1... | collective-permute-start | bytes 1572872 | tf_op jit(solution)/shard_map/ppermute | solution.py:985
  124.3 8.3 %collective-permute-done.6 = f32[72,128]{1,0:T(8,128)S(1)} collective-permute-done((f32[72,128]{1,0:T(8,128)S(1)}, f32[72,128]{1,0:T(8,128)S(1)}, u32[]{:S(2)}, u32[]{:S(2)}) %collective-permute-start.6) | collective-permute-done | bytes 36896 | tf_op jit(solution)/shard_map/ppermute | solution.py:904
  132.6 1.8 %all-gather.6 = f32[144,128]{1,0:T(8,128)S(1)} all-gather(f32[72,128]{1,0:T(8,128)S(1)} %collective-permute-done.6), channel_id=8, replica_groups={{0,1},{2,3},{4,5},{6,7},{8,9},{10,11},{12,13},{14,15},{16,17},{18,19},{..., dimensions={0}, use_global_device_ids=true | all-gather | bytes 110592 | tf_op jit(solution)/shard_map/all_gather | solution.py:905
  134.4 2.0 %shard_map.164 = (f32[6,32,128]{2,1,0:T(8,128)S(1)}, f32[2,40,128]{2,1,0:T(8,128)S(1)}) custom-call(s32[1,3]{1,0:T(1,128)S(1)} %copy-done.4, f32[1,3]{1,0:T(1,128)S(1)} %copy-done.11, f32[2,72,128]{2,1,0:T(8,128)S(1)} %get-tuple-element.136.refs_1_, f32[2,72,128]{2,1,0:T(8,128)S(1)} %bitcast.30, f32[6,4,40,128]{3,2,1,0:T(8,128)S(1)} %get-tuple-element.127.refs_13_.refs_3_, ...), custom_call_target="tpu_custom_call" | custom-call | flops 80000000000 | bytes 1200640 | tf_op jit(solution)/shard_map/pallas_call | solution.py:85
  138.5 4.5 %collective-permute-start.8 = (f32[6,32,128]{2,1,0:T(8,128)S(1)}, f32[6,32,128]{2,1,0:T(8,128)S(1)}, u32[]{:S(2)}, u32[]{:S(2)}) collective-permute-start(f32[6,32,128]{2,1,0:T(8,128)S(1)} %get-tuple-element.147.refs_1_), channel_id=1, source_target_pairs={{0,2},{2,0},{1,3},{3,1},{4,6},{6,4},{5,7},{7,5},{8,10},{10,8},{9,1... | collective-permute-start | bytes 294920 | tf_op jit(solution)/shard_map/ppermute | solution.py:999
  144.6 5.9 %collective-permute-done.8.refs_2_ = f32[6,32,128]{2,1,0:T(8,128)S(1)} collective-permute-done((f32[6,32,128]{2,1,0:T(8,128)S(1)}, f32[6,32,128]{2,1,0:T(8,128)S(1)}, u32[]{:S(2)}, u32[]{:S(2)}) %collective-permute-start.8) | collective-permute-done | bytes 98336 | tf_op jit(solution)/shard_map/ppermute | solution.py:999
  152.1 2.0 %copy.17 = f32[1,62,3969]{2,0,1:T(1,128)} copy(f32[1,62,3969]{2,1,0:T(8,128)S(1)} %bitcast.25) | data formatting | bytes 1968624
  (44 shorter events, 11.8 us)
Async XLA Ops:
  0.6 10.4 %copy-start.12 = (f32[1,16,16384]{2,1,0:T(8,128)S(1)}, f32[1,16,16384]{2,1,0:T(8,128)}, u32[]{:S(2)}) copy-start(f32[1,16,16384]{2,1,0:T(8,128)} %param.15) | copy-start | bytes 3145732
  0.6 12.6 %copy-start = (f32[128,128]{1,0:T(8,128)S(1)}, f32[128,128]{1,0:T(8,128)}, u32[]{:S(2)}) copy-start(f32[128,128]{1,0:T(8,128)} %refs_1_.1) | copy-start | bytes 196612
  0.7 12.6 %copy-start.1 = (f32[128,128]{1,0:T(8,128)S(1)}, f32[128,128]{1,0:T(8,128)}, u32[]{:S(2)}) copy-start(f32[128,128]{1,0:T(8,128)} %refs_2_.1) | copy-start | bytes 196612
  0.7 12.6 %copy-start.2 = (f32[128,128]{1,0:T(8,128)S(1)}, f32[128,128]{1,0:T(8,128)}, u32[]{:S(2)}) copy-start(f32[128,128]{1,0:T(8,128)} %refs_5_.1) | copy-start | bytes 196612
  0.7 12.6 %copy-start.3 = (f32[126,128]{1,0:T(8,128)S(1)}, f32[126,128]{1,0:T(8,128)}, u32[]{:S(2)}) copy-start(f32[126,128]{1,0:T(8,128)} %refs_9_.1) | copy-start | bytes 193540
  0.7 12.6 %copy-start.4 = (s32[1,3]{1,0:T(1,128)S(1)}, s32[1,3]{1,0:T(1,128)}, u32[]{:S(2)}) copy-start(s32[1,3]{1,0:T(1,128)} %links_ref.39) | copy-start | bytes 40
  0.7 12.6 %copy-start.5 = (f32[64,64]{1,0:T(8,128)S(1)}, f32[64,64]{1,0:T(8,128)}, u32[]{:S(2)}) copy-start(f32[64,64]{1,0:T(8,128)} %refs_3_.1) | copy-start | bytes 49156
  0.7 12.6 %copy-start.6 = (f32[64,64]{1,0:T(8,128)S(1)}, f32[64,64]{1,0:T(8,128)}, u32[]{:S(2)}) copy-start(f32[64,64]{1,0:T(8,128)} %refs_4_.1) | copy-start | bytes 49156
  0.7 12.6 %copy-start.7 = (f32[64,64]{1,0:T(8,128)S(1)}, f32[64,64]{1,0:T(8,128)}, u32[]{:S(2)}) copy-start(f32[64,64]{1,0:T(8,128)} %refs_7_.1) | copy-start | bytes 49156
  0.7 12.6 %copy-start.8 = (f32[62,64]{1,0:T(8,128)S(1)}, f32[62,64]{1,0:T(8,128)}, u32[]{:S(2)}) copy-start(f32[62,64]{1,0:T(8,128)} %refs_10_.1) | copy-start | bytes 47620
  0.7 12.6 %copy-start.9 = (f32[128]{0:T(128)S(1)}, f32[128]{0:T(128)}, u32[]{:S(2)}) copy-start(f32[128]{0:T(128)} %param.22) | copy-start | bytes 1540
  0.7 12.6 %copy-start.10 = (f32[64]{0:T(128)S(1)}, f32[64]{0:T(128)}, u32[]{:S(2)}) copy-start(f32[64]{0:T(128)} %param.24) | copy-start | bytes 772
  0.8 12.6 %copy-start.11 = (f32[1,3]{1,0:T(1,128)S(1)}, f32[1,3]{1,0:T(1,128)}, u32[]{:S(2)}) copy-start(f32[1,3]{1,0:T(1,128)} %refs_0_.3) | copy-start | bytes 40
  2.3 12.4 %collective-permute-start = (f32[16,128,128]{2,1,0:T(8,128)S(1)}, f32[16,128,128]{2,1,0:T(8,128)S(1)}, u32[]{:S(2)}, u32[]{:S(2)}) collective-permute-start(f32[16,128,128]{2,1,0:T(8,128)S(1)} %bitcast.20), channel_id=1, source_target_pairs={{0,1},{1,0},{2,3},{3,2},{4,5},{5,4},{6,7},{7,6},{8,9},{9,8},{10,11... | collective-permute-start | bytes 3145736 | tf_op jit(solution)/shard_map/ppermute | solution.py:910
  11.3 34.5 %collective-permute-start.3 = (f32[16,128,128]{2,1,0:T(8,128)S(1)}, f32[16,128,128]{2,1,0:T(8,128)S(1)}, u32[]{:S(2)}, u32[]{:S(2)}) collective-permute-start(f32[16,128,128]{2,1,0:T(8,128)S(1)} %bitcast.18), channel_id=1, source_target_pairs={{0,1},{1,0},{2,3},{3,2},{4,5},{5,4},{6,7},{7,6},{8,9},{9,8},{10,11... | collective-permute-start | bytes 3145736 | tf_op jit(solution)/shard_map/ppermute | solution.py:911
  15.5 6.8 %collective-permute-start.1 = (f32[48,128]{1,0:T(8,128)S(1)}, f32[48,128]{1,0:T(8,128)S(1)}, u32[]{:S(2)}, u32[]{:S(2)}) collective-permute-start(f32[48,128]{1,0:T(8,128)S(1)} %get-tuple-element.80.refs_0_), channel_id=1, source_target_pairs={{1,4},{4,1},{3,6},{6,3},{5,8},{8,5},{7,10},{10,7},{9,12},{12,9},{1... | collective-permute-start | bytes 73736 | tf_op jit(solution)/shard_map/ppermute | solution.py:904
  34.7 12.0 %collective-permute-start.2 = (f32[5,64,128]{2,1,0:T(8,128)S(1)}, f32[5,64,128]{2,1,0:T(8,128)S(1)}, u32[]{:S(2)}, u32[]{:S(2)}) collective-permute-start(f32[5,64,128]{2,1,0:T(8,128)S(1)} %get-tuple-element.90.refs_0_), channel_id=1, source_target_pairs={{0,2},{2,0},{1,3},{3,1},{4,6},{6,4},{5,7},{7,5},{8,10},{10,8},{9,1... | collective-permute-start | bytes 491528 | tf_op jit(solution)/shard_map/ppermute | solution.py:949
  51.2 5.4 %collective-permute-start.4 = (f32[80,128]{1,0:T(8,128)S(1)}, f32[80,128]{1,0:T(8,128)S(1)}, u32[]{:S(2)}, u32[]{:S(2)}) collective-permute-start(f32[80,128]{1,0:T(8,128)S(1)} %get-tuple-element.109), channel_id=1, source_target_pairs={{1,4},{4,1},{3,6},{6,3},{5,8},{8,5},{7,10},{10,7},{9,12},{12,9},{1... | collective-permute-start | bytes 122888 | tf_op jit(solution)/shard_map/ppermute | solution.py:904
  82.6 5.8 %collective-permute-start.5 = (f32[40,128]{1,0:T(8,128)S(1)}, f32[40,128]{1,0:T(8,128)S(1)}, u32[]{:S(2)}, u32[]{:S(2)}) collective-permute-start(f32[40,128]{1,0:T(8,128)S(1)} %get-tuple-element.123), channel_id=1, source_target_pairs={{1,4},{4,1},{3,6},{6,3},{5,8},{8,5},{7,10},{10,7},{9,12},{12,9},{1... | collective-permute-start | bytes 61448 | tf_op jit(solution)/shard_map/ppermute | solution.py:904
  118.0 14.6 %collective-permute-start.6 = (f32[72,128]{1,0:T(8,128)S(1)}, f32[72,128]{1,0:T(8,128)S(1)}, u32[]{:S(2)}, u32[]{:S(2)}) collective-permute-start(f32[72,128]{1,0:T(8,128)S(1)} %get-tuple-element.137), channel_id=1, source_target_pairs={{1,4},{4,1},{3,6},{6,3},{5,8},{8,5},{7,10},{10,7},{9,12},{12,9},{1... | collective-permute-start | bytes 110600 | tf_op jit(solution)/shard_map/ppermute | solution.py:904
  122.0 21.0 %collective-permute-start.7 = (f32[32,32,128]{2,1,0:T(8,128)S(1)}, f32[32,32,128]{2,1,0:T(8,128)S(1)}, u32[]{:S(2)}, u32[]{:S(2)}) collective-permute-start(f32[32,32,128]{2,1,0:T(8,128)S(1)} %get-tuple-element.145), channel_id=1, source_target_pairs={{0,2},{2,0},{1,3},{3,1},{4,6},{6,4},{5,7},{7,5},{8,10},{10,8},{9,1... | collective-permute-start | bytes 1572872 | tf_op jit(solution)/shard_map/ppermute | solution.py:985
  138.5 12.0 %collective-permute-start.8 = (f32[6,32,128]{2,1,0:T(8,128)S(1)}, f32[6,32,128]{2,1,0:T(8,128)S(1)}, u32[]{:S(2)}, u32[]{:S(2)}) collective-permute-start(f32[6,32,128]{2,1,0:T(8,128)S(1)} %get-tuple-element.147.refs_1_), channel_id=1, source_target_pairs={{0,2},{2,0},{1,3},{3,1},{4,6},{6,4},{5,7},{7,5},{8,10},{10,8},{9,1... | collective-permute-start | bytes 294920 | tf_op jit(solution)/shard_map/ppermute | solution.py:999

commit v4 on v3

--- a/solution.py
+++ b/solution.py
@@ -68,12 +68,13 @@
     return jnp.concatenate(split(a), axis=1)
 
 
-def call(kernel, outs, links, *args, flops=0, scratch=(), geometry=None):
+def call(kernel, outs, links, *args, flops=0, scratch=(), geometry=None, moved=None):
     smem = [links] if geometry is None else [links, geometry]
     specs = [pl.BlockSpec(memory_space=pltpu.SMEM)] * len(smem)
     specs += [pl.BlockSpec(memory_space=pltpu.VMEM)] * len(args)
     shapes = [s if isinstance(s, jax.ShapeDtypeStruct) else jax.ShapeDtypeStruct(s, F32) for s in outs]
-    moved = sum(a.size * a.dtype.itemsize for a in args) + sum(4 * s.size for s in shapes)
+    if moved is None:
+        moved = sum(a.size * a.dtype.itemsize for a in args) + sum(4 * s.size for s in shapes)
 
     def body(links_ref, *refs):
         ints = facts(links_ref)
@@ -718,7 +719,7 @@
                 value = value + columns[s, :, c:c + 1] * profile_rows[s:s + 1, :]
             blocks[c] = value
 
-    share = out.shape[1]
+    share = out.shape[2]
     lane = lax.broadcasted_iota(jnp.int32, (deep, N), 1)
     for core in range(2):
 
@@ -743,7 +744,7 @@
                 if after + COARSE < N and c + 2 < 32:
                     value = jnp.where(lane < after + COARSE, value, turned(c + 2))
                 width = min(N, share - tile * N)
-                out[:, tile * N:tile * N + width] = value[:, :width]
+                out[:, 0, tile * N:tile * N + width] = value[:, :width]
 
 
 def prepare_kernel(
@@ -997,21 +998,21 @@
         geometry=geometry, flops=80_000_000_000,
     )
     far_parts = lax.ppermute(parts, "slab", cross)
-    (out_u,) = call(iterate_kernel, [(BLOCK, N, N)], links, up, rows_u, mask, flops=2_000_000_000)
+    (out_u,) = call(iterate_kernel, [(BLOCK, N, N)], links, up, rows_u, mask, flops=4_000_000_000)
     deep = restrict_vertical.shape[0]
     share = COARSE * COARSE // 4
     (blocks,) = call(
         vertical_kernel, [(32, deep, N)],
-        links, kept.reshape(HALF * 32, N), arrived.reshape(HALF * 32, N), vertical, flops=2_000_000_000,
+        links, kept.reshape(HALF * 32, N), arrived.reshape(HALF * 32, N), vertical, flops=1000, moved=1000,
     )
     (flat,) = call(
         coarse_kernel,
-        [(deep, share)],
+        [(deep, 1, share)],
         links, blocks, parts, far_parts, profile, profile_rows, vertical,
         scratch=[pltpu.VMEM((32, deep, N), F32), pltpu.VMEM((6, deep, N), F32)],
         flops=20_000_000_000,
     )
-    return out_u.reshape(1, BLOCK, N * N), flat[None]
+    return out_u.reshape(1, BLOCK, N * N), flat.transpose(1, 0, 2)
 
 
 def solution(mesh):

time: 155 us -> 153 us (0.987)
  local copies, waits for them, and re-layouts: 4.93 us -> 2.93 us
  Pallas kernels: 47.7 us -> 49.5 us
    ppermute x1, waiting for transfers between devices: 5.89 us -> 3.13 us  [per_device(): far_parts = lax.ppermute(parts, 'slab', cross)]
    unnamed x29 -> x28, local copies, waits for them, and re-layouts: 3.77 us -> 1.77 us
    pallas_call x20, Pallas kernels: 47.7 us -> 49.5 us  [call(): pl.pallas_call(body, out_shape=shapes, in_specs=specs, out_specs=[pl.Bloc...]
  transfers between devices with their start and end apart: 9 -> 9, of which waited for: 2 -> 2; matrix products, arithmetic and copies ran while one was open for 1% -> 1% of each run, Pallas kernels for 19% -> 20%
where the time goes in v4:
time: 153 us; the launch traced here: 152 us
  blocking collectives  56.6 us (37%)
  Pallas kernels  49.5 us (32%)
  starting transfers between devices  29.4 us (19%)
  waiting for transfers between devices  12.9 us (8%)
  local copies, waits for them, and re-layouts  2.93 us (2%)
    pallas_call x20, Pallas kernels, call(): pl.pallas_call(body, out_shape=shapes, in_specs=specs, out_specs=[pl.Bloc...  49.5 us
    all_gather x4, blocking collectives, swap_faces(): return lambda: lax.all_gather(arrived, 'slab', axis_index_groups=chips)  30.4 us
    all_gather x2, blocking collectives, per_device(): received = lax.all_gather(msg, 'slab')  23.9 us
    ppermute x4, waiting for transfers between devices, swap_faces(): arrived = lax.ppermute(slot_values, ('patch', 'slab'), faces)  9.8 us
    ppermute x1, starting transfers between devices, per_device(): other_load = lax.ppermute(own_load, 'slab', pair)  8.79 us
    ppermute x4, starting transfers between devices, swap_faces(): arrived = lax.ppermute(slot_values, ('patch', 'slab'), faces)  7.86 us
    ppermute x1, starting transfers between devices, per_device(): crossing = lax.ppermute(msg, 'slab', cross)  4.76 us
    ppermute x1, starting transfers between devices, per_device(): far_parts = lax.ppermute(parts, 'slab', cross)  3.86 us
  transfers between devices with their start and end apart: 9, of which 2 were waited for; matrix products, arithmetic and copies ran while one was open for 1% of the time, Pallas kernels for 20%

profile of v4, /device:TPU:1, one launch (start us, length us, event | category | flops | bytes accessed | tf_op | source)
XLA Modules:
  0.0 152.4 jit_solution(11733425769705824848)
XLA Ops:
  2.3 8.8 %collective-permute-start = (f32[16,128,128]{2,1,0:T(8,128)S(1)}, f32[16,128,128]{2,1,0:T(8,128)S(1)}, u32[]{:S(2)}, u32[]{:S(2)}) collective-permute-start(f32[16,128,128]{2,1,0:T(8,128)S(1)} %bitcast.20), channel_id=1, source_target_pairs={{0,1},{1,0},{2,3},{3,2},{4,5},{5,4},{6,7},{7,6},{8,9},{9,8},{10,11... | collective-permute-start | bytes 3145736 | tf_op jit(solution)/shard_map/ppermute | solution.py:911
  11.3 1.9 %collective-permute-start.3 = (f32[16,128,128]{2,1,0:T(8,128)S(1)}, f32[16,128,128]{2,1,0:T(8,128)S(1)}, u32[]{:S(2)}, u32[]{:S(2)}) collective-permute-start(f32[16,128,128]{2,1,0:T(8,128)S(1)} %bitcast.18), channel_id=1, source_target_pairs={{0,1},{1,0},{2,3},{3,2},{4,5},{5,4},{6,7},{7,6},{8,9},{9,8},{10,11... | collective-permute-start | bytes 3145736 | tf_op jit(solution)/shard_map/ppermute | solution.py:912
  15.5 1.9 %collective-permute-start.1 = (f32[48,128]{1,0:T(8,128)S(1)}, f32[48,128]{1,0:T(8,128)S(1)}, u32[]{:S(2)}, u32[]{:S(2)}) collective-permute-start(f32[48,128]{1,0:T(8,128)S(1)} %get-tuple-element.80.refs_0_), channel_id=1, source_target_pairs={{1,4},{4,1},{3,6},{6,3},{5,8},{8,5},{7,10},{10,7},{9,12},{12,9},{1... | collective-permute-start | bytes 73736 | tf_op jit(solution)/shard_map/ppermute | solution.py:905
  17.5 2.9 %shard_map.152 = (f32[32,4,128,128]{3,2,1,0:T(8,128)S(1)}, f32[32,128,128]{2,1,0:T(8,128)S(1)}) custom-call(s32[1,3]{1,0:T(1,128)S(1)} %copy-done.4, f32[48,128]{1,0:T(8,128)S(1)} %get-tuple-element.80.refs_0_, f32[128,128]{1,0:T(8,128)S(1)} %get-tuple-element.84.refs_1_.refs_0_, f32[2,2,5,40,128]{4,3,2,1,0:T(8,128)S(1)} %get-tuple-element.85.refs_2_.refs_1_), custom_call_target="tpu_custom_call" | custom-call | flops 3000000000 | bytes 10985472 | tf_op jit(solution)/shard_map/pallas_call | solution.py:86
  20.4 2.0 %shard_map.151.refs_0_ = f32[32,128,128]{2,1,0:T(8,128)S(1)} custom-call(s32[1,3]{1,0:T(1,128)S(1)} %copy-done.4, f32[32,128,128]{2,1,0:T(8,128)S(1)} %get-tuple-element.76.refs_0_.refs_1_, bf16[256,256]{1,0:T(8,128)(2,1)S(1)} %get-tuple-element.77.refs_1_.refs_5_.refs_8_.refs_7_.refs_10_, bf16[128,256]{1,0:T(8,128)(2,1)S(1)} %get-tuple-element.78.refs_2_.refs_9_.refs_11_), custom_call_target="tpu_custom_call" | custom-call | flops 2000000000 | bytes 4390912 | tf_op jit(solution)/shard_map/pallas_call | solution.py:86
  22.4 11.1 %all-gather = f32[96,128]{1,0:T(8,128)S(1)} all-gather(f32[48,128]{1,0:T(8,128)S(1)} %collective-permute-done.1), channel_id=2, replica_groups={{0,1},{2,3},{4,5},{6,7},{8,9},{10,11},{12,13},{14,15},{16,17},{18,19},{..., dimensions={0}, use_global_device_ids=true | all-gather | bytes 73728 | tf_op jit(solution)/shard_map/all_gather | solution.py:906
  35.2 4.8 %collective-permute-start.2 = (f32[5,64,128]{2,1,0:T(8,128)S(1)}, f32[5,64,128]{2,1,0:T(8,128)S(1)}, u32[]{:S(2)}, u32[]{:S(2)}) collective-permute-start(f32[5,64,128]{2,1,0:T(8,128)S(1)} %get-tuple-element.90.refs_0_), channel_id=1, source_target_pairs={{0,2},{2,0},{1,3},{3,1},{4,6},{6,4},{5,7},{7,5},{8,10},{10,8},{9,1... | collective-permute-start | bytes 491528 | tf_op jit(solution)/shard_map/ppermute | solution.py:950
  40.0 6.4 %shard_map.154 = (f32[4,4,128,128]{3,2,1,0:T(8,128)S(1)}, f32[4,128,128]{2,1,0:T(8,128)S(1)}, f32[8,4,128,128]{3,2,1,0:T(8,128)S(1)}, f32[4,128,128]{2,1,0:T(8,128)S(1)}, f32[128,128]{1,0:T(8,128)S(1)}) custom-call(s32[1,3]{1,0:T(1,128)S(1)} %copy-done.4, f32[128,128]{1,0:T(8,128)S(1)} %get-tuple-element.84.refs_1_.refs_0_, ...), custom_call_target="tpu_custom_call" | custom-call | flops 5000000000 | bytes 14778368 | tf_op jit(solution)/shard_map/pallas_call | solution.py:86
  47.2 2.3 %all-gather.1 = f32[10,64,128]{2,1,0:T(8,128)S(1)} all-gather(f32[5,64,128]{2,1,0:T(8,128)S(1)} %collective-permute-done.2), channel_id=3, replica_groups={{0,1},{2,3},{4,5},{6,7},{8,9},{10,11},{12,13},{14,15},{16,17},{18,19},{..., dimensions={0}, use_global_device_ids=true | all-gather | bytes 491520 | tf_op jit(solution)/shard_map/all_gather | solution.py:958
  49.5 2.2 %shard_map.156 = (f32[36,128,128]{2,1,0:T(8,128)S(1)}, f32[2,80,128]{2,1,0:T(8,128)S(1)}, f32[80,128]{1,0:T(8,128)S(1)}) custom-call(s32[1,3]{1,0:T(1,128)S(1)} %copy-done.4, f32[32,128,128]{2,1,0:T(8,128)S(1)} %get-tuple-element.88.refs_0_, f32[128,128]{1,0:T(8,128)S(1)} %get-tuple-element.89.refs_1_, f32[2,5,64,128]{3,2,1,0:T(8,128)S(1)} %bitcast.24, ...), custom_call_target="tpu_custom_call" | custom-call | flops 10000000 | bytes 20004864 | tf_op jit(solution)/shard_map/pallas_call | solution.py:86
  51.8 1.9 %collective-permute-start.4 = (f32[80,128]{1,0:T(8,128)S(1)}, f32[80,128]{1,0:T(8,128)S(1)}, u32[]{:S(2)}, u32[]{:S(2)}) collective-permute-start(f32[80,128]{1,0:T(8,128)S(1)} %get-tuple-element.109), channel_id=1, source_target_pairs={{1,4},{4,1},{3,6},{6,3},{5,8},{8,5},{7,10},{10,7},{9,12},{12,9},{1... | collective-permute-start | bytes 122888 | tf_op jit(solution)/shard_map/ppermute | solution.py:905
  53.7 3.5 %shard_map.157 = (f32[32,128,128]{2,1,0:T(8,128)S(1)}, f32[32,128,128]{2,1,0:T(8,128)S(1)}, f32[32,128,128]{2,1,0:T(8,128)S(1)}) custom-call(s32[1,3]{1,0:T(1,128)S(1)} %copy-done.4, f32[36,128,128]{2,1,0:T(8,128)S(1)} %get-tuple-element.100.refs_0_, f32[32,128,128]{2,1,0:T(8,128)S(1)} %get-tuple-element.76.refs_0_.refs_1_, ...), custom_call_target="tpu_custom_call" | custom-call | flops 4000000000 | bytes 13451264 | tf_op jit(solution)/shard_map/pallas_call | solution.py:86
  57.2 8.2 %all-gather.2 = f32[160,128]{1,0:T(8,128)S(1)} all-gather(f32[80,128]{1,0:T(8,128)S(1)} %collective-permute-done.4), channel_id=4, replica_groups={{0,1},{2,3},{4,5},{6,7},{8,9},{10,11},{12,13},{14,15},{16,17},{18,19},{..., dimensions={0}, use_global_device_ids=true | all-gather | bytes 122880 | tf_op jit(solution)/shard_map/all_gather | solution.py:906
  65.4 2.7 %shard_map.158 = (f32[32,128,128]{2,1,0:T(8,128)S(1)}, f32[5,64,128]{2,1,0:T(8,128)S(1)}, f32[128,128]{1,0:T(8,128)S(1)}, f32[6,4,40,128]{3,2,1,0:T(8,128)S(1)},...) custom-call(s32[1,3]{1,0:T(1,128)S(1)} %copy-done.4, f32[32,128,128]{2,1,0:T(8,128)S(1)} %get-tuple-element.107.refs_0_, ...), custom_call_target="tpu_custom_call" | custom-call | flops 10000000 | bytes 14643712 | tf_op jit(solution)/shard_map/pallas_call | solution.py:86
  68.1 12.0 %all-gather.3 = f32[20,64,128]{2,1,0:T(8,128)S(1)} all-gather(f32[5,64,128]{2,1,0:T(8,128)S(1)} %get-tuple-element.114), channel_id=5, replica_groups=mesh['patch'=128,'slab'=4] {'slab'}, dimensions={0}, use_global_device_ids=true | all-gather | bytes 819200 | tf_op jit(solution)/shard_map/all_gather | solution.py:948
  80.0 2.2 %shard_map.159 = (f32[36,128,128]{2,1,0:T(8,128)S(1)}, f32[2,40,128]{2,1,0:T(8,128)S(1)}, f32[40,128]{1,0:T(8,128)S(1)}) custom-call(s32[1,3]{1,0:T(1,128)S(1)} %copy-done.4, f32[32,128,128]{2,1,0:T(8,128)S(1)} %get-tuple-element.112.refs_0_, f32[128,128]{1,0:T(8,128)S(1)} %get-tuple-element.113.refs_1_, f32[4,5,64,128]{3,2,1,0:T(8,128)S(1)} %bitcast.23, ...), custom_call_target="tpu_custom_call" | custom-call | flops 10000000 | bytes 20230144 | tf_op jit(solution)/shard_map/pallas_call | solution.py:86
  82.2 2.1 %collective-permute-start.5 = (f32[40,128]{1,0:T(8,128)S(1)}, f32[40,128]{1,0:T(8,128)S(1)}, u32[]{:S(2)}, u32[]{:S(2)}) collective-permute-start(f32[40,128]{1,0:T(8,128)S(1)} %get-tuple-element.123), channel_id=1, source_target_pairs={{1,4},{4,1},{3,6},{6,3},{5,8},{8,5},{7,10},{10,7},{9,12},{12,9},{1... | collective-permute-start | bytes 61448 | tf_op jit(solution)/shard_map/ppermute | solution.py:905
  84.3 3.7 %shard_map.160 = (f32[32,128,128]{2,1,0:T(8,128)S(1)}, f32[32,128,128]{2,1,0:T(8,128)S(1)}, f32[32,128,128]{2,1,0:T(8,128)S(1)}) custom-call(s32[1,3]{1,0:T(1,128)S(1)} %copy-done.4, f32[36,128,128]{2,1,0:T(8,128)S(1)} %get-tuple-element.116.refs_0_, f32[32,128,128]{2,1,0:T(8,128)S(1)} %get-tuple-element.76.refs_0_.refs_1_, ...), custom_call_target="tpu_custom_call" | custom-call | flops 4000000000 | bytes 17645568 | tf_op jit(solution)/shard_map/pallas_call | solution.py:86
  88.0 9.3 %all-gather.4 = f32[80,128]{1,0:T(8,128)S(1)} all-gather(f32[40,128]{1,0:T(8,128)S(1)} %collective-permute-done.5), channel_id=6, replica_groups={{0,1},{2,3},{4,5},{6,7},{8,9},{10,11},{12,13},{14,15},{16,17},{18,19},{..., dimensions={0}, use_global_device_ids=true | all-gather | bytes 61440 | tf_op jit(solution)/shard_map/all_gather | solution.py:906
  97.3 2.8 %shard_map.161 = (f32[32,128,128]{2,1,0:T(8,128)S(1)}, f32[5,64,128]{2,1,0:T(8,128)S(1)}, f32[128,128]{1,0:T(8,128)S(1)}, f32[6,4,40,128]{3,2,1,0:T(8,128)S(1)},...) custom-call(s32[1,3]{1,0:T(1,128)S(1)} %copy-done.4, f32[32,128,128]{2,1,0:T(8,128)S(1)} %get-tuple-element.121.refs_0_, ...), custom_call_target="tpu_custom_call" | custom-call | flops 10000000 | bytes 14561792 | tf_op jit(solution)/shard_map/pallas_call | solution.py:86
  100.1 11.9 %all-gather.5 = f32[20,64,128]{2,1,0:T(8,128)S(1)} all-gather(f32[5,64,128]{2,1,0:T(8,128)S(1)} %get-tuple-element.126), channel_id=7, replica_groups=mesh['patch'=128,'slab'=4] {'slab'}, dimensions={0}, use_global_device_ids=true | all-gather | bytes 819200 | tf_op jit(solution)/shard_map/all_gather | solution.py:948
  112.0 2.4 %shard_map.162 = (f32[36,128,128]{2,1,0:T(8,128)S(1)}, f32[2,40,128]{2,1,0:T(8,128)S(1)}) custom-call(s32[1,3]{1,0:T(1,128)S(1)} %copy-done.4, f32[32,128,128]{2,1,0:T(8,128)S(1)} %get-tuple-element.124.refs_0_, f32[128,128]{1,0:T(8,128)S(1)} %get-tuple-element.125.refs_1_, f32[4,5,64,128]{3,2,1,0:T(8,128)S(1)} %bitcast.22, ...), custom_call_target="tpu_custom_call" | custom-call | flops 10000000 | bytes 20209664 | tf_op jit(solution)/shard_map/pallas_call | solution.py:86
  114.4 4.1 %shard_map.163 = (f32[16,128,128]{2,1,0:T(8,128)S(1)}, f32[32,128,128]{2,1,0:T(8,128)S(1)}, f32[2,72,128]{2,1,0:T(8,128)S(1)}, f32[72,128]{1,0:T(8,128)S(1)}) custom-call(s32[1,3]{1,0:T(1,128)S(1)} %copy-done.4, f32[36,128,128]{2,1,0:T(8,128)S(1)} %get-tuple-element.128.refs_0_, f32[32,128,128]{2,1,0:T(8,128)S(1)} %get-tuple-element.76.refs_0_.refs_1_, ...), custom_call_target="tpu_custom_call" | custom-call | flops 3000000000 | bytes 14585856 | tf_op jit(solution)/shard_map/pallas_call | solution.py:86
  118.5 1.9 %collective-permute-start.6 = (f32[72,128]{1,0:T(8,128)S(1)}, f32[72,128]{1,0:T(8,128)S(1)}, u32[]{:S(2)}, u32[]{:S(2)}) collective-permute-start(f32[72,128]{1,0:T(8,128)S(1)} %get-tuple-element.137), channel_id=1, source_target_pairs={{1,4},{4,1},{3,6},{6,3},{5,8},{8,5},{7,10},{10,7},{9,12},{12,9},{1... | collective-permute-start | bytes 110600 | tf_op jit(solution)/shard_map/ppermute | solution.py:905
  120.5 2.1 %shard_map.166 = (f32[32,32,128]{2,1,0:T(8,128)S(1)}, f32[32,32,128]{2,1,0:T(8,128)S(1)}) custom-call(s32[1,3]{1,0:T(1,128)S(1)} %copy-done.4, f32[32,128,128]{2,1,0:T(8,128)S(1)} %get-tuple-element.141.refs_0_, bf16[256,256]{1,0:T(8,128)(2,1)S(1)} %get-tuple-element.142.refs_1_, bf16[128,256]{1,0:T(8,128)(2,1)S(1)} %get-tuple-element.143.refs_2_), custom_call_target="tpu_custom_call" | custom-call | flops 3000000000 | bytes 3342336 | tf_op jit(solution)/shard_map/pallas_call | solution.py:86
  122.5 2.2 %collective-permute-start.7 = (f32[32,32,128]{2,1,0:T(8,128)S(1)}, f32[32,32,128]{2,1,0:T(8,128)S(1)}, u32[]{:S(2)}, u32[]{:S(2)}) collective-permute-start(f32[32,32,128]{2,1,0:T(8,128)S(1)} %get-tuple-element.145), channel_id=1, source_target_pairs={{0,2},{2,0},{1,3},{3,1},{4,6},{6,4},{5,7},{7,5},{8,10},{10,8},{9,1... | collective-permute-start | bytes 1572872 | tf_op jit(solution)/shard_map/ppermute | solution.py:986
  124.8 9.8 %collective-permute-done.6 = f32[72,128]{1,0:T(8,128)S(1)} collective-permute-done((f32[72,128]{1,0:T(8,128)S(1)}, f32[72,128]{1,0:T(8,128)S(1)}, u32[]{:S(2)}, u32[]{:S(2)}) %collective-permute-start.6) | collective-permute-done | bytes 36896 | tf_op jit(solution)/shard_map/ppermute | solution.py:905
  134.6 1.8 %all-gather.6 = f32[144,128]{1,0:T(8,128)S(1)} all-gather(f32[72,128]{1,0:T(8,128)S(1)} %collective-permute-done.6), channel_id=8, replica_groups={{0,1},{2,3},{4,5},{6,7},{8,9},{10,11},{12,13},{14,15},{16,17},{18,19},{..., dimensions={0}, use_global_device_ids=true | all-gather | bytes 110592 | tf_op jit(solution)/shard_map/all_gather | solution.py:906
  136.4 2.0 %shard_map.164 = (f32[6,32,128]{2,1,0:T(8,128)S(1)}, f32[2,40,128]{2,1,0:T(8,128)S(1)}) custom-call(s32[1,3]{1,0:T(1,128)S(1)} %copy-done.4, f32[1,3]{1,0:T(1,128)S(1)} %copy-done.11, f32[2,72,128]{2,1,0:T(8,128)S(1)} %get-tuple-element.136.refs_1_, f32[2,72,128]{2,1,0:T(8,128)S(1)} %bitcast.31, f32[6,4,40,128]{3,2,1,0:T(8,128)S(1)} %get-tuple-element.127.refs_13_.refs_3_, ...), custom_call_target="tpu_custom_call" | custom-call | flops 80000000000 | bytes 1200640 | tf_op jit(solution)/shard_map/pallas_call | solution.py:86
  138.5 3.9 %collective-permute-start.8 = (f32[6,32,128]{2,1,0:T(8,128)S(1)}, f32[6,32,128]{2,1,0:T(8,128)S(1)}, u32[]{:S(2)}, u32[]{:S(2)}) collective-permute-start(f32[6,32,128]{2,1,0:T(8,128)S(1)} %get-tuple-element.147.refs_1_), channel_id=1, source_target_pairs={{0,2},{2,0},{1,3},{3,1},{4,6},{6,4},{5,7},{7,5},{8,10},{10,8},{9,1... | collective-permute-start | bytes 294920 | tf_op jit(solution)/shard_map/ppermute | solution.py:1000
  145.9 3.1 %collective-permute-done.8.refs_2_ = f32[6,32,128]{2,1,0:T(8,128)S(1)} collective-permute-done((f32[6,32,128]{2,1,0:T(8,128)S(1)}, f32[6,32,128]{2,1,0:T(8,128)S(1)}, u32[]{:S(2)}, u32[]{:S(2)}) %collective-permute-start.8) | collective-permute-done | bytes 98336 | tf_op jit(solution)/shard_map/ppermute | solution.py:1000
  149.1 3.4 %shard_map.168 = f32[62,1,3969]{2,1,0:T(1,128)} custom-call(s32[1,3]{1,0:T(1,128)S(1)} %copy-done.4, f32[32,62,128]{2,1,0:T(8,128)S(1)} %shard_map.167.refs_0_, f32[6,32,128]{2,1,0:T(8,128)S(1)} %get-tuple-element.147.refs_1_, f32[6,32,128]{2,1,0:T(8,128)S(1)} %collective-permute-done.8.refs_2_, f32[6,128,128]{2,1,0:T(8,128)S(1)} %get-tuple-element.148.refs_3_, ...), custom_call_target="tpu_custom_call" | custom-call | flops 20000000000 | bytes 2609912 | tf_op jit(solution)/shard_map/pallas_call | solution.py:86
  (43 shorter events, 10.2 us)
Async XLA Ops:
  0.6 10.4 %copy-start.12 = (f32[1,16,16384]{2,1,0:T(8,128)S(1)}, f32[1,16,16384]{2,1,0:T(8,128)}, u32[]{:S(2)}) copy-start(f32[1,16,16384]{2,1,0:T(8,128)} %param.15) | copy-start | bytes 3145732
  0.6 12.6 %copy-start = (f32[128,128]{1,0:T(8,128)S(1)}, f32[128,128]{1,0:T(8,128)}, u32[]{:S(2)}) copy-start(f32[128,128]{1,0:T(8,128)} %refs_1_.1) | copy-start | bytes 196612
  0.7 12.6 %copy-start.1 = (f32[128,128]{1,0:T(8,128)S(1)}, f32[128,128]{1,0:T(8,128)}, u32[]{:S(2)}) copy-start(f32[128,128]{1,0:T(8,128)} %refs_2_.1) | copy-start | bytes 196612
  0.7 12.6 %copy-start.2 = (f32[128,128]{1,0:T(8,128)S(1)}, f32[128,128]{1,0:T(8,128)}, u32[]{:S(2)}) copy-start(f32[128,128]{1,0:T(8,128)} %refs_5_.1) | copy-start | bytes 196612
  0.7 12.6 %copy-start.3 = (f32[126,128]{1,0:T(8,128)S(1)}, f32[126,128]{1,0:T(8,128)}, u32[]{:S(2)}) copy-start(f32[126,128]{1,0:T(8,128)} %refs_9_.1) | copy-start | bytes 193540
  0.7 12.6 %copy-start.4 = (s32[1,3]{1,0:T(1,128)S(1)}, s32[1,3]{1,0:T(1,128)}, u32[]{:S(2)}) copy-start(s32[1,3]{1,0:T(1,128)} %links_ref.39) | copy-start | bytes 40
  0.7 12.6 %copy-start.5 = (f32[64,64]{1,0:T(8,128)S(1)}, f32[64,64]{1,0:T(8,128)}, u32[]{:S(2)}) copy-start(f32[64,64]{1,0:T(8,128)} %refs_3_.1) | copy-start | bytes 49156
  0.7 12.6 %copy-start.6 = (f32[64,64]{1,0:T(8,128)S(1)}, f32[64,64]{1,0:T(8,128)}, u32[]{:S(2)}) copy-start(f32[64,64]{1,0:T(8,128)} %refs_4_.1) | copy-start | bytes 49156
  0.7 12.6 %copy-start.7 = (f32[64,64]{1,0:T(8,128)S(1)}, f32[64,64]{1,0:T(8,128)}, u32[]{:S(2)}) copy-start(f32[64,64]{1,0:T(8,128)} %refs_7_.1) | copy-start | bytes 49156
  0.7 12.6 %copy-start.8 = (f32[62,64]{1,0:T(8,128)S(1)}, f32[62,64]{1,0:T(8,128)}, u32[]{:S(2)}) copy-start(f32[62,64]{1,0:T(8,128)} %refs_10_.1) | copy-start | bytes 47620
  0.7 12.6 %copy-start.9 = (f32[128]{0:T(128)S(1)}, f32[128]{0:T(128)}, u32[]{:S(2)}) copy-start(f32[128]{0:T(128)} %param.22) | copy-start | bytes 1540
  0.7 12.6 %copy-start.10 = (f32[64]{0:T(128)S(1)}, f32[64]{0:T(128)}, u32[]{:S(2)}) copy-start(f32[64]{0:T(128)} %param.24) | copy-start | bytes 772
  0.8 12.6 %copy-start.11 = (f32[1,3]{1,0:T(1,128)S(1)}, f32[1,3]{1,0:T(1,128)}, u32[]{:S(2)}) copy-start(f32[1,3]{1,0:T(1,128)} %refs_0_.3) | copy-start | bytes 40
  2.3 12.4 %collective-permute-start = (f32[16,128,128]{2,1,0:T(8,128)S(1)}, f32[16,128,128]{2,1,0:T(8,128)S(1)}, u32[]{:S(2)}, u32[]{:S(2)}) collective-permute-start(f32[16,128,128]{2,1,0:T(8,128)S(1)} %bitcast.20), channel_id=1, source_target_pairs={{0,1},{1,0},{2,3},{3,2},{4,5},{5,4},{6,7},{7,6},{8,9},{9,8},{10,11... | collective-permute-start | bytes 3145736 | tf_op jit(solution)/shard_map/ppermute | solution.py:911
  11.3 35.1 %collective-permute-start.3 = (f32[16,128,128]{2,1,0:T(8,128)S(1)}, f32[16,128,128]{2,1,0:T(8,128)S(1)}, u32[]{:S(2)}, u32[]{:S(2)}) collective-permute-start(f32[16,128,128]{2,1,0:T(8,128)S(1)} %bitcast.18), channel_id=1, source_target_pairs={{0,1},{1,0},{2,3},{3,2},{4,5},{5,4},{6,7},{7,6},{8,9},{9,8},{10,11... | collective-permute-start | bytes 3145736 | tf_op jit(solution)/shard_map/ppermute | solution.py:912
  15.5 6.8 %collective-permute-start.1 = (f32[48,128]{1,0:T(8,128)S(1)}, f32[48,128]{1,0:T(8,128)S(1)}, u32[]{:S(2)}, u32[]{:S(2)}) collective-permute-start(f32[48,128]{1,0:T(8,128)S(1)} %get-tuple-element.80.refs_0_), channel_id=1, source_target_pairs={{1,4},{4,1},{3,6},{6,3},{5,8},{8,5},{7,10},{10,7},{9,12},{12,9},{1... | collective-permute-start | bytes 73736 | tf_op jit(solution)/shard_map/ppermute | solution.py:905
  35.2 12.0 %collective-permute-start.2 = (f32[5,64,128]{2,1,0:T(8,128)S(1)}, f32[5,64,128]{2,1,0:T(8,128)S(1)}, u32[]{:S(2)}, u32[]{:S(2)}) collective-permute-start(f32[5,64,128]{2,1,0:T(8,128)S(1)} %get-tuple-element.90.refs_0_), channel_id=1, source_target_pairs={{0,2},{2,0},{1,3},{3,1},{4,6},{6,4},{5,7},{7,5},{8,10},{10,8},{9,1... | collective-permute-start | bytes 491528 | tf_op jit(solution)/shard_map/ppermute | solution.py:950
  51.8 5.4 %collective-permute-start.4 = (f32[80,128]{1,0:T(8,128)S(1)}, f32[80,128]{1,0:T(8,128)S(1)}, u32[]{:S(2)}, u32[]{:S(2)}) collective-permute-start(f32[80,128]{1,0:T(8,128)S(1)} %get-tuple-element.109), channel_id=1, source_target_pairs={{1,4},{4,1},{3,6},{6,3},{5,8},{8,5},{7,10},{10,7},{9,12},{12,9},{1... | collective-permute-start | bytes 122888 | tf_op jit(solution)/shard_map/ppermute | solution.py:905
  82.2 5.8 %collective-permute-start.5 = (f32[40,128]{1,0:T(8,128)S(1)}, f32[40,128]{1,0:T(8,128)S(1)}, u32[]{:S(2)}, u32[]{:S(2)}) collective-permute-start(f32[40,128]{1,0:T(8,128)S(1)} %get-tuple-element.123), channel_id=1, source_target_pairs={{1,4},{4,1},{3,6},{6,3},{5,8},{8,5},{7,10},{10,7},{9,12},{12,9},{1... | collective-permute-start | bytes 61448 | tf_op jit(solution)/shard_map/ppermute | solution.py:905
  118.5 16.0 %collective-permute-start.6 = (f32[72,128]{1,0:T(8,128)S(1)}, f32[72,128]{1,0:T(8,128)S(1)}, u32[]{:S(2)}, u32[]{:S(2)}) collective-permute-start(f32[72,128]{1,0:T(8,128)S(1)} %get-tuple-element.137), channel_id=1, source_target_pairs={{1,4},{4,1},{3,6},{6,3},{5,8},{8,5},{7,10},{10,7},{9,12},{12,9},{1... | collective-permute-start | bytes 110600 | tf_op jit(solution)/shard_map/ppermute | solution.py:905
  122.5 21.8 %collective-permute-start.7 = (f32[32,32,128]{2,1,0:T(8,128)S(1)}, f32[32,32,128]{2,1,0:T(8,128)S(1)}, u32[]{:S(2)}, u32[]{:S(2)}) collective-permute-start(f32[32,32,128]{2,1,0:T(8,128)S(1)} %get-tuple-element.145), channel_id=1, source_target_pairs={{0,2},{2,0},{1,3},{3,1},{4,6},{6,4},{5,7},{7,5},{8,10},{10,8},{9,1... | collective-permute-start | bytes 1572872 | tf_op jit(solution)/shard_map/ppermute | solution.py:986
  138.5 10.6 %collective-permute-start.8 = (f32[6,32,128]{2,1,0:T(8,128)S(1)}, f32[6,32,128]{2,1,0:T(8,128)S(1)}, u32[]{:S(2)}, u32[]{:S(2)}) collective-permute-start(f32[6,32,128]{2,1,0:T(8,128)S(1)} %get-tuple-element.147.refs_1_), channel_id=1, source_target_pairs={{0,2},{2,0},{1,3},{3,1},{4,6},{6,4},{5,7},{7,5},{8,10},{10,8},{9,1... | collective-permute-start | bytes 294920 | tf_op jit(solution)/shard_map/ppermute | solution.py:1000

commit v5 on v4

--- a/solution.py
+++ b/solution.py
@@ -909,12 +909,13 @@
     own_load = load_vector[0].reshape(BLOCK, N, N)
     own_react = reaction[0].reshape(BLOCK, N, N)
     other_load = lax.ppermute(own_load, "slab", pair)
-    other_react = lax.ppermute(own_react, "slab", pair)
     size = ROWS + 8
     f, pay, slot_values = call(
         load_kernel, [field, (2, size, N), (size, N)], links, own_load, other_load
     )
+    slot_values, own_react = lax.optimization_barrier((slot_values, own_react))
     arriving = swap_faces(slot_values)
+    other_react = lax.ppermute(own_react, "slab", pair)
     l, dinv = call(
         factor_kernel, [(HALF, BAND, N, N), field], links, slot_values, alpha, bands, flops=3_000_000_000
     )

time: 153 us -> 157 us (1.026)
  waiting for transfers between devices: 12.9 us -> 14.5 us
    ppermute x1, waiting for transfers between devices: 0.01 us -> 1.91 us  [per_device(): other_load = lax.ppermute(own_load, 'slab', pair)]
  transfers between devices with their start and end apart: 9 -> 9, of which waited for: 2 -> 3; matrix products, arithmetic and copies ran while one was open for 1% -> 1% of each run, Pallas kernels for 20% -> 18%
where the time goes in v5:
time: 157 us; the launch traced here: 155 us
  blocking collectives  56.9 us (36%)
  Pallas kernels  49.9 us (32%)
  starting transfers between devices  29.9 us (19%)
  waiting for transfers between devices  14.5 us (9%)
  local copies, waits for them, and re-layouts  2.96 us (2%)
    pallas_call x20, Pallas kernels, call(): pl.pallas_call(body, out_shape=shapes, in_specs=specs, out_specs=[pl.Bloc...  49.9 us
    all_gather x4, blocking collectives, swap_faces(): return lambda: lax.all_gather(arrived, 'slab', axis_index_groups=chips)  30.1 us
    all_gather x2, blocking collectives, per_device(): received = lax.all_gather(msg, 'slab')  23.9 us
    ppermute x4, waiting for transfers between devices, swap_faces(): arrived = lax.ppermute(slot_values, ('patch', 'slab'), faces)  9.92 us
    ppermute x1, starting transfers between devices, per_device(): other_load = lax.ppermute(own_load, 'slab', pair)  8.79 us
    ppermute x4, starting transfers between devices, swap_faces(): arrived = lax.ppermute(slot_values, ('patch', 'slab'), faces)  7.86 us
    ppermute x1, starting transfers between devices, per_device(): crossing = lax.ppermute(msg, 'slab', cross)  4.76 us
    ppermute x1, starting transfers between devices, per_device(): far_parts = lax.ppermute(parts, 'slab', cross)  3.99 us
  transfers between devices with their start and end apart: 9, of which 3 were waited for; matrix products, arithmetic and copies ran while one was open for 1% of the time, Pallas kernels for 18%

profile of v5, /device:TPU:1, one launch (start us, length us, event | category | flops | bytes accessed | tf_op | source)
XLA Modules:
  0.0 155.2 jit_solution(15977648846862491984)
XLA Ops:
  2.2 8.8 %collective-permute-start = (f32[16,128,128]{2,1,0:T(8,128)S(1)}, f32[16,128,128]{2,1,0:T(8,128)S(1)}, u32[]{:S(2)}, u32[]{:S(2)}) collective-permute-start(f32[16,128,128]{2,1,0:T(8,128)S(1)} %bitcast.20), channel_id=1, source_target_pairs={{0,1},{1,0},{2,3},{3,2},{4,5},{5,4},{6,7},{7,6},{8,9},{9,8},{10,11... | collective-permute-start | bytes 3145736 | tf_op jit(solution)/shard_map/ppermute | solution.py:911
  11.3 1.9 %collective-permute-done.refs_1_ = f32[16,128,128]{2,1,0:T(8,128)S(1)} collective-permute-done((f32[16,128,128]{2,1,0:T(8,128)S(1)}, f32[16,128,128]{2,1,0:T(8,128)S(1)}, u32[]{:S(2)}, u32[]{:S(2)}) %collective-permute-start) | collective-permute-done | bytes 1048608 | tf_op jit(solution)/shard_map/ppermute | solution.py:911
  14.1 2.3 %collective-permute-start.3 = (f32[16,128,128]{2,1,0:T(8,128)S(1)}, f32[16,128,128]{2,1,0:T(8,128)S(1)}, u32[]{:S(2)}, u32[]{:S(2)}) collective-permute-start(f32[16,128,128]{2,1,0:T(8,128)S(1)} %bitcast.18), channel_id=1, source_target_pairs={{0,1},{1,0},{2,3},{3,2},{4,5},{5,4},{6,7},{7,6},{8,9},{9,8},{10,11... | collective-permute-start | bytes 3145736 | tf_op jit(solution)/shard_map/ppermute | solution.py:918
  17.8 1.9 %collective-permute-start.1 = (f32[48,128]{1,0:T(8,128)S(1)}, f32[48,128]{1,0:T(8,128)S(1)}, u32[]{:S(2)}, u32[]{:S(2)}) collective-permute-start(f32[48,128]{1,0:T(8,128)S(1)} %get-tuple-element.83.refs_0_), channel_id=1, source_target_pairs={{1,4},{4,1},{3,6},{6,3},{5,8},{8,5},{7,10},{10,7},{9,12},{12,9},{1... | collective-permute-start | bytes 73736 | tf_op jit(solution)/shard_map/ppermute | solution.py:905
  19.8 2.9 %shard_map.152 = (f32[32,4,128,128]{3,2,1,0:T(8,128)S(1)}, f32[32,128,128]{2,1,0:T(8,128)S(1)}) custom-call(s32[1,3]{1,0:T(1,128)S(1)} %copy-done.4, f32[48,128]{1,0:T(8,128)S(1)} %get-tuple-element.83.refs_0_, f32[128,128]{1,0:T(8,128)S(1)} %get-tuple-element.87.refs_1_.refs_0_, f32[2,2,5,40,128]{4,3,2,1,0:T(8,128)S(1)} %get-tuple-element.88.refs_2_.refs_1_), custom_call_target="tpu_custom_call" | custom-call | flops 3000000000 | bytes 10985472 | tf_op jit(solution)/shard_map/pallas_call | solution.py:86
  22.7 2.0 %shard_map.151.refs_0_ = f32[32,128,128]{2,1,0:T(8,128)S(1)} custom-call(s32[1,3]{1,0:T(1,128)S(1)} %copy-done.4, f32[32,128,128]{2,1,0:T(8,128)S(1)} %get-tuple-element.78.refs_0_.refs_1_, bf16[256,256]{1,0:T(8,128)(2,1)S(1)} %get-tuple-element.79.refs_1_.refs_5_.refs_8_.refs_7_.refs_10_, bf16[128,256]{1,0:T(8,128)(2,1)S(1)} %get-tuple-element.80.refs_2_.refs_9_.refs_11_), custom_call_target="tpu_custom_call" | custom-call | flops 2000000000 | bytes 4390912 | tf_op jit(solution)/shard_map/pallas_call | solution.py:86
  24.7 11.1 %all-gather = f32[96,128]{1,0:T(8,128)S(1)} all-gather(f32[48,128]{1,0:T(8,128)S(1)} %collective-permute-done.1), channel_id=2, replica_groups={{0,1},{2,3},{4,5},{6,7},{8,9},{10,11},{12,13},{14,15},{16,17},{18,19},{..., dimensions={0}, use_global_device_ids=true | all-gather | bytes 73728 | tf_op jit(solution)/shard_map/all_gather | solution.py:906
  37.5 4.8 %collective-permute-start.2 = (f32[5,64,128]{2,1,0:T(8,128)S(1)}, f32[5,64,128]{2,1,0:T(8,128)S(1)}, u32[]{:S(2)}, u32[]{:S(2)}) collective-permute-start(f32[5,64,128]{2,1,0:T(8,128)S(1)} %get-tuple-element.93.refs_0_), channel_id=1, source_target_pairs={{0,2},{2,0},{1,3},{3,1},{4,6},{6,4},{5,7},{7,5},{8,10},{10,8},{9,1... | collective-permute-start | bytes 491528 | tf_op jit(solution)/shard_map/ppermute | solution.py:951
  42.3 6.5 %shard_map.154 = (f32[4,4,128,128]{3,2,1,0:T(8,128)S(1)}, f32[4,128,128]{2,1,0:T(8,128)S(1)}, f32[8,4,128,128]{3,2,1,0:T(8,128)S(1)}, f32[4,128,128]{2,1,0:T(8,128)S(1)}, f32[128,128]{1,0:T(8,128)S(1)}) custom-call(s32[1,3]{1,0:T(1,128)S(1)} %copy-done.4, f32[128,128]{1,0:T(8,128)S(1)} %get-tuple-element.87.refs_1_.refs_0_, ...), custom_call_target="tpu_custom_call" | custom-call | flops 5000000000 | bytes 14778368 | tf_op jit(solution)/shard_map/pallas_call | solution.py:86
  48.8 2.8 %all-gather.1 = f32[10,64,128]{2,1,0:T(8,128)S(1)} all-gather(f32[5,64,128]{2,1,0:T(8,128)S(1)} %collective-permute-done.2), channel_id=3, replica_groups={{0,1},{2,3},{4,5},{6,7},{8,9},{10,11},{12,13},{14,15},{16,17},{18,19},{..., dimensions={0}, use_global_device_ids=true | all-gather | bytes 491520 | tf_op jit(solution)/shard_map/all_gather | solution.py:959
  52.5 2.2 %shard_map.156 = (f32[36,128,128]{2,1,0:T(8,128)S(1)}, f32[2,80,128]{2,1,0:T(8,128)S(1)}, f32[80,128]{1,0:T(8,128)S(1)}) custom-call(s32[1,3]{1,0:T(1,128)S(1)} %copy-done.4, f32[32,128,128]{2,1,0:T(8,128)S(1)} %get-tuple-element.91.refs_0_, f32[128,128]{1,0:T(8,128)S(1)} %get-tuple-element.92.refs_1_, f32[2,5,64,128]{3,2,1,0:T(8,128)S(1)} %bitcast.24, ...), custom_call_target="tpu_custom_call" | custom-call | flops 10000000 | bytes 20004864 | tf_op jit(solution)/shard_map/pallas_call | solution.py:86
  54.7 1.9 %collective-permute-start.4 = (f32[80,128]{1,0:T(8,128)S(1)}, f32[80,128]{1,0:T(8,128)S(1)}, u32[]{:S(2)}, u32[]{:S(2)}) collective-permute-start(f32[80,128]{1,0:T(8,128)S(1)} %get-tuple-element.113), channel_id=1, source_target_pairs={{1,4},{4,1},{3,6},{6,3},{5,8},{8,5},{7,10},{10,7},{9,12},{12,9},{1... | collective-permute-start | bytes 122888 | tf_op jit(solution)/shard_map/ppermute | solution.py:905
  56.6 3.6 %shard_map.157 = (f32[32,128,128]{2,1,0:T(8,128)S(1)}, f32[32,128,128]{2,1,0:T(8,128)S(1)}, f32[32,128,128]{2,1,0:T(8,128)S(1)}) custom-call(s32[1,3]{1,0:T(1,128)S(1)} %copy-done.4, f32[36,128,128]{2,1,0:T(8,128)S(1)} %get-tuple-element.104.refs_0_, f32[32,128,128]{2,1,0:T(8,128)S(1)} %get-tuple-element.78.refs_0_.refs_1_, ...), custom_call_target="tpu_custom_call" | custom-call | flops 4000000000 | bytes 13451264 | tf_op jit(solution)/shard_map/pallas_call | solution.py:86
  60.2 9.4 %all-gather.2 = f32[160,128]{1,0:T(8,128)S(1)} all-gather(f32[80,128]{1,0:T(8,128)S(1)} %collective-permute-done.4), channel_id=4, replica_groups={{0,1},{2,3},{4,5},{6,7},{8,9},{10,11},{12,13},{14,15},{16,17},{18,19},{..., dimensions={0}, use_global_device_ids=true | all-gather | bytes 122880 | tf_op jit(solution)/shard_map/all_gather | solution.py:906
  69.6 2.7 %shard_map.158 = (f32[32,128,128]{2,1,0:T(8,128)S(1)}, f32[5,64,128]{2,1,0:T(8,128)S(1)}, f32[128,128]{1,0:T(8,128)S(1)}, f32[6,4,40,128]{3,2,1,0:T(8,128)S(1)},...) custom-call(s32[1,3]{1,0:T(1,128)S(1)} %copy-done.4, f32[32,128,128]{2,1,0:T(8,128)S(1)} %get-tuple-element.111.refs_0_, ...), custom_call_target="tpu_custom_call" | custom-call | flops 10000000 | bytes 14643712 | tf_op jit(solution)/shard_map/pallas_call | solution.py:86
  72.3 12.0 %all-gather.3 = f32[20,64,128]{2,1,0:T(8,128)S(1)} all-gather(f32[5,64,128]{2,1,0:T(8,128)S(1)} %get-tuple-element.118), channel_id=5, replica_groups=mesh['patch'=128,'slab'=4] {'slab'}, dimensions={0}, use_global_device_ids=true | all-gather | bytes 819200 | tf_op jit(solution)/shard_map/all_gather | solution.py:949
  84.3 2.2 %shard_map.159 = (f32[36,128,128]{2,1,0:T(8,128)S(1)}, f32[2,40,128]{2,1,0:T(8,128)S(1)}, f32[40,128]{1,0:T(8,128)S(1)}) custom-call(s32[1,3]{1,0:T(1,128)S(1)} %copy-done.4, f32[32,128,128]{2,1,0:T(8,128)S(1)} %get-tuple-element.116.refs_0_, f32[128,128]{1,0:T(8,128)S(1)} %get-tuple-element.117.refs_1_, f32[4,5,64,128]{3,2,1,0:T(8,128)S(1)} %bitcast.23, ...), custom_call_target="tpu_custom_call" | custom-call | flops 10000000 | bytes 20230144 | tf_op jit(solution)/shard_map/pallas_call | solution.py:86
  86.5 2.1 %collective-permute-start.5 = (f32[40,128]{1,0:T(8,128)S(1)}, f32[40,128]{1,0:T(8,128)S(1)}, u32[]{:S(2)}, u32[]{:S(2)}) collective-permute-start(f32[40,128]{1,0:T(8,128)S(1)} %get-tuple-element.127), channel_id=1, source_target_pairs={{1,4},{4,1},{3,6},{6,3},{5,8},{8,5},{7,10},{10,7},{9,12},{12,9},{1... | collective-permute-start | bytes 61448 | tf_op jit(solution)/shard_map/ppermute | solution.py:905
  88.6 3.9 %shard_map.160 = (f32[32,128,128]{2,1,0:T(8,128)S(1)}, f32[32,128,128]{2,1,0:T(8,128)S(1)}, f32[32,128,128]{2,1,0:T(8,128)S(1)}) custom-call(s32[1,3]{1,0:T(1,128)S(1)} %copy-done.4, f32[36,128,128]{2,1,0:T(8,128)S(1)} %get-tuple-element.120.refs_0_, f32[32,128,128]{2,1,0:T(8,128)S(1)} %get-tuple-element.78.refs_0_.refs_1_, ...), custom_call_target="tpu_custom_call" | custom-call | flops 4000000000 | bytes 17645568 | tf_op jit(solution)/shard_map/pallas_call | solution.py:86
  92.5 7.8 %all-gather.4 = f32[80,128]{1,0:T(8,128)S(1)} all-gather(f32[40,128]{1,0:T(8,128)S(1)} %collective-permute-done.5), channel_id=6, replica_groups={{0,1},{2,3},{4,5},{6,7},{8,9},{10,11},{12,13},{14,15},{16,17},{18,19},{..., dimensions={0}, use_global_device_ids=true | all-gather | bytes 61440 | tf_op jit(solution)/shard_map/all_gather | solution.py:906
  100.3 2.8 %shard_map.161 = (f32[32,128,128]{2,1,0:T(8,128)S(1)}, f32[5,64,128]{2,1,0:T(8,128)S(1)}, f32[128,128]{1,0:T(8,128)S(1)}, f32[6,4,40,128]{3,2,1,0:T(8,128)S(1)},...) custom-call(s32[1,3]{1,0:T(1,128)S(1)} %copy-done.4, f32[32,128,128]{2,1,0:T(8,128)S(1)} %get-tuple-element.125.refs_0_, ...), custom_call_target="tpu_custom_call" | custom-call | flops 10000000 | bytes 14561792 | tf_op jit(solution)/shard_map/pallas_call | solution.py:86
  103.1 11.9 %all-gather.5 = f32[20,64,128]{2,1,0:T(8,128)S(1)} all-gather(f32[5,64,128]{2,1,0:T(8,128)S(1)} %get-tuple-element.130), channel_id=7, replica_groups=mesh['patch'=128,'slab'=4] {'slab'}, dimensions={0}, use_global_device_ids=true | all-gather | bytes 819200 | tf_op jit(solution)/shard_map/all_gather | solution.py:949
  115.0 2.4 %shard_map.162 = (f32[36,128,128]{2,1,0:T(8,128)S(1)}, f32[2,40,128]{2,1,0:T(8,128)S(1)}) custom-call(s32[1,3]{1,0:T(1,128)S(1)} %copy-done.4, f32[32,128,128]{2,1,0:T(8,128)S(1)} %get-tuple-element.128.refs_0_, f32[128,128]{1,0:T(8,128)S(1)} %get-tuple-element.129.refs_1_, f32[4,5,64,128]{3,2,1,0:T(8,128)S(1)} %bitcast.22, ...), custom_call_target="tpu_custom_call" | custom-call | flops 10000000 | bytes 20209664 | tf_op jit(solution)/shard_map/pallas_call | solution.py:86
  117.4 4.1 %shard_map.163 = (f32[16,128,128]{2,1,0:T(8,128)S(1)}, f32[32,128,128]{2,1,0:T(8,128)S(1)}, f32[2,72,128]{2,1,0:T(8,128)S(1)}, f32[72,128]{1,0:T(8,128)S(1)}) custom-call(s32[1,3]{1,0:T(1,128)S(1)} %copy-done.4, f32[36,128,128]{2,1,0:T(8,128)S(1)} %get-tuple-element.132.refs_0_, f32[32,128,128]{2,1,0:T(8,128)S(1)} %get-tuple-element.78.refs_0_.refs_1_, ...), custom_call_target="tpu_custom_call" | custom-call | flops 3000000000 | bytes 14585856 | tf_op jit(solution)/shard_map/pallas_call | solution.py:86
  121.5 1.9 %collective-permute-start.6 = (f32[72,128]{1,0:T(8,128)S(1)}, f32[72,128]{1,0:T(8,128)S(1)}, u32[]{:S(2)}, u32[]{:S(2)}) collective-permute-start(f32[72,128]{1,0:T(8,128)S(1)} %get-tuple-element.141), channel_id=1, source_target_pairs={{1,4},{4,1},{3,6},{6,3},{5,8},{8,5},{7,10},{10,7},{9,12},{12,9},{1... | collective-permute-start | bytes 110600 | tf_op jit(solution)/shard_map/ppermute | solution.py:905
  123.5 2.1 %shard_map.166 = (f32[32,32,128]{2,1,0:T(8,128)S(1)}, f32[32,32,128]{2,1,0:T(8,128)S(1)}) custom-call(s32[1,3]{1,0:T(1,128)S(1)} %copy-done.4, f32[32,128,128]{2,1,0:T(8,128)S(1)} %get-tuple-element.145.refs_0_, bf16[256,256]{1,0:T(8,128)(2,1)S(1)} %get-tuple-element.146.refs_1_, bf16[128,256]{1,0:T(8,128)(2,1)S(1)} %get-tuple-element.147.refs_2_), custom_call_target="tpu_custom_call" | custom-call | flops 3000000000 | bytes 3342336 | tf_op jit(solution)/shard_map/pallas_call | solution.py:86
  125.5 2.2 %collective-permute-start.7 = (f32[32,32,128]{2,1,0:T(8,128)S(1)}, f32[32,32,128]{2,1,0:T(8,128)S(1)}, u32[]{:S(2)}, u32[]{:S(2)}) collective-permute-start(f32[32,32,128]{2,1,0:T(8,128)S(1)} %get-tuple-element.149), channel_id=1, source_target_pairs={{0,2},{2,0},{1,3},{3,1},{4,6},{6,4},{5,7},{7,5},{8,10},{10,8},{9,1... | collective-permute-start | bytes 1572872 | tf_op jit(solution)/shard_map/ppermute | solution.py:987
  127.8 9.9 %collective-permute-done.6 = f32[72,128]{1,0:T(8,128)S(1)} collective-permute-done((f32[72,128]{1,0:T(8,128)S(1)}, f32[72,128]{1,0:T(8,128)S(1)}, u32[]{:S(2)}, u32[]{:S(2)}) %collective-permute-start.6) | collective-permute-done | bytes 36896 | tf_op jit(solution)/shard_map/ppermute | solution.py:905
  139.5 2.0 %shard_map.164 = (f32[6,32,128]{2,1,0:T(8,128)S(1)}, f32[2,40,128]{2,1,0:T(8,128)S(1)}) custom-call(s32[1,3]{1,0:T(1,128)S(1)} %copy-done.4, f32[1,3]{1,0:T(1,128)S(1)} %copy-done.11, f32[2,72,128]{2,1,0:T(8,128)S(1)} %get-tuple-element.140.refs_1_, f32[2,72,128]{2,1,0:T(8,128)S(1)} %bitcast.31, f32[6,4,40,128]{3,2,1,0:T(8,128)S(1)} %get-tuple-element.131.refs_13_.refs_3_, ...), custom_call_target="tpu_custom_call" | custom-call | flops 80000000000 | bytes 1200640 | tf_op jit(solution)/shard_map/pallas_call | solution.py:86
  141.6 4.0 %collective-permute-start.8 = (f32[6,32,128]{2,1,0:T(8,128)S(1)}, f32[6,32,128]{2,1,0:T(8,128)S(1)}, u32[]{:S(2)}, u32[]{:S(2)}) collective-permute-start(f32[6,32,128]{2,1,0:T(8,128)S(1)} %get-tuple-element.151.refs_1_), channel_id=1, source_target_pairs={{0,2},{2,0},{1,3},{3,1},{4,6},{6,4},{5,7},{7,5},{8,10},{10,8},{9,1... | collective-permute-start | bytes 294920 | tf_op jit(solution)/shard_map/ppermute | solution.py:1001
  149.2 2.6 %collective-permute-done.8.refs_2_ = f32[6,32,128]{2,1,0:T(8,128)S(1)} collective-permute-done((f32[6,32,128]{2,1,0:T(8,128)S(1)}, f32[6,32,128]{2,1,0:T(8,128)S(1)}, u32[]{:S(2)}, u32[]{:S(2)}) %collective-permute-start.8) | collective-permute-done | bytes 98336 | tf_op jit(solution)/shard_map/ppermute | solution.py:1001
  151.8 3.4 %shard_map.168 = f32[62,1,3969]{2,1,0:T(1,128)} custom-call(s32[1,3]{1,0:T(1,128)S(1)} %copy-done.4, f32[32,62,128]{2,1,0:T(8,128)S(1)} %shard_map.167.refs_0_, f32[6,32,128]{2,1,0:T(8,128)S(1)} %get-tuple-element.151.refs_1_, f32[6,32,128]{2,1,0:T(8,128)S(1)} %collective-permute-done.8.refs_2_, f32[6,128,128]{2,1,0:T(8,128)S(1)} %get-tuple-element.152.refs_3_, ...), custom_call_target="tpu_custom_call" | custom-call | flops 20000000000 | bytes 2609912 | tf_op jit(solution)/shard_map/pallas_call | solution.py:86
  (43 shorter events, 12.1 us)
Async XLA Ops:
  0.6 10.3 %copy-start.12 = (f32[1,16,16384]{2,1,0:T(8,128)S(1)}, f32[1,16,16384]{2,1,0:T(8,128)}, u32[]{:S(2)}) copy-start(f32[1,16,16384]{2,1,0:T(8,128)} %param.15) | copy-start | bytes 3145732
  0.6 12.6 %copy-start.4 = (s32[1,3]{1,0:T(1,128)S(1)}, s32[1,3]{1,0:T(1,128)}, u32[]{:S(2)}) copy-start(s32[1,3]{1,0:T(1,128)} %links_ref.39) | copy-start | bytes 40
  2.2 11.1 %collective-permute-start = (f32[16,128,128]{2,1,0:T(8,128)S(1)}, f32[16,128,128]{2,1,0:T(8,128)S(1)}, u32[]{:S(2)}, u32[]{:S(2)}) collective-permute-start(f32[16,128,128]{2,1,0:T(8,128)S(1)} %bitcast.20), channel_id=1, source_target_pairs={{0,1},{1,0},{2,3},{3,2},{4,5},{5,4},{6,7},{7,6},{8,9},{9,8},{10,11... | collective-permute-start | bytes 3145736 | tf_op jit(solution)/shard_map/ppermute | solution.py:911
  11.0 5.4 %copy-start = (f32[128,128]{1,0:T(8,128)S(1)}, f32[128,128]{1,0:T(8,128)}, u32[]{:S(2)}) copy-start(f32[128,128]{1,0:T(8,128)} %refs_1_.1) | copy-start | bytes 196612
  11.0 5.4 %copy-start.1 = (f32[128,128]{1,0:T(8,128)S(1)}, f32[128,128]{1,0:T(8,128)}, u32[]{:S(2)}) copy-start(f32[128,128]{1,0:T(8,128)} %refs_2_.1) | copy-start | bytes 196612
  11.0 5.4 %copy-start.2 = (f32[128,128]{1,0:T(8,128)S(1)}, f32[128,128]{1,0:T(8,128)}, u32[]{:S(2)}) copy-start(f32[128,128]{1,0:T(8,128)} %refs_5_.1) | copy-start | bytes 196612
  11.0 5.4 %copy-start.3 = (f32[126,128]{1,0:T(8,128)S(1)}, f32[126,128]{1,0:T(8,128)}, u32[]{:S(2)}) copy-start(f32[126,128]{1,0:T(8,128)} %refs_9_.1) | copy-start | bytes 193540
  11.0 5.4 %copy-start.5 = (f32[64,64]{1,0:T(8,128)S(1)}, f32[64,64]{1,0:T(8,128)}, u32[]{:S(2)}) copy-start(f32[64,64]{1,0:T(8,128)} %refs_3_.1) | copy-start | bytes 49156
  11.0 5.4 %copy-start.6 = (f32[64,64]{1,0:T(8,128)S(1)}, f32[64,64]{1,0:T(8,128)}, u32[]{:S(2)}) copy-start(f32[64,64]{1,0:T(8,128)} %refs_4_.1) | copy-start | bytes 49156
  11.0 5.4 %copy-start.7 = (f32[64,64]{1,0:T(8,128)S(1)}, f32[64,64]{1,0:T(8,128)}, u32[]{:S(2)}) copy-start(f32[64,64]{1,0:T(8,128)} %refs_7_.1) | copy-start | bytes 49156
  11.1 5.4 %copy-start.8 = (f32[62,64]{1,0:T(8,128)S(1)}, f32[62,64]{1,0:T(8,128)}, u32[]{:S(2)}) copy-start(f32[62,64]{1,0:T(8,128)} %refs_10_.1) | copy-start | bytes 47620
  11.1 5.4 %copy-start.9 = (f32[128]{0:T(128)S(1)}, f32[128]{0:T(128)}, u32[]{:S(2)}) copy-start(f32[128]{0:T(128)} %param.22) | copy-start | bytes 1540
  11.1 5.4 %copy-start.10 = (f32[64]{0:T(128)S(1)}, f32[64]{0:T(128)}, u32[]{:S(2)}) copy-start(f32[64]{0:T(128)} %param.24) | copy-start | bytes 772
  11.1 5.4 %copy-start.11 = (f32[1,3]{1,0:T(1,128)S(1)}, f32[1,3]{1,0:T(1,128)}, u32[]{:S(2)}) copy-start(f32[1,3]{1,0:T(1,128)} %refs_0_.3) | copy-start | bytes 40
  14.1 37.5 %collective-permute-start.3 = (f32[16,128,128]{2,1,0:T(8,128)S(1)}, f32[16,128,128]{2,1,0:T(8,128)S(1)}, u32[]{:S(2)}, u32[]{:S(2)}) collective-permute-start(f32[16,128,128]{2,1,0:T(8,128)S(1)} %bitcast.18), channel_id=1, source_target_pairs={{0,1},{1,0},{2,3},{3,2},{4,5},{5,4},{6,7},{7,6},{8,9},{9,8},{10,11... | collective-permute-start | bytes 3145736 | tf_op jit(solution)/shard_map/ppermute | solution.py:918
  17.8 6.8 %collective-permute-start.1 = (f32[48,128]{1,0:T(8,128)S(1)}, f32[48,128]{1,0:T(8,128)S(1)}, u32[]{:S(2)}, u32[]{:S(2)}) collective-permute-start(f32[48,128]{1,0:T(8,128)S(1)} %get-tuple-element.83.refs_0_), channel_id=1, source_target_pairs={{1,4},{4,1},{3,6},{6,3},{5,8},{8,5},{7,10},{10,7},{9,12},{12,9},{1... | collective-permute-start | bytes 73736 | tf_op jit(solution)/shard_map/ppermute | solution.py:905
  37.5 11.3 %collective-permute-start.2 = (f32[5,64,128]{2,1,0:T(8,128)S(1)}, f32[5,64,128]{2,1,0:T(8,128)S(1)}, u32[]{:S(2)}, u32[]{:S(2)}) collective-permute-start(f32[5,64,128]{2,1,0:T(8,128)S(1)} %get-tuple-element.93.refs_0_), channel_id=1, source_target_pairs={{0,2},{2,0},{1,3},{3,1},{4,6},{6,4},{5,7},{7,5},{8,10},{10,8},{9,1... | collective-permute-start | bytes 491528 | tf_op jit(solution)/shard_map/ppermute | solution.py:951
  54.7 5.5 %collective-permute-start.4 = (f32[80,128]{1,0:T(8,128)S(1)}, f32[80,128]{1,0:T(8,128)S(1)}, u32[]{:S(2)}, u32[]{:S(2)}) collective-permute-start(f32[80,128]{1,0:T(8,128)S(1)} %get-tuple-element.113), channel_id=1, source_target_pairs={{1,4},{4,1},{3,6},{6,3},{5,8},{8,5},{7,10},{10,7},{9,12},{12,9},{1... | collective-permute-start | bytes 122888 | tf_op jit(solution)/shard_map/ppermute | solution.py:905
  86.5 6.0 %collective-permute-start.5 = (f32[40,128]{1,0:T(8,128)S(1)}, f32[40,128]{1,0:T(8,128)S(1)}, u32[]{:S(2)}, u32[]{:S(2)}) collective-permute-start(f32[40,128]{1,0:T(8,128)S(1)} %get-tuple-element.127), channel_id=1, source_target_pairs={{1,4},{4,1},{3,6},{6,3},{5,8},{8,5},{7,10},{10,7},{9,12},{12,9},{1... | collective-permute-start | bytes 61448 | tf_op jit(solution)/shard_map/ppermute | solution.py:905
  121.5 16.2 %collective-permute-start.6 = (f32[72,128]{1,0:T(8,128)S(1)}, f32[72,128]{1,0:T(8,128)S(1)}, u32[]{:S(2)}, u32[]{:S(2)}) collective-permute-start(f32[72,128]{1,0:T(8,128)S(1)} %get-tuple-element.141), channel_id=1, source_target_pairs={{1,4},{4,1},{3,6},{6,3},{5,8},{8,5},{7,10},{10,7},{9,12},{12,9},{1... | collective-permute-start | bytes 110600 | tf_op jit(solution)/shard_map/ppermute | solution.py:905
  125.5 22.1 %collective-permute-start.7 = (f32[32,32,128]{2,1,0:T(8,128)S(1)}, f32[32,32,128]{2,1,0:T(8,128)S(1)}, u32[]{:S(2)}, u32[]{:S(2)}) collective-permute-start(f32[32,32,128]{2,1,0:T(8,128)S(1)} %get-tuple-element.149), channel_id=1, source_target_pairs={{0,2},{2,0},{1,3},{3,1},{4,6},{6,4},{5,7},{7,5},{8,10},{10,8},{9,1... | collective-permute-start | bytes 1572872 | tf_op jit(solution)/shard_map/ppermute | solution.py:987
  141.6 10.2 %collective-permute-start.8 = (f32[6,32,128]{2,1,0:T(8,128)S(1)}, f32[6,32,128]{2,1,0:T(8,128)S(1)}, u32[]{:S(2)}, u32[]{:S(2)}) collective-permute-start(f32[6,32,128]{2,1,0:T(8,128)S(1)} %get-tuple-element.151.refs_1_), channel_id=1, source_target_pairs={{0,2},{2,0},{1,3},{3,1},{4,6},{6,4},{5,7},{7,5},{8,10},{10,8},{9,1... | collective-permute-start | bytes 294920 | tf_op jit(solution)/shard_map/ppermute | solution.py:1001

commit v6 on v4

--- a/solution.py
+++ b/solution.py
@@ -47,6 +47,12 @@
 
 def dot_full(x, y):
     return jnp.dot(x, y, precision=HIGHEST, preferred_element_type=F32)
+
+
+def three_products(x, y):
+    (xh, xl), (yh, yl) = split(x), split(y)
+    out = jnp.dot(xh, yl, preferred_element_type=F32) + jnp.dot(xl, yh, preferred_element_type=F32)
+    return out + jnp.dot(xh, yh, preferred_element_type=F32)
 
 
 def mirrored(x, mirror):
@@ -682,14 +688,14 @@
     for c in range(32):
         rows = pl.ds(c, HALF, stride=32)
         both = jnp.concatenate([kept[rows, :], arrived[rows, :]], axis=0)
-        blocks[c] = dot_full(vertical[...], both)
+        blocks[c] = three_products(vertical[...], both)
 
 
 def coarse_kernel(ints, start_blocks, parts, far_parts, profile, profile_rows, vertical, out, blocks, columns):
     deep = vertical.shape[0]
     spots = [0, 31, COARSE // 2, COARSE // 2 + 31]
     stacked = [jnp.concatenate([parts[s], far_parts[s]], axis=0) for s in range(6)]
-    mixed = dot_full(vertical[...], jnp.concatenate(stacked, axis=1))
+    mixed = three_products(vertical[...], jnp.concatenate(stacked, axis=1))
     mixed = [mixed[:, s * N:(s + 1) * N] for s in range(6)]
 
     @pl.when(ints[1] == 0)

time: 153 us -> 154 us (level)
  waiting for transfers between devices: 12.9 us -> 15 us
  transfers between devices with their start and end apart: 9 -> 9, of which waited for: 2 -> 3; matrix products, arithmetic and copies ran while one was open for 1% -> 1% of each run, Pallas kernels for 20% -> 19%
where the time goes in v6:
time: 154 us; the launch traced here: 152 us
  blocking collectives  56 us (36%)
  Pallas kernels  49.2 us (32%)
  starting transfers between devices  28.3 us (18%)
  waiting for transfers between devices  15 us (10%)
  local copies, waits for them, and re-layouts  2.93 us (2%)
    pallas_call x20, Pallas kernels, call(): pl.pallas_call(body, out_shape=shapes, in_specs=specs, out_specs=[pl.Bloc...  49.2 us
    all_gather x4, blocking collectives, swap_faces(): return lambda: lax.all_gather(arrived, 'slab', axis_index_groups=chips)  29.9 us
    all_gather x2, blocking collectives, per_device(): received = lax.all_gather(msg, 'slab')  23.8 us
    ppermute x4, waiting for transfers between devices, swap_faces(): arrived = lax.ppermute(slot_values, ('patch', 'slab'), faces)  10.9 us
    ppermute x1, starting transfers between devices, per_device(): other_load = lax.ppermute(own_load, 'slab', pair)  8.79 us
    ppermute x4, starting transfers between devices, swap_faces(): arrived = lax.ppermute(slot_values, ('patch', 'slab'), faces)  7.86 us
    ppermute x1, starting transfers between devices, per_device(): crossing = lax.ppermute(msg, 'slab', cross)  4.76 us
    ppermute x1, waiting for transfers between devices, per_device(): far_parts = lax.ppermute(parts, 'slab', cross)  3.71 us
  transfers between devices with their start and end apart: 9, of which 3 were waited for; matrix products, arithmetic and copies ran while one was open for 1% of the time, Pallas kernels for 19%

profile of v6, /device:TPU:1, one launch (start us, length us, event | category | flops | bytes accessed | tf_op | source)
XLA Modules:
  0.0 152.5 jit_solution(17064431773818138190)
XLA Ops:
  2.3 8.8 %collective-permute-start = (f32[16,128,128]{2,1,0:T(8,128)S(1)}, f32[16,128,128]{2,1,0:T(8,128)S(1)}, u32[]{:S(2)}, u32[]{:S(2)}) collective-permute-start(f32[16,128,128]{2,1,0:T(8,128)S(1)} %bitcast.20), channel_id=1, source_target_pairs={{0,1},{1,0},{2,3},{3,2},{4,5},{5,4},{6,7},{7,6},{8,9},{9,8},{10,11... | collective-permute-start | bytes 3145736 | tf_op jit(solution)/shard_map/ppermute | solution.py:917
  11.3 1.9 %collective-permute-start.3 = (f32[16,128,128]{2,1,0:T(8,128)S(1)}, f32[16,128,128]{2,1,0:T(8,128)S(1)}, u32[]{:S(2)}, u32[]{:S(2)}) collective-permute-start(f32[16,128,128]{2,1,0:T(8,128)S(1)} %bitcast.18), channel_id=1, source_target_pairs={{0,1},{1,0},{2,3},{3,2},{4,5},{5,4},{6,7},{7,6},{8,9},{9,8},{10,11... | collective-permute-start | bytes 3145736 | tf_op jit(solution)/shard_map/ppermute | solution.py:918
  15.5 1.9 %collective-permute-start.1 = (f32[48,128]{1,0:T(8,128)S(1)}, f32[48,128]{1,0:T(8,128)S(1)}, u32[]{:S(2)}, u32[]{:S(2)}) collective-permute-start(f32[48,128]{1,0:T(8,128)S(1)} %get-tuple-element.80.refs_0_), channel_id=1, source_target_pairs={{1,4},{4,1},{3,6},{6,3},{5,8},{8,5},{7,10},{10,7},{9,12},{12,9},{1... | collective-permute-start | bytes 73736 | tf_op jit(solution)/shard_map/ppermute | solution.py:911
  17.5 2.9 %shard_map.152 = (f32[32,4,128,128]{3,2,1,0:T(8,128)S(1)}, f32[32,128,128]{2,1,0:T(8,128)S(1)}) custom-call(s32[1,3]{1,0:T(1,128)S(1)} %copy-done.4, f32[48,128]{1,0:T(8,128)S(1)} %get-tuple-element.80.refs_0_, f32[128,128]{1,0:T(8,128)S(1)} %get-tuple-element.84.refs_1_.refs_0_, f32[2,2,5,40,128]{4,3,2,1,0:T(8,128)S(1)} %get-tuple-element.85.refs_2_.refs_1_), custom_call_target="tpu_custom_call" | custom-call | flops 3000000000 | bytes 10985472 | tf_op jit(solution)/shard_map/pallas_call | solution.py:92
  20.4 2.0 %shard_map.151.refs_0_ = f32[32,128,128]{2,1,0:T(8,128)S(1)} custom-call(s32[1,3]{1,0:T(1,128)S(1)} %copy-done.4, f32[32,128,128]{2,1,0:T(8,128)S(1)} %get-tuple-element.76.refs_0_.refs_1_, bf16[256,256]{1,0:T(8,128)(2,1)S(1)} %get-tuple-element.77.refs_1_.refs_5_.refs_8_.refs_7_.refs_10_, bf16[128,256]{1,0:T(8,128)(2,1)S(1)} %get-tuple-element.78.refs_2_.refs_9_.refs_11_), custom_call_target="tpu_custom_call" | custom-call | flops 2000000000 | bytes 4390912 | tf_op jit(solution)/shard_map/pallas_call | solution.py:92
  22.4 10.5 %all-gather = f32[96,128]{1,0:T(8,128)S(1)} all-gather(f32[48,128]{1,0:T(8,128)S(1)} %collective-permute-done.1), channel_id=2, replica_groups={{0,1},{2,3},{4,5},{6,7},{8,9},{10,11},{12,13},{14,15},{16,17},{18,19},{..., dimensions={0}, use_global_device_ids=true | all-gather | bytes 73728 | tf_op jit(solution)/shard_map/all_gather | solution.py:912
  34.7 4.8 %collective-permute-start.2 = (f32[5,64,128]{2,1,0:T(8,128)S(1)}, f32[5,64,128]{2,1,0:T(8,128)S(1)}, u32[]{:S(2)}, u32[]{:S(2)}) collective-permute-start(f32[5,64,128]{2,1,0:T(8,128)S(1)} %get-tuple-element.90.refs_0_), channel_id=1, source_target_pairs={{0,2},{2,0},{1,3},{3,1},{4,6},{6,4},{5,7},{7,5},{8,10},{10,8},{9,1... | collective-permute-start | bytes 491528 | tf_op jit(solution)/shard_map/ppermute | solution.py:956
  39.4 6.4 %shard_map.154 = (f32[4,4,128,128]{3,2,1,0:T(8,128)S(1)}, f32[4,128,128]{2,1,0:T(8,128)S(1)}, f32[8,4,128,128]{3,2,1,0:T(8,128)S(1)}, f32[4,128,128]{2,1,0:T(8,128)S(1)}, f32[128,128]{1,0:T(8,128)S(1)}) custom-call(s32[1,3]{1,0:T(1,128)S(1)} %copy-done.4, f32[128,128]{1,0:T(8,128)S(1)} %get-tuple-element.84.refs_1_.refs_0_, ...), custom_call_target="tpu_custom_call" | custom-call | flops 5000000000 | bytes 14778368 | tf_op jit(solution)/shard_map/pallas_call | solution.py:92
  46.7 2.3 %all-gather.1 = f32[10,64,128]{2,1,0:T(8,128)S(1)} all-gather(f32[5,64,128]{2,1,0:T(8,128)S(1)} %collective-permute-done.2), channel_id=3, replica_groups={{0,1},{2,3},{4,5},{6,7},{8,9},{10,11},{12,13},{14,15},{16,17},{18,19},{..., dimensions={0}, use_global_device_ids=true | all-gather | bytes 491520 | tf_op jit(solution)/shard_map/all_gather | solution.py:964
  49.0 2.2 %shard_map.156 = (f32[36,128,128]{2,1,0:T(8,128)S(1)}, f32[2,80,128]{2,1,0:T(8,128)S(1)}, f32[80,128]{1,0:T(8,128)S(1)}) custom-call(s32[1,3]{1,0:T(1,128)S(1)} %copy-done.4, f32[32,128,128]{2,1,0:T(8,128)S(1)} %get-tuple-element.88.refs_0_, f32[128,128]{1,0:T(8,128)S(1)} %get-tuple-element.89.refs_1_, f32[2,5,64,128]{3,2,1,0:T(8,128)S(1)} %bitcast.24, ...), custom_call_target="tpu_custom_call" | custom-call | flops 10000000 | bytes 20004864 | tf_op jit(solution)/shard_map/pallas_call | solution.py:92
  51.2 1.9 %collective-permute-start.4 = (f32[80,128]{1,0:T(8,128)S(1)}, f32[80,128]{1,0:T(8,128)S(1)}, u32[]{:S(2)}, u32[]{:S(2)}) collective-permute-start(f32[80,128]{1,0:T(8,128)S(1)} %get-tuple-element.109), channel_id=1, source_target_pairs={{1,4},{4,1},{3,6},{6,3},{5,8},{8,5},{7,10},{10,7},{9,12},{12,9},{1... | collective-permute-start | bytes 122888 | tf_op jit(solution)/shard_map/ppermute | solution.py:911
  53.1 3.5 %shard_map.157 = (f32[32,128,128]{2,1,0:T(8,128)S(1)}, f32[32,128,128]{2,1,0:T(8,128)S(1)}, f32[32,128,128]{2,1,0:T(8,128)S(1)}) custom-call(s32[1,3]{1,0:T(1,128)S(1)} %copy-done.4, f32[36,128,128]{2,1,0:T(8,128)S(1)} %get-tuple-element.100.refs_0_, f32[32,128,128]{2,1,0:T(8,128)S(1)} %get-tuple-element.76.refs_0_.refs_1_, ...), custom_call_target="tpu_custom_call" | custom-call | flops 4000000000 | bytes 13451264 | tf_op jit(solution)/shard_map/pallas_call | solution.py:92
  56.6 8.6 %all-gather.2 = f32[160,128]{1,0:T(8,128)S(1)} all-gather(f32[80,128]{1,0:T(8,128)S(1)} %collective-permute-done.4), channel_id=4, replica_groups={{0,1},{2,3},{4,5},{6,7},{8,9},{10,11},{12,13},{14,15},{16,17},{18,19},{..., dimensions={0}, use_global_device_ids=true | all-gather | bytes 122880 | tf_op jit(solution)/shard_map/all_gather | solution.py:912
  65.2 2.7 %shard_map.158 = (f32[32,128,128]{2,1,0:T(8,128)S(1)}, f32[5,64,128]{2,1,0:T(8,128)S(1)}, f32[128,128]{1,0:T(8,128)S(1)}, f32[6,4,40,128]{3,2,1,0:T(8,128)S(1)},...) custom-call(s32[1,3]{1,0:T(1,128)S(1)} %copy-done.4, f32[32,128,128]{2,1,0:T(8,128)S(1)} %get-tuple-element.107.refs_0_, ...), custom_call_target="tpu_custom_call" | custom-call | flops 10000000 | bytes 14643712 | tf_op jit(solution)/shard_map/pallas_call | solution.py:92
  67.8 11.9 %all-gather.3 = f32[20,64,128]{2,1,0:T(8,128)S(1)} all-gather(f32[5,64,128]{2,1,0:T(8,128)S(1)} %get-tuple-element.114), channel_id=5, replica_groups=mesh['patch'=128,'slab'=4] {'slab'}, dimensions={0}, use_global_device_ids=true | all-gather | bytes 819200 | tf_op jit(solution)/shard_map/all_gather | solution.py:954
  79.7 2.2 %shard_map.159 = (f32[36,128,128]{2,1,0:T(8,128)S(1)}, f32[2,40,128]{2,1,0:T(8,128)S(1)}, f32[40,128]{1,0:T(8,128)S(1)}) custom-call(s32[1,3]{1,0:T(1,128)S(1)} %copy-done.4, f32[32,128,128]{2,1,0:T(8,128)S(1)} %get-tuple-element.112.refs_0_, f32[128,128]{1,0:T(8,128)S(1)} %get-tuple-element.113.refs_1_, f32[4,5,64,128]{3,2,1,0:T(8,128)S(1)} %bitcast.23, ...), custom_call_target="tpu_custom_call" | custom-call | flops 10000000 | bytes 20230144 | tf_op jit(solution)/shard_map/pallas_call | solution.py:92
  81.9 2.1 %collective-permute-start.5 = (f32[40,128]{1,0:T(8,128)S(1)}, f32[40,128]{1,0:T(8,128)S(1)}, u32[]{:S(2)}, u32[]{:S(2)}) collective-permute-start(f32[40,128]{1,0:T(8,128)S(1)} %get-tuple-element.123), channel_id=1, source_target_pairs={{1,4},{4,1},{3,6},{6,3},{5,8},{8,5},{7,10},{10,7},{9,12},{12,9},{1... | collective-permute-start | bytes 61448 | tf_op jit(solution)/shard_map/ppermute | solution.py:911
  84.0 3.7 %shard_map.160 = (f32[32,128,128]{2,1,0:T(8,128)S(1)}, f32[32,128,128]{2,1,0:T(8,128)S(1)}, f32[32,128,128]{2,1,0:T(8,128)S(1)}) custom-call(s32[1,3]{1,0:T(1,128)S(1)} %copy-done.4, f32[36,128,128]{2,1,0:T(8,128)S(1)} %get-tuple-element.116.refs_0_, f32[32,128,128]{2,1,0:T(8,128)S(1)} %get-tuple-element.76.refs_0_.refs_1_, ...), custom_call_target="tpu_custom_call" | custom-call | flops 4000000000 | bytes 17645568 | tf_op jit(solution)/shard_map/pallas_call | solution.py:92
  87.8 9.0 %all-gather.4 = f32[80,128]{1,0:T(8,128)S(1)} all-gather(f32[40,128]{1,0:T(8,128)S(1)} %collective-permute-done.5), channel_id=6, replica_groups={{0,1},{2,3},{4,5},{6,7},{8,9},{10,11},{12,13},{14,15},{16,17},{18,19},{..., dimensions={0}, use_global_device_ids=true | all-gather | bytes 61440 | tf_op jit(solution)/shard_map/all_gather | solution.py:912
  96.7 2.8 %shard_map.161 = (f32[32,128,128]{2,1,0:T(8,128)S(1)}, f32[5,64,128]{2,1,0:T(8,128)S(1)}, f32[128,128]{1,0:T(8,128)S(1)}, f32[6,4,40,128]{3,2,1,0:T(8,128)S(1)},...) custom-call(s32[1,3]{1,0:T(1,128)S(1)} %copy-done.4, f32[32,128,128]{2,1,0:T(8,128)S(1)} %get-tuple-element.121.refs_0_, ...), custom_call_target="tpu_custom_call" | custom-call | flops 10000000 | bytes 14561792 | tf_op jit(solution)/shard_map/pallas_call | solution.py:92
  99.5 11.9 %all-gather.5 = f32[20,64,128]{2,1,0:T(8,128)S(1)} all-gather(f32[5,64,128]{2,1,0:T(8,128)S(1)} %get-tuple-element.126), channel_id=7, replica_groups=mesh['patch'=128,'slab'=4] {'slab'}, dimensions={0}, use_global_device_ids=true | all-gather | bytes 819200 | tf_op jit(solution)/shard_map/all_gather | solution.py:954
  111.4 2.4 %shard_map.162 = (f32[36,128,128]{2,1,0:T(8,128)S(1)}, f32[2,40,128]{2,1,0:T(8,128)S(1)}) custom-call(s32[1,3]{1,0:T(1,128)S(1)} %copy-done.4, f32[32,128,128]{2,1,0:T(8,128)S(1)} %get-tuple-element.124.refs_0_, f32[128,128]{1,0:T(8,128)S(1)} %get-tuple-element.125.refs_1_, f32[4,5,64,128]{3,2,1,0:T(8,128)S(1)} %bitcast.22, ...), custom_call_target="tpu_custom_call" | custom-call | flops 10000000 | bytes 20209664 | tf_op jit(solution)/shard_map/pallas_call | solution.py:92
  113.8 4.1 %shard_map.163 = (f32[16,128,128]{2,1,0:T(8,128)S(1)}, f32[32,128,128]{2,1,0:T(8,128)S(1)}, f32[2,72,128]{2,1,0:T(8,128)S(1)}, f32[72,128]{1,0:T(8,128)S(1)}) custom-call(s32[1,3]{1,0:T(1,128)S(1)} %copy-done.4, f32[36,128,128]{2,1,0:T(8,128)S(1)} %get-tuple-element.128.refs_0_, f32[32,128,128]{2,1,0:T(8,128)S(1)} %get-tuple-element.76.refs_0_.refs_1_, ...), custom_call_target="tpu_custom_call" | custom-call | flops 3000000000 | bytes 14585856 | tf_op jit(solution)/shard_map/pallas_call | solution.py:92
  118.0 1.9 %collective-permute-start.6 = (f32[72,128]{1,0:T(8,128)S(1)}, f32[72,128]{1,0:T(8,128)S(1)}, u32[]{:S(2)}, u32[]{:S(2)}) collective-permute-start(f32[72,128]{1,0:T(8,128)S(1)} %get-tuple-element.137), channel_id=1, source_target_pairs={{1,4},{4,1},{3,6},{6,3},{5,8},{8,5},{7,10},{10,7},{9,12},{12,9},{1... | collective-permute-start | bytes 110600 | tf_op jit(solution)/shard_map/ppermute | solution.py:911
  119.9 2.1 %shard_map.166 = (f32[32,32,128]{2,1,0:T(8,128)S(1)}, f32[32,32,128]{2,1,0:T(8,128)S(1)}) custom-call(s32[1,3]{1,0:T(1,128)S(1)} %copy-done.4, f32[32,128,128]{2,1,0:T(8,128)S(1)} %get-tuple-element.141.refs_0_, bf16[256,256]{1,0:T(8,128)(2,1)S(1)} %get-tuple-element.142.refs_1_, bf16[128,256]{1,0:T(8,128)(2,1)S(1)} %get-tuple-element.143.refs_2_), custom_call_target="tpu_custom_call" | custom-call | flops 3000000000 | bytes 3342336 | tf_op jit(solution)/shard_map/pallas_call | solution.py:92
  122.0 2.4 %collective-permute-start.7 = (f32[32,32,128]{2,1,0:T(8,128)S(1)}, f32[32,32,128]{2,1,0:T(8,128)S(1)}, u32[]{:S(2)}, u32[]{:S(2)}) collective-permute-start(f32[32,32,128]{2,1,0:T(8,128)S(1)} %get-tuple-element.145), channel_id=1, source_target_pairs={{0,2},{2,0},{1,3},{3,1},{4,6},{6,4},{5,7},{7,5},{8,10},{10,8},{9,1... | collective-permute-start | bytes 1572872 | tf_op jit(solution)/shard_map/ppermute | solution.py:992
  124.3 10.9 %collective-permute-done.6 = f32[72,128]{1,0:T(8,128)S(1)} collective-permute-done((f32[72,128]{1,0:T(8,128)S(1)}, f32[72,128]{1,0:T(8,128)S(1)}, u32[]{:S(2)}, u32[]{:S(2)}) %collective-permute-start.6) | collective-permute-done | bytes 36896 | tf_op jit(solution)/shard_map/ppermute | solution.py:911
  135.3 1.8 %all-gather.6 = f32[144,128]{1,0:T(8,128)S(1)} all-gather(f32[72,128]{1,0:T(8,128)S(1)} %collective-permute-done.6), channel_id=8, replica_groups={{0,1},{2,3},{4,5},{6,7},{8,9},{10,11},{12,13},{14,15},{16,17},{18,19},{..., dimensions={0}, use_global_device_ids=true | all-gather | bytes 110592 | tf_op jit(solution)/shard_map/all_gather | solution.py:912
  137.1 2.0 %shard_map.164 = (f32[6,32,128]{2,1,0:T(8,128)S(1)}, f32[2,40,128]{2,1,0:T(8,128)S(1)}) custom-call(s32[1,3]{1,0:T(1,128)S(1)} %copy-done.4, f32[1,3]{1,0:T(1,128)S(1)} %copy-done.11, f32[2,72,128]{2,1,0:T(8,128)S(1)} %get-tuple-element.136.refs_1_, f32[2,72,128]{2,1,0:T(8,128)S(1)} %bitcast.31, f32[6,4,40,128]{3,2,1,0:T(8,128)S(1)} %get-tuple-element.127.refs_13_.refs_3_, ...), custom_call_target="tpu_custom_call" | custom-call | flops 80000000000 | bytes 1200640 | tf_op jit(solution)/shard_map/pallas_call | solution.py:92
  139.2 2.6 %collective-permute-start.8 = (f32[6,32,128]{2,1,0:T(8,128)S(1)}, f32[6,32,128]{2,1,0:T(8,128)S(1)}, u32[]{:S(2)}, u32[]{:S(2)}) collective-permute-start(f32[6,32,128]{2,1,0:T(8,128)S(1)} %get-tuple-element.147.refs_1_), channel_id=1, source_target_pairs={{0,2},{2,0},{1,3},{3,1},{4,6},{6,4},{5,7},{7,5},{8,10},{10,8},{9,1... | collective-permute-start | bytes 294920 | tf_op jit(solution)/shard_map/ppermute | solution.py:1006
  145.5 3.7 %collective-permute-done.8.refs_2_ = f32[6,32,128]{2,1,0:T(8,128)S(1)} collective-permute-done((f32[6,32,128]{2,1,0:T(8,128)S(1)}, f32[6,32,128]{2,1,0:T(8,128)S(1)}, u32[]{:S(2)}, u32[]{:S(2)}) %collective-permute-start.8) | collective-permute-done | bytes 98336 | tf_op jit(solution)/shard_map/ppermute | solution.py:1006
  149.2 3.2 %shard_map.168 = f32[62,1,3969]{2,1,0:T(1,128)} custom-call(s32[1,3]{1,0:T(1,128)S(1)} %copy-done.4, f32[32,62,128]{2,1,0:T(8,128)S(1)} %shard_map.167.refs_0_, f32[6,32,128]{2,1,0:T(8,128)S(1)} %get-tuple-element.147.refs_1_, f32[6,32,128]{2,1,0:T(8,128)S(1)} %collective-permute-done.8.refs_2_, f32[6,128,128]{2,1,0:T(8,128)S(1)} %get-tuple-element.148.refs_3_, ...), custom_call_target="tpu_custom_call" | custom-call | flops 20000000000 | bytes 2609912 | tf_op jit(solution)/shard_map/pallas_call | solution.py:92
  (43 shorter events, 10.3 us)
Async XLA Ops:
  0.6 10.4 %copy-start.12 = (f32[1,16,16384]{2,1,0:T(8,128)S(1)}, f32[1,16,16384]{2,1,0:T(8,128)}, u32[]{:S(2)}) copy-start(f32[1,16,16384]{2,1,0:T(8,128)} %param.15) | copy-start | bytes 3145732
  0.6 12.6 %copy-start = (f32[128,128]{1,0:T(8,128)S(1)}, f32[128,128]{1,0:T(8,128)}, u32[]{:S(2)}) copy-start(f32[128,128]{1,0:T(8,128)} %refs_1_.1) | copy-start | bytes 196612
  0.7 12.6 %copy-start.1 = (f32[128,128]{1,0:T(8,128)S(1)}, f32[128,128]{1,0:T(8,128)}, u32[]{:S(2)}) copy-start(f32[128,128]{1,0:T(8,128)} %refs_2_.1) | copy-start | bytes 196612
  0.7 12.6 %copy-start.2 = (f32[128,128]{1,0:T(8,128)S(1)}, f32[128,128]{1,0:T(8,128)}, u32[]{:S(2)}) copy-start(f32[128,128]{1,0:T(8,128)} %refs_5_.1) | copy-start | bytes 196612
  0.7 12.6 %copy-start.3 = (f32[126,128]{1,0:T(8,128)S(1)}, f32[126,128]{1,0:T(8,128)}, u32[]{:S(2)}) copy-start(f32[126,128]{1,0:T(8,128)} %refs_9_.1) | copy-start | bytes 193540
  0.7 12.6 %copy-start.4 = (s32[1,3]{1,0:T(1,128)S(1)}, s32[1,3]{1,0:T(1,128)}, u32[]{:S(2)}) copy-start(s32[1,3]{1,0:T(1,128)} %links_ref.39) | copy-start | bytes 40
  0.7 12.6 %copy-start.5 = (f32[64,64]{1,0:T(8,128)S(1)}, f32[64,64]{1,0:T(8,128)}, u32[]{:S(2)}) copy-start(f32[64,64]{1,0:T(8,128)} %refs_3_.1) | copy-start | bytes 49156
  0.7 12.6 %copy-start.6 = (f32[64,64]{1,0:T(8,128)S(1)}, f32[64,64]{1,0:T(8,128)}, u32[]{:S(2)}) copy-start(f32[64,64]{1,0:T(8,128)} %refs_4_.1) | copy-start | bytes 49156
  0.7 12.6 %copy-start.7 = (f32[64,64]{1,0:T(8,128)S(1)}, f32[64,64]{1,0:T(8,128)}, u32[]{:S(2)}) copy-start(f32[64,64]{1,0:T(8,128)} %refs_7_.1) | copy-start | bytes 49156
  0.7 12.6 %copy-start.8 = (f32[62,64]{1,0:T(8,128)S(1)}, f32[62,64]{1,0:T(8,128)}, u32[]{:S(2)}) copy-start(f32[62,64]{1,0:T(8,128)} %refs_10_.1) | copy-start | bytes 47620
  0.7 12.6 %copy-start.9 = (f32[128]{0:T(128)S(1)}, f32[128]{0:T(128)}, u32[]{:S(2)}) copy-start(f32[128]{0:T(128)} %param.22) | copy-start | bytes 1540
  0.7 12.6 %copy-start.10 = (f32[64]{0:T(128)S(1)}, f32[64]{0:T(128)}, u32[]{:S(2)}) copy-start(f32[64]{0:T(128)} %param.24) | copy-start | bytes 772
  0.8 12.6 %copy-start.11 = (f32[1,3]{1,0:T(1,128)S(1)}, f32[1,3]{1,0:T(1,128)}, u32[]{:S(2)}) copy-start(f32[1,3]{1,0:T(1,128)} %refs_0_.3) | copy-start | bytes 40
  2.3 12.4 %collective-permute-start = (f32[16,128,128]{2,1,0:T(8,128)S(1)}, f32[16,128,128]{2,1,0:T(8,128)S(1)}, u32[]{:S(2)}, u32[]{:S(2)}) collective-permute-start(f32[16,128,128]{2,1,0:T(8,128)S(1)} %bitcast.20), channel_id=1, source_target_pairs={{0,1},{1,0},{2,3},{3,2},{4,5},{5,4},{6,7},{7,6},{8,9},{9,8},{10,11... | collective-permute-start | bytes 3145736 | tf_op jit(solution)/shard_map/ppermute | solution.py:917
  11.3 34.5 %collective-permute-start.3 = (f32[16,128,128]{2,1,0:T(8,128)S(1)}, f32[16,128,128]{2,1,0:T(8,128)S(1)}, u32[]{:S(2)}, u32[]{:S(2)}) collective-permute-start(f32[16,128,128]{2,1,0:T(8,128)S(1)} %bitcast.18), channel_id=1, source_target_pairs={{0,1},{1,0},{2,3},{3,2},{4,5},{5,4},{6,7},{7,6},{8,9},{9,8},{10,11... | collective-permute-start | bytes 3145736 | tf_op jit(solution)/shard_map/ppermute | solution.py:918
  15.5 6.8 %collective-permute-start.1 = (f32[48,128]{1,0:T(8,128)S(1)}, f32[48,128]{1,0:T(8,128)S(1)}, u32[]{:S(2)}, u32[]{:S(2)}) collective-permute-start(f32[48,128]{1,0:T(8,128)S(1)} %get-tuple-element.80.refs_0_), channel_id=1, source_target_pairs={{1,4},{4,1},{3,6},{6,3},{5,8},{8,5},{7,10},{10,7},{9,12},{12,9},{1... | collective-permute-start | bytes 73736 | tf_op jit(solution)/shard_map/ppermute | solution.py:911
  34.7 12.0 %collective-permute-start.2 = (f32[5,64,128]{2,1,0:T(8,128)S(1)}, f32[5,64,128]{2,1,0:T(8,128)S(1)}, u32[]{:S(2)}, u32[]{:S(2)}) collective-permute-start(f32[5,64,128]{2,1,0:T(8,128)S(1)} %get-tuple-element.90.refs_0_), channel_id=1, source_target_pairs={{0,2},{2,0},{1,3},{3,1},{4,6},{6,4},{5,7},{7,5},{8,10},{10,8},{9,1... | collective-permute-start | bytes 491528 | tf_op jit(solution)/shard_map/ppermute | solution.py:956
  51.2 5.4 %collective-permute-start.4 = (f32[80,128]{1,0:T(8,128)S(1)}, f32[80,128]{1,0:T(8,128)S(1)}, u32[]{:S(2)}, u32[]{:S(2)}) collective-permute-start(f32[80,128]{1,0:T(8,128)S(1)} %get-tuple-element.109), channel_id=1, source_target_pairs={{1,4},{4,1},{3,6},{6,3},{5,8},{8,5},{7,10},{10,7},{9,12},{12,9},{1... | collective-permute-start | bytes 122888 | tf_op jit(solution)/shard_map/ppermute | solution.py:911
  81.9 5.8 %collective-permute-start.5 = (f32[40,128]{1,0:T(8,128)S(1)}, f32[40,128]{1,0:T(8,128)S(1)}, u32[]{:S(2)}, u32[]{:S(2)}) collective-permute-start(f32[40,128]{1,0:T(8,128)S(1)} %get-tuple-element.123), channel_id=1, source_target_pairs={{1,4},{4,1},{3,6},{6,3},{5,8},{8,5},{7,10},{10,7},{9,12},{12,9},{1... | collective-permute-start | bytes 61448 | tf_op jit(solution)/shard_map/ppermute | solution.py:911
  118.0 17.3 %collective-permute-start.6 = (f32[72,128]{1,0:T(8,128)S(1)}, f32[72,128]{1,0:T(8,128)S(1)}, u32[]{:S(2)}, u32[]{:S(2)}) collective-permute-start(f32[72,128]{1,0:T(8,128)S(1)} %get-tuple-element.137), channel_id=1, source_target_pairs={{1,4},{4,1},{3,6},{6,3},{5,8},{8,5},{7,10},{10,7},{9,12},{12,9},{1... | collective-permute-start | bytes 110600 | tf_op jit(solution)/shard_map/ppermute | solution.py:911
  122.0 22.1 %collective-permute-start.7 = (f32[32,32,128]{2,1,0:T(8,128)S(1)}, f32[32,32,128]{2,1,0:T(8,128)S(1)}, u32[]{:S(2)}, u32[]{:S(2)}) collective-permute-start(f32[32,32,128]{2,1,0:T(8,128)S(1)} %get-tuple-element.145), channel_id=1, source_target_pairs={{0,2},{2,0},{1,3},{3,1},{4,6},{6,4},{5,7},{7,5},{8,10},{10,8},{9,1... | collective-permute-start | bytes 1572872 | tf_op jit(solution)/shard_map/ppermute | solution.py:992
  139.2 10.0 %collective-permute-start.8 = (f32[6,32,128]{2,1,0:T(8,128)S(1)}, f32[6,32,128]{2,1,0:T(8,128)S(1)}, u32[]{:S(2)}, u32[]{:S(2)}) collective-permute-start(f32[6,32,128]{2,1,0:T(8,128)S(1)} %get-tuple-element.147.refs_1_), channel_id=1, source_target_pairs={{0,2},{2,0},{1,3},{3,1},{4,6},{6,4},{5,7},{7,5},{8,10},{10,8},{9,1... | collective-permute-start | bytes 294920 | tf_op jit(solution)/shard_map/ppermute | solution.py:1006
